TPU v7x, 512 devices: a whole 4x4x16 slice. The times are simulated.
512 devices in a mesh: pair: 64 (over z, x), day: 8 (over y, core).
Axes of the slice: x: 4, y: 4, z: 16, core: 2. Of those that a mesh axis runs over, the one named last changes fastest.
Arguments:
- spectra: float32 [8, 4096, 4096], P('day', 'pair'), may hold values from -6 to 6
- station_pairs: int32 [16384, 2], P('pair'), may hold values from 0 to 4095, as said below
- station_home: int32 [4096], replicated, may hold values from 0 to 4095, as said below
- block_lists: int32 [64, 64, 8], replicated, may hold values from -1 to 63, as said below
Outputs:
- stacked: float32 [16384, 256], P(('pair', 'day'))
Inputs may be any that keep to these rules, and one draw needn't show every extreme that they name: `station_home`: A permutation: each station has its own stored row. `station_pairs`: the two stations of a pair differ. `block_lists`: entry [o, s, k] is a row within station block s (stored rows s * 64 to (s + 1) * 64 - 1) or -1; the valid entries of [o, s] are distinct and come first, at least one. Every pair block has some station block with all 8 slots valid, and some pair block has all slots valid from every station block.
All inputs are finite; a program needn't handle non-finite values.
Results may differ from a plain program's by a relative error of at most 0.015.
Values may be sent and summed in bfloat16 or wider, within the bound.
No kernel may reach another device: no remote copies, remote signals or barrier semaphores. Data moves between devices by JAX's collectives and lax.ppermute only.
A program may use at most 64 MiB of HBM per device.

v0:
```python
import math

import jax
import jax.numpy as jnp
from jax import lax
from jax.sharding import PartitionSpec as P

FREQS = 2048
LAGS = 256
HALF = 32


def lag_basis():
    freq_index = jnp.arange(FREQS, dtype=jnp.int32)
    lag_index = jnp.arange(LAGS, dtype=jnp.int32) - LAGS // 2
    phase_steps = jnp.mod(freq_index[:, None] * lag_index[None, :], 2 * FREQS)
    angles = phase_steps.astype(jnp.float32) * (2.0 * math.pi / (2 * FREQS))
    scaling = 1.0 / math.sqrt(FREQS)
    return jnp.concatenate([jnp.cos(angles) * scaling, -jnp.sin(angles) * scaling], axis=0).astype(
        jnp.bfloat16
    )


def whiten(station_rows):
    row_count = station_rows.shape[0]
    freq_count = station_rows.shape[1] // 2
    real_part = station_rows[:, :freq_count]
    imag_part = station_rows[:, freq_count:]
    amplitude = jnp.sqrt(real_part * real_part + imag_part * imag_part)
    extended = jnp.concatenate(
        [amplitude[:, freq_count - 128 :], amplitude, amplitude[:, :128]], axis=1
    )
    tile_count = freq_count // 128
    grouped = extended.reshape(row_count, tile_count + 2, 128)
    windows = jnp.concatenate(
        [grouped[:, :tile_count], grouped[:, 1 : tile_count + 1], grouped[:, 2:]], axis=2
    )
    band_rows = jnp.arange(384, dtype=jnp.int32)[:, None]
    band_cols = jnp.arange(128, dtype=jnp.int32)[None, :]
    band_matrix = (jnp.abs(band_rows - band_cols - 128) <= HALF).astype(jnp.float32)
    running = jnp.einsum(
        "snu,uv->snv", windows, band_matrix, precision=lax.Precision.HIGHEST
    ).reshape(row_count, freq_count)
    denominator = running / (2 * HALF + 1) + 1e-05
    return jnp.concatenate([real_part / denominator, imag_part / denominator], axis=1).astype(
        jnp.bfloat16
    )


def cross_spectra(first_end, second_end):
    first_real = first_end[:, :FREQS].astype(jnp.float32)
    first_imag = first_end[:, FREQS:].astype(jnp.float32)
    second_real = second_end[:, :FREQS].astype(jnp.float32)
    second_imag = second_end[:, FREQS:].astype(jnp.float32)
    real_cross = first_real * second_real + first_imag * second_imag
    imag_cross = first_imag * second_real - first_real * second_imag
    return jnp.concatenate([real_cross, imag_cross], axis=1).astype(jnp.bfloat16)


def body(spectra, station_pairs, station_home, block_lists):
    owner_index = lax.axis_index("pair")
    day_count = spectra.shape[0] * lax.axis_size("day")
    block_rows = spectra.shape[1]
    blocks_total = block_lists.shape[0]
    capacity = block_lists.shape[2]
    pair_slots = station_pairs.shape[0]
    received_rows = blocks_total * capacity
    basis = lag_basis()
    storage = jnp.take(station_home, station_pairs, axis=0)
    source_block = storage // block_rows
    source_row = storage % block_rows
    wanted = lax.dynamic_index_in_dim(block_lists, owner_index, 0, keepdims=False)
    candidates = jnp.take(wanted, source_block, axis=0)
    hits = candidates == source_row[:, :, None]
    present = jnp.any(hits, axis=2)
    slot_index = jnp.arange(capacity, dtype=jnp.int32)
    matched = jnp.sum(jnp.where(hits, slot_index[None, None, :], 0), axis=2)
    positions = jnp.where(present, source_block * capacity + matched, -1)
    endpoints = jnp.concatenate([positions[:, 0], positions[:, 1]], axis=0)
    outgoing = lax.dynamic_index_in_dim(block_lists, owner_index, 1, keepdims=False).reshape(
        received_rows
    )
    picker = (outgoing[:, None] == jnp.arange(block_rows, dtype=jnp.int32)[None, :]).astype(
        jnp.bfloat16
    )
    selector = (endpoints[:, None] == jnp.arange(received_rows, dtype=jnp.int32)[None, :]).astype(
        jnp.bfloat16
    )
    whitened = whiten(spectra[0])
    outbound = jnp.dot(picker, whitened, preferred_element_type=jnp.bfloat16)
    outbound = outbound.reshape(blocks_total, capacity, 2 * FREQS)
    inbound = lax.all_to_all(outbound, "pair", split_axis=0, concat_axis=0, tiled=True).reshape(
        received_rows, 2 * FREQS
    )
    chosen = jnp.dot(selector, inbound, preferred_element_type=jnp.bfloat16)
    cross = cross_spectra(chosen[:pair_slots], chosen[pair_slots:])
    accumulated = cross.astype(jnp.float32)
    shares = lax.psum_scatter(
        accumulated.astype(jnp.bfloat16), "day", scatter_dimension=0, tiled=True
    ).astype(jnp.float32)
    stacked = jnp.dot(
        shares,
        basis.astype(jnp.float32),
        precision=lax.Precision.HIGHEST,
        preferred_element_type=jnp.float32,
    )
    return stacked / math.sqrt(day_count)


def solution(mesh):
    in_specs = (P("day", "pair", None), P("pair", None), P(), P())
    out_specs = P(("pair", "day"), None)
    return jax.shard_map(body, mesh=mesh, in_specs=in_specs, out_specs=out_specs, check_vma=False)
```

profile of v0, /device:TPU:1, one launch (start us, length us, event | category | flops | bytes accessed | tf_op | source)
XLA Modules:
  0.0 271.4 jit_solution(5073229853449100689)
XLA Ops:
  6.5 0.0 copy-start
  6.5 1.4 add_sqrt_fusion
  8.0 0.1 reshape.64
  8.1 0.0 copy-start.2
  8.1 0.1 fusion.47
  8.3 0.8 fusion.25
  9.1 0.3 copy-done.2
  9.3 0.3 fusion.31
  9.6 0.0 copy-done
  9.6 1.2 dynamic-slice_reduce_fusion
  10.9 0.1 eq.45
  11.0 3.3 %convolution_bitcast_fusion = bf16[64,8,4096]{2,1,0:T(8,128)(2,1)} fusion(bf16[64,2048]{1,0:T(8,128)(2,1)S(1)} %get-tuple-element.12, bf16[64,2048]{1,0:T(8,128)(2,1)S(1)} %get-tuple-element.11, s32[512]{0:T(512)S(1)} %eq.45), kind=kOutput, calls=%fused_computation.2 | convolution fusion | flops 269516800 | bytes 4720640 | tf_op jit(solution)/shard_map/dot_general | solution.py:90
  14.3 0.0 copy-start.3
  14.3 19.5 %all-to-all-start = ((bf16[64,8,4096]{2,1,0:T(8,128)(2,1)}), bf16[64,8,4096]{2,1,0:T(8,128)(2,1)}, u32[]{:S(2)}, u32[]{:S(2)}) async-start(bf16[64,8,4096]{2,1,0:T(8,128)(2,1)} %convolution_bitcast_fusion), calls=%async_computation | async-start | bytes 8388608 | tf_op jit(solution)/shard_map/all_to_all | solution.py:92
  33.8 0.0 copy-start.1
  33.8 0.2 reduce-scatter.2.cloned.1.call-start
  34.0 0.1 copy.29
  34.1 0.0 copy-done.3
  34.1 0.1 copy.26
  34.3 0.1 reshape.69
  34.4 0.1 copy-done.1
  34.5 3.1 %gather_fusion = s32[512]{0:T(512)S(1)} fusion(s32[4096]{0:T(1024)S(1)} %copy-done.1, s32[1024]{0:T(1024)S(1)} %pad_clamp_fusion.1), kind=kCustom, calls=%fused_computation | custom fusion | bytes 6144 | tf_op jit(solution)/shard_map/jit(_take)/gather | solution.py:69
  37.6 0.1 reshape.68
  37.8 0.1 copy.27
  37.9 0.1 copy.30
  38.0 0.1 reshape.77
  38.2 0.2 copy.28
  38.4 0.1 copy.31
  38.5 1.0 gather_fusion.1
  39.6 5.8 %select_reduce_fusion = (s32[256,2]{1,0:T(8,128)S(1)}, pred[256,2,8]{2,1,0:T(4,128)(4,1)S(1)}) fusion(s32[256,2]{1,0:T(8,128)S(1)} %copy.31, s32[256,2,8]{2,1,0:T(2,128)S(1)} %bitcast.25, pred[256,2]{1,0:T(8,128)(4,1)S(1)} %copy.28), kind=kLoop, calls=%fused_computation.51 | loop fusion | flops 15872 | bytes 25088 | tf_op jit(solution)/shard_map/reduce_sum | solution.py:77
  45.4 4.4 %reduce_or.9 = pred[256,2]{1,0:T(8,128)(4,1)S(1)} reduce(pred[256,2,8]{2,1,0:T(4,128)(4,1)S(1)} %get-tuple-element.6, pred[]{:T(512)} %constant.97.clone.1), dimensions={2}, to_apply=%region_0.1 | reduce | flops 3584 | bytes 4609 | tf_op jit(solution)/shard_map/reduce_or | solution.py:75
  49.8 0.1 copy.33
  49.9 0.1 copy.32
  50.1 167.4 %all-to-all-done = bf16[64,8,4096]{2,1,0:T(8,128)(2,1)} async-done(((bf16[64,8,4096]{2,1,0:T(8,128)(2,1)}), bf16[64,8,4096]{2,1,0:T(8,128)(2,1)}, u32[]{:S(2)}, u32[]{:S(2)}) %all-to-all-start) | async-done | bytes 4194336 | tf_op jit(solution)/shard_map/all_to_all | solution.py:92
  217.4 4.6 %fusion = bf16[512,4096]{1,0:T(8,128)(2,1)S(1)} fusion(bf16[64,8,4096]{2,1,0:T(8,128)(2,1)} %all-to-all-done, s32[512]{0:T(512)S(1)} %pad_add_fusion), kind=kOutput, calls=%fused_computation.3 | convolution fusion | flops 2147745792 | bytes 8390656 | tf_op jit(solution)/shard_map/dot_general | solution.py:95
  222.0 1.0 fusion.3
  223.0 1.6 pad_maximum_fusion
  224.5 0.0 reduce-scatter.2.cloned.1.call-update
  224.6 8.7 %multiply_convert_fusion.1 = (bf16[2048,256]{1,0:T(8,128)(2,1)S(1)}, bf16[2048,256]{1,0:T(8,128)(2,1)S(1)}) fusion(s32[256]{0:T(256)S(1)} %iota_add_fusion), kind=kLoop, calls=%fused_computation.25 | loop fusion | flops 9961472 | bytes 2098176 | tf_op jit(solution)/shard_map/convert
  233.3 29.2 %reduce-scatter.2.cloned.1.call-done = bf16[32,4096]{1,0:T(8,128)(2,1)} async-done(((bf16[256,4096]{1,0:T(8,128)(2,1)}), bf16[32,4096]{1,0:T(8,128)(2,1)}) %reduce-scatter.2.cloned.1.call-update) | async-done | bytes 262160 | tf_op jit(solution)/shard_map/reduce_scatter | solution.py:98
  262.5 2.0 fusion.28
  (13 shorter events, 0.1 us)
Async XLA Ops:
  6.5 3.1 %copy-start = (s32[64,64,8]{1,2,0:T(8,128)S(1)}, s32[64,64,8]{1,2,0:T(8,128)}, u32[]{:S(2)}) copy-start(s32[64,64,8]{1,2,0:T(8,128)} %param.7) | copy-start | bytes 393220
  8.1 1.2 copy-start.2
  14.3 19.9 %copy-start.3 = (s32[256,2]{0,1:T(2,128)S(1)}, s32[256,2]{0,1:T(2,128)}, u32[]{:S(2)}) copy-start(s32[256,2]{0,1:T(2,128)} %param.5) | copy-start | bytes 6148
  14.3 203.2 %all-to-all-start = ((bf16[64,8,4096]{2,1,0:T(8,128)(2,1)}), bf16[64,8,4096]{2,1,0:T(8,128)(2,1)}, u32[]{:S(2)}, u32[]{:S(2)}) async-start(bf16[64,8,4096]{2,1,0:T(8,128)(2,1)} %convolution_bitcast_fusion), calls=%async_computation | async-start | bytes 8388608 | tf_op jit(solution)/shard_map/all_to_all | solution.py:92
  33.8 0.7 copy-start.1
  33.8 228.7 %reduce-scatter.2.cloned.1.call-start = ((), (), s32[]{:S(2)}) async-start(), calls=%async_computation.2 | async-start | bytes 2359296 | tf_op jit(solution)/shard_map/reduce_scatter | solution.py:98
Sparse Core Ops, SparseCore 0:
  224.7 37.7 reduce-scatter.1
where the time goes:
time: 273 us; the launch traced here: 271 us
  waiting for transfers between devices  197 us (72%)
  other arithmetic  23.3 us (9%)
  starting transfers between devices  19.7 us (7%)
  between operations  13.6 us (5%)
  matrix products  10.7 us (4%)
  local copies, waits for them, and re-layouts  7.43 us (3%)
    all_to_all x1, waiting for transfers between devices, body(): lax.all_to_all(outbound, 'pair', split_axis=0, concat_axis=0, tiled=True)  167 us
    reduce_scatter x1, waiting for transfers between devices, body(): lax.psum_scatter(accumulated.astype(jnp.bfloat16), 'day', scatter_dimensi...  29.2 us
    all_to_all x1, starting transfers between devices, body(): lax.all_to_all(outbound, 'pair', split_axis=0, concat_axis=0, tiled=True)  19.5 us
    another operation x3, other arithmetic  9.94 us
    reduce_sum x1, other arithmetic, body(): matched = jnp.sum(jnp.where(hits, slot_index[None, None, :], 0), axis=2)  5.81 us
  transfers between devices with their start and end apart: 2, of which 2 were waited for; matrix products, arithmetic and copies ran while one was open for 9% of the time, Pallas kernels for 0%

commit v1 on v0

v1 whole, which is shorter than its diff:
```python
import functools
import math

import jax
import jax.numpy as jnp
from jax import lax
from jax.experimental import pallas as pl
from jax.experimental.pallas import tpu as pltpu
from jax.sharding import Mesh
from jax.sharding import PartitionSpec as P

HALF = 32
LAGS = 256
LANES = 128


def basis_slice(first, count, freqs):
    freq_index = first + jnp.arange(count, dtype=jnp.int32)
    lag_index = jnp.arange(LAGS, dtype=jnp.int32) - LAGS // 2
    phase_steps = jnp.mod(freq_index[:, None] * lag_index[None, :], 2 * freqs)
    angles = phase_steps.astype(jnp.float32) * (2.0 * math.pi / (2 * freqs))
    scaling = 1.0 / math.sqrt(freqs)
    return jnp.concatenate([jnp.cos(angles) * scaling, -jnp.sin(angles) * scaling], axis=0).astype(
        jnp.bfloat16
    )


def whiten(station_rows):
    row_count = station_rows.shape[0]
    freq_count = station_rows.shape[1] // 2
    real_part = station_rows[:, :freq_count]
    imag_part = station_rows[:, freq_count:]
    amplitude = jnp.sqrt(real_part * real_part + imag_part * imag_part)
    extended = jnp.concatenate(
        [amplitude[:, freq_count - LANES :], amplitude, amplitude[:, :LANES]], axis=1
    )
    tile_count = freq_count // LANES
    grouped = extended.reshape(row_count, tile_count + 2, LANES)
    windows = jnp.concatenate(
        [grouped[:, :tile_count], grouped[:, 1 : tile_count + 1], grouped[:, 2:]], axis=2
    )
    band_rows = jnp.arange(3 * LANES, dtype=jnp.int32)[:, None]
    band_cols = jnp.arange(LANES, dtype=jnp.int32)[None, :]
    band_matrix = (jnp.abs(band_rows - band_cols - LANES) <= HALF).astype(jnp.float32)
    running = jnp.einsum(
        "snu,uv->snv", windows, band_matrix, precision=lax.Precision.HIGHEST
    ).reshape(row_count, freq_count)
    denominator = running / (2 * HALF + 1) + 1e-05
    return (real_part / denominator).astype(jnp.bfloat16), (imag_part / denominator).astype(
        jnp.bfloat16
    )


def correlate_kernel(count, index_ref, *refs):
    blocks = refs[:count]
    basis_ref, out_ref, table, cross, sems = refs[count:]
    block_rows = blocks[0].shape[0]
    pair_count = out_ref.shape[0]
    copies = [
        pltpu.make_async_copy(
            blocks[k], table.at[pl.ds(k * block_rows, block_rows)], sems.at[k]
        )
        for k in range(count)
    ]
    for copy in copies:
        copy.start()
    zero_rows = table.shape[0] - count * block_rows
    table[pl.ds(count * block_rows, zero_rows)] = jnp.zeros((zero_rows, 8, LANES), table.dtype)
    for copy in copies:
        copy.wait()
    low = lax.broadcasted_iota(jnp.int32, (8, LANES), 0) < 4

    group = 8

    def one_group(g, carry):
        for u in range(group):
            p = g * group + u
            a = table[index_ref[0, p]].astype(jnp.float32)
            b = table[index_ref[1, p]].astype(jnp.float32)
            straight = a * b
            crossed = a * pltpu.roll(b, 4, 0)
            real_cross = straight + pltpu.roll(straight, 4, 0)
            imag_cross = crossed - pltpu.roll(crossed, 4, 0)
            start = pl.multiple_of(p * 8, 8)
            cross[pl.ds(start, 8), :] = jnp.where(low, real_cross, imag_cross)
        return carry

    lax.fori_loop(0, pair_count // group, one_group, 0)
    step = 256

    def one_dot(i, carry):
        start = pl.multiple_of(i * step * 8, step * 8)
        rows = jnp.concatenate(
            [
                cross[pl.ds(start + k, step, stride=8), :].astype(jnp.bfloat16)
                for k in range(8)
            ],
            axis=1,
        )
        product = jnp.dot(rows, basis_ref[...], preferred_element_type=jnp.float32)
        out_ref[pl.ds(pl.multiple_of(i * step, step), step), :] = product.astype(out_ref.dtype)
        return carry

    lax.fori_loop(0, pair_count // step, one_dot, 0)


def correlate(index, blocks, basis):
    count = len(blocks)
    block_rows = blocks[0].shape[0]
    pair_count = index.shape[1]
    vmem = pl.BlockSpec(memory_space=pltpu.VMEM)
    return pl.pallas_call(
        functools.partial(correlate_kernel, count),
        out_shape=jax.ShapeDtypeStruct((pair_count, LAGS), jnp.bfloat16),
        in_specs=[pl.BlockSpec(memory_space=pltpu.SMEM)]
        + [pl.BlockSpec(memory_space=pl.ANY)] * count
        + [vmem],
        out_specs=vmem,
        scratch_shapes=[
            pltpu.VMEM((count * block_rows + 8, 8, LANES), jnp.bfloat16),
            pltpu.VMEM((pair_count * 8, LANES), jnp.float32),
            pltpu.SemaphoreType.DMA((count,)),
        ],
        compiler_params=pltpu.CompilerParams(vmem_limit_bytes=36 * 1024 * 1024),
    )(index, *blocks, basis)


def ring(block, axis):
    size = lax.axis_size(axis)
    up = [(i, (i + 1) % size) for i in range(size)]
    down = [(i, (i - 1) % size) for i in range(size)]
    gathered = [None] * size
    gathered[0] = block
    from_below = from_above = block
    for step in range(1, size // 2 + 1):
        from_below = lax.ppermute(from_below, axis, up)
        gathered[size - step] = from_below
        if step < size - step:
            from_above = lax.ppermute(from_above, axis, down)
            gathered[step] = from_above
    return gathered


def pick(table, digits_high, digits_low):
    rows, cols = table.shape
    hot = (digits_high[:, None] == jnp.arange(rows, dtype=jnp.int32)[None, :]).astype(jnp.bfloat16)
    digits = jnp.concatenate([table // 64, table % 64], axis=1).astype(jnp.bfloat16)
    found = jnp.dot(hot, digits, preferred_element_type=jnp.float32)
    mask = digits_low[:, None] == jnp.arange(cols, dtype=jnp.int32)[None, :]
    high = jnp.sum(jnp.where(mask, found[:, :cols], 0.0), axis=1)
    low = jnp.sum(jnp.where(mask, found[:, cols:], 0.0), axis=1)
    return (high * 64.0 + low).astype(jnp.int32)


def body(spectra, station_pairs, station_home, block_lists):
    xs, ys, cs, zs = (lax.axis_size(n) for n in ("x", "y", "c", "z"))
    z, x = lax.axis_index("z"), lax.axis_index("x")
    owner = z * xs + x
    rows = spectra.shape[1]
    freqs = spectra.shape[2] // 2
    share = freqs // xs
    day_count = spectra.shape[0] * ys * cs
    pair_slots = station_pairs.shape[0]
    station_count = station_home.shape[0]

    ends = jnp.concatenate([station_pairs[:, 0], station_pairs[:, 1]], axis=0)
    storage = pick(station_home.reshape(64, station_count // 64), ends // 64, ends % 64)
    source_block = storage // rows
    source_row = storage % rows
    wanted = lax.dynamic_index_in_dim(block_lists, owner, 0, keepdims=False)
    hot = (source_block[:, None] == jnp.arange(wanted.shape[0], dtype=jnp.int32)[None, :]).astype(
        jnp.bfloat16
    )
    candidates = jnp.dot(hot, wanted.astype(jnp.bfloat16), preferred_element_type=jnp.float32)
    listed = jnp.any(candidates == source_row.astype(jnp.float32)[:, None], axis=1)
    plane_rows = rows * xs
    ahead = jnp.mod(storage // plane_rows - z, zs)
    place = jnp.where(listed, ahead * plane_rows + storage % plane_rows, zs * plane_rows)
    place = jnp.broadcast_to(place.reshape(1, 4, LANES), (xs, 4, LANES))
    places = lax.all_to_all(place, "x", 0, 0, tiled=True).reshape(xs, 2, pair_slots)
    index = places.transpose(1, 0, 2).reshape(2, xs * pair_slots)

    real_part, imag_part = whiten(spectra[0])
    outbound = jnp.concatenate(
        [
            real_part.reshape(rows, xs, share // LANES, LANES),
            imag_part.reshape(rows, xs, share // LANES, LANES),
        ],
        axis=2,
    ).transpose(1, 0, 2, 3)
    block = lax.all_to_all(outbound, "x", 0, 0, tiled=True).reshape(plane_rows, 8, LANES)
    blocks = ring(block, "z")
    partial = correlate(index, blocks, basis_slice(x * share, share, freqs))

    group = xs * ys * cs
    slots = xs * pair_slots // group
    shares = lax.all_to_all(
        partial.reshape(group, slots, LAGS), ("x", "y", "c"), 0, 0, tiled=True
    )
    return jnp.sum(shares.astype(jnp.float32), axis=0) / math.sqrt(day_count)


def solution(mesh):
    inner = Mesh(mesh.devices.reshape(16, 4, 4, 2), ("z", "x", "y", "c"))
    in_specs = (P(("y", "c"), ("z", "x"), None), P(("z", "x"), None), P(), P())
    out_specs = P(("z", "x", "y", "c"), None)
    return jax.shard_map(
        body, mesh=inner, in_specs=in_specs, out_specs=out_specs, check_vma=False
    )
```

time: 273 us -> 165 us (0.60)
  waiting for transfers between devices: 197 us -> 47.7 us
  starting transfers between devices: 19.7 us -> 58.7 us
  blocking collectives: 0 us -> 37.6 us
  other arithmetic: 23.3 us -> 5.35 us
  between operations: 13.6 us -> 0.36 us
  Pallas kernels: 0 us -> 9.27 us
  matrix products: 10.7 us -> 2.08 us
  local copies, waits for them, and re-layouts: 7.43 us -> 2.71 us
    all_to_all x1, waiting for transfers between devices: 167 us -> 0.01 us  [body(): lax.all_to_all(place, 'x', 0, 0, tiled=True).reshape(xs, 2, pair_slots)]
    ppermute x0 -> x15, starting transfers between devices: none -> 55.5 us  [the longest x7 36.9 us: ring(): from_above = lax.ppermute(from_above, axis, down)]
    ppermute x0 -> x15, waiting for transfers between devices: none -> 47.7 us  [the longest x8 47 us: ring(): from_below = lax.ppermute(from_below, axis, up)]
    all_to_all x0 -> x2, blocking collectives: none -> 37.6 us  [the longest x1 26 us: body(): lax.all_to_all(partial.reshape(group, slots, LAGS), ('x', 'y', 'c'), 0, 0...]
    reduce_scatter x1 -> x0, waiting for transfers between devices: 29.2 us -> none  [body(): lax.psum_scatter(accumulated.astype(jnp.bfloat16), 'day', scatter_dimensi...]
    all_to_all x1, starting transfers between devices: 19.5 us -> 3.25 us  [body(): lax.all_to_all(place, 'x', 0, 0, tiled=True).reshape(xs, 2, pair_slots)]
    pallas_call x0 -> x1, Pallas kernels: none -> 9.27 us  [correlate(): pl.pallas_call(functools.partial(correlate_kernel, count), out_shape=jax....]
    dot_general x3 -> x2, matrix products: 9.87 us -> 1.26 us  [the longest x1 0.96 us: body(): jnp.dot(hot, wanted.astype(jnp.bfloat16), preferred_element_type=jnp.floa...]
  transfers between devices with their start and end apart: 2 -> 16, of which waited for: 2 -> 9; matrix products, arithmetic and copies ran while one was open for 9% -> 3% of each run, Pallas kernels for 0% -> 0%
where the time goes in v1:
time: 165 us; the launch traced here: 164 us
  starting transfers between devices  58.7 us (36%)
  waiting for transfers between devices  47.7 us (29%)
  blocking collectives  37.6 us (23%)
  Pallas kernels  9.27 us (6%)
  other arithmetic  5.35 us (3%)
  local copies, waits for them, and re-layouts  2.71 us (2%)
  matrix products  2.08 us (1%)
    ppermute x8, waiting for transfers between devices, ring(): from_below = lax.ppermute(from_below, axis, up)  47 us
    ppermute x7, starting transfers between devices, ring(): from_above = lax.ppermute(from_above, axis, down)  36.9 us
    all_to_all x1, blocking collectives, body(): lax.all_to_all(partial.reshape(group, slots, LAGS), ('x', 'y', 'c'), 0, 0...  26 us
    ppermute x8, starting transfers between devices, ring(): from_below = lax.ppermute(from_below, axis, up)  18.5 us
    all_to_all x1, blocking collectives, body(): lax.all_to_all(outbound, 'x', 0, 0, tiled=True)  11.6 us
    pallas_call x1, Pallas kernels, correlate(): pl.pallas_call(functools.partial(correlate_kernel, count), out_shape=jax....  9.27 us
  transfers between devices with their start and end apart: 16, of which 9 were waited for; matrix products, arithmetic and copies ran while one was open for 3% of the time, Pallas kernels for 0%

profile of v1, /device:TPU:1, one launch (start us, length us, event | category | flops | bytes accessed | tf_op | source)
XLA Modules:
  0.0 163.8 jit_solution(567443185319039835)
XLA Ops:
  0.0 1.4 add_sqrt_fusion
  1.4 0.1 reshape.244
  1.5 0.1 fusion.51
  1.7 0.0 copy-start.2
  1.7 0.8 fusion.9
  2.5 0.4 copy-done.2
  2.9 0.2 fusion.16
  3.1 0.2 reshape.245
  3.3 0.2 reshape.246
  3.5 0.0 copy-start.3
  3.5 0.0 copy-start.4
  3.5 0.3 copy_bitcast_fusion
  3.8 11.6 %all_to_all.15 = bf16[4,64,8,128]{3,2,1,0:T(8,128)(2,1)S(1)} all-to-all(bf16[4,64,8,128]{3,2,1,0:T(8,128)(2,1)S(1)} %copy_bitcast_fusion), channel_id=1, replica_groups=mesh['z'=16,'x'=4,'y'=4,'c'=2] {'x'}, dimensions={0} | all-to-all | bytes 1048576 | tf_op jit(solution)/shard_map/all_to_all | solution.py:191
  15.4 5.2 %collective-permute-start.7 = (bf16[256,8,128]{2,1,0:T(8,128)(2,1)S(1)}, bf16[256,8,128]{2,1,0:T(8,128)(2,1)S(1)}, u32[]{:S(2)}, u32[]{:S(2)}) collective-permute-start(bf16[256,8,128]{2,1,0:T(8,128)(2,1)S(1)} %bitcast.44), channel_id=1, source_target_pairs={{0,32},{32,64},{64,96},{96,128},{128,160},{160,192},{192,224},{224... | collective-permute-start | bytes 1572872 | tf_op jit(solution)/shard_map/ppermute | solution.py:136
  20.5 9.5 %collective-permute-start = (bf16[256,8,128]{2,1,0:T(8,128)(2,1)S(1)}, bf16[256,8,128]{2,1,0:T(8,128)(2,1)S(1)}, u32[]{:S(2)}, u32[]{:S(2)}) collective-permute-start(bf16[256,8,128]{2,1,0:T(8,128)(2,1)S(1)} %bitcast.45), channel_id=1, source_target_pairs={{0,480},{32,0},{64,32},{96,64},{128,96},{160,128},{192,160},{224,1... | collective-permute-start | bytes 1572872 | tf_op jit(solution)/shard_map/ppermute | solution.py:139
  30.0 8.4 %collective-permute-done.7.refs_15_ = bf16[256,8,128]{2,1,0:T(8,128)(2,1)S(1)} collective-permute-done((bf16[256,8,128]{2,1,0:T(8,128)(2,1)S(1)}, bf16[256,8,128]{2,1,0:T(8,128)(2,1)S(1)}, u32[]{:S(2)}, u32[]{:S(2)}) %collective-permute-start.7) | collective-permute-done | bytes 524320 | tf_op jit(solution)/shard_map/ppermute | solution.py:136
  38.5 1.9 %collective-permute-start.8 = (bf16[256,8,128]{2,1,0:T(8,128)(2,1)S(1)}, bf16[256,8,128]{2,1,0:T(8,128)(2,1)S(1)}, u32[]{:S(2)}, u32[]{:S(2)}) collective-permute-start(bf16[256,8,128]{2,1,0:T(8,128)(2,1)S(1)} %collective-permute-done.7.refs_15_), channel_id=1, source_target_pairs={{0,32},{32,64},{64,96},{96,128},{128,160},{160,192},{192,224},{224... | collective-permute-start | bytes 1572872 | tf_op jit(solution)/shard_map/ppermute | solution.py:136
  40.4 4.6 %collective-permute-start.1 = (bf16[256,8,128]{2,1,0:T(8,128)(2,1)S(1)}, bf16[256,8,128]{2,1,0:T(8,128)(2,1)S(1)}, u32[]{:S(2)}, u32[]{:S(2)}) collective-permute-start(bf16[256,8,128]{2,1,0:T(8,128)(2,1)S(1)} %collective-permute-done.refs_1_), channel_id=1, source_target_pairs={{0,480},{32,0},{64,32},{96,64},{128,96},{160,128},{192,160},{224,1... | collective-permute-start | bytes 1572872 | tf_op jit(solution)/shard_map/ppermute | solution.py:139
  45.0 7.5 %collective-permute-done.8.refs_14_ = bf16[256,8,128]{2,1,0:T(8,128)(2,1)S(1)} collective-permute-done((bf16[256,8,128]{2,1,0:T(8,128)(2,1)S(1)}, bf16[256,8,128]{2,1,0:T(8,128)(2,1)S(1)}, u32[]{:S(2)}, u32[]{:S(2)}) %collective-permute-start.8) | collective-permute-done | bytes 524320 | tf_op jit(solution)/shard_map/ppermute | solution.py:136
  52.5 1.9 %collective-permute-start.9 = (bf16[256,8,128]{2,1,0:T(8,128)(2,1)S(1)}, bf16[256,8,128]{2,1,0:T(8,128)(2,1)S(1)}, u32[]{:S(2)}, u32[]{:S(2)}) collective-permute-start(bf16[256,8,128]{2,1,0:T(8,128)(2,1)S(1)} %collective-permute-done.8.refs_14_), channel_id=1, source_target_pairs={{0,32},{32,64},{64,96},{96,128},{128,160},{160,192},{192,224},{224... | collective-permute-start | bytes 1572872 | tf_op jit(solution)/shard_map/ppermute | solution.py:136
  54.4 4.6 %collective-permute-start.2 = (bf16[256,8,128]{2,1,0:T(8,128)(2,1)S(1)}, bf16[256,8,128]{2,1,0:T(8,128)(2,1)}, u32[]{:S(2)}, u32[]{:S(2)}) collective-permute-start(bf16[256,8,128]{2,1,0:T(8,128)(2,1)S(1)} %collective-permute-done.1.refs_2_), channel_id=1, source_target_pairs={{0,480},{32,0},{64,32},{96,64},{128,96},{160,128},{192,160},{224,1... | collective-permute-start | bytes 1572872 | tf_op jit(solution)/shard_map/ppermute | solution.py:139
  59.0 6.6 %collective-permute-done.9.refs_13_ = bf16[256,8,128]{2,1,0:T(8,128)(2,1)S(1)} collective-permute-done((bf16[256,8,128]{2,1,0:T(8,128)(2,1)S(1)}, bf16[256,8,128]{2,1,0:T(8,128)(2,1)S(1)}, u32[]{:S(2)}, u32[]{:S(2)}) %collective-permute-start.9) | collective-permute-done | bytes 524320 | tf_op jit(solution)/shard_map/ppermute | solution.py:136
  65.6 1.9 %collective-permute-start.10 = (bf16[256,8,128]{2,1,0:T(8,128)(2,1)S(1)}, bf16[256,8,128]{2,1,0:T(8,128)(2,1)}, u32[]{:S(2)}, u32[]{:S(2)}) collective-permute-start(bf16[256,8,128]{2,1,0:T(8,128)(2,1)S(1)} %collective-permute-done.9.refs_13_), channel_id=1, source_target_pairs={{0,32},{32,64},{64,96},{96,128},{128,160},{160,192},{192,224},{224... | collective-permute-start | bytes 1572872 | tf_op jit(solution)/shard_map/ppermute | solution.py:136
  67.5 4.6 %collective-permute-start.3 = (bf16[256,8,128]{2,1,0:T(8,128)(2,1)}, bf16[256,8,128]{2,1,0:T(8,128)(2,1)}, u32[]{:S(2)}, u32[]{:S(2)}) collective-permute-start(bf16[256,8,128]{2,1,0:T(8,128)(2,1)} %collective-permute-done.2.refs_3_), channel_id=1, source_target_pairs={{0,480},{32,0},{64,32},{96,64},{128,96},{160,128},{192,160},{224,1... | collective-permute-start | bytes 1572872 | tf_op jit(solution)/shard_map/ppermute | solution.py:139
  72.1 5.8 %collective-permute-done.10.refs_12_ = bf16[256,8,128]{2,1,0:T(8,128)(2,1)} collective-permute-done((bf16[256,8,128]{2,1,0:T(8,128)(2,1)S(1)}, bf16[256,8,128]{2,1,0:T(8,128)(2,1)}, u32[]{:S(2)}, u32[]{:S(2)}) %collective-permute-start.10) | collective-permute-done | bytes 524320 | tf_op jit(solution)/shard_map/ppermute | solution.py:136
  77.8 1.9 %collective-permute-start.11 = (bf16[256,8,128]{2,1,0:T(8,128)(2,1)}, bf16[256,8,128]{2,1,0:T(8,128)(2,1)}, u32[]{:S(2)}, u32[]{:S(2)}) collective-permute-start(bf16[256,8,128]{2,1,0:T(8,128)(2,1)} %collective-permute-done.10.refs_12_), channel_id=1, source_target_pairs={{0,32},{32,64},{64,96},{96,128},{128,160},{160,192},{192,224},{224... | collective-permute-start | bytes 1572872 | tf_op jit(solution)/shard_map/ppermute | solution.py:136
  79.8 0.1 reshape.241
  79.9 4.6 %collective-permute-start.4 = (bf16[256,8,128]{2,1,0:T(8,128)(2,1)}, bf16[256,8,128]{2,1,0:T(8,128)(2,1)}, u32[]{:S(2)}, u32[]{:S(2)}) collective-permute-start(bf16[256,8,128]{2,1,0:T(8,128)(2,1)} %collective-permute-done.3.refs_4_), channel_id=1, source_target_pairs={{0,480},{32,0},{64,32},{96,64},{128,96},{160,128},{192,160},{224,1... | collective-permute-start | bytes 1572872 | tf_op jit(solution)/shard_map/ppermute | solution.py:139
  84.5 4.8 %collective-permute-done.11.refs_11_ = bf16[256,8,128]{2,1,0:T(8,128)(2,1)} collective-permute-done((bf16[256,8,128]{2,1,0:T(8,128)(2,1)}, bf16[256,8,128]{2,1,0:T(8,128)(2,1)}, u32[]{:S(2)}, u32[]{:S(2)}) %collective-permute-start.11) | collective-permute-done | bytes 524320 | tf_op jit(solution)/shard_map/ppermute | solution.py:136
  89.3 1.9 %collective-permute-start.12 = (bf16[256,8,128]{2,1,0:T(8,128)(2,1)}, bf16[256,8,128]{2,1,0:T(8,128)(2,1)}, u32[]{:S(2)}, u32[]{:S(2)}) collective-permute-start(bf16[256,8,128]{2,1,0:T(8,128)(2,1)} %collective-permute-done.11.refs_11_), channel_id=1, source_target_pairs={{0,32},{32,64},{64,96},{96,128},{128,160},{160,192},{192,224},{224... | collective-permute-start | bytes 1572872 | tf_op jit(solution)/shard_map/ppermute | solution.py:136
  91.2 0.3 fusion.18
  91.6 4.6 %collective-permute-start.5 = (bf16[256,8,128]{2,1,0:T(8,128)(2,1)}, bf16[256,8,128]{2,1,0:T(8,128)(2,1)}, u32[]{:S(2)}, u32[]{:S(2)}) collective-permute-start(bf16[256,8,128]{2,1,0:T(8,128)(2,1)} %collective-permute-done.4.refs_5_), channel_id=1, source_target_pairs={{0,480},{32,0},{64,32},{96,64},{128,96},{160,128},{192,160},{224,1... | collective-permute-start | bytes 1572872 | tf_op jit(solution)/shard_map/ppermute | solution.py:139
  96.2 4.5 %collective-permute-done.12.refs_10_ = bf16[256,8,128]{2,1,0:T(8,128)(2,1)} collective-permute-done((bf16[256,8,128]{2,1,0:T(8,128)(2,1)}, bf16[256,8,128]{2,1,0:T(8,128)(2,1)}, u32[]{:S(2)}, u32[]{:S(2)}) %collective-permute-start.12) | collective-permute-done | bytes 524320 | tf_op jit(solution)/shard_map/ppermute | solution.py:136
  100.7 1.9 %collective-permute-start.13 = (bf16[256,8,128]{2,1,0:T(8,128)(2,1)}, bf16[256,8,128]{2,1,0:T(8,128)(2,1)}, u32[]{:S(2)}, u32[]{:S(2)}) collective-permute-start(bf16[256,8,128]{2,1,0:T(8,128)(2,1)} %collective-permute-done.12.refs_10_), channel_id=1, source_target_pairs={{0,32},{32,64},{64,96},{96,128},{128,160},{160,192},{192,224},{224... | collective-permute-start | bytes 1572872 | tf_op jit(solution)/shard_map/ppermute | solution.py:136
  102.7 1.0 fusion.12
  103.6 0.6 broadcast_in_dim.13
  104.2 3.2 %all-to-all-start = ((s32[4,4,128]{2,1,0:T(4,128)}), s32[4,4,128]{2,1,0:T(4,128)S(1)}, u32[]{:S(2)}, u32[]{:S(2)}) async-start(s32[4,4,128]{2,1,0:T(4,128)} %broadcast_in_dim.13), calls=%async_computation | async-start | bytes 16384 | tf_op jit(solution)/shard_map/all_to_all | solution.py:180
  107.5 4.6 %collective-permute-start.6 = (bf16[256,8,128]{2,1,0:T(8,128)(2,1)}, bf16[256,8,128]{2,1,0:T(8,128)(2,1)}, u32[]{:S(2)}, u32[]{:S(2)}) collective-permute-start(bf16[256,8,128]{2,1,0:T(8,128)(2,1)} %collective-permute-done.5.refs_6_), channel_id=1, source_target_pairs={{0,480},{32,0},{64,32},{96,64},{128,96},{160,128},{192,160},{224,1... | collective-permute-start | bytes 1572872 | tf_op jit(solution)/shard_map/ppermute | solution.py:139
  112.1 1.1 collective-permute-done.13.refs_9_
  113.2 1.9 %collective-permute-start.14 = (bf16[256,8,128]{2,1,0:T(8,128)(2,1)}, bf16[256,8,128]{2,1,0:T(8,128)(2,1)}, u32[]{:S(2)}, u32[]{:S(2)}) collective-permute-start(bf16[256,8,128]{2,1,0:T(8,128)(2,1)} %collective-permute-done.13.refs_9_), channel_id=1, source_target_pairs={{0,32},{32,64},{64,96},{96,128},{128,160},{160,192},{192,224},{224... | collective-permute-start | bytes 1572872 | tf_op jit(solution)/shard_map/ppermute | solution.py:136
  115.2 2.5 %multiply_convert_fusion.1 = (bf16[512,256]{1,0:T(8,128)(2,1)S(1)}, bf16[512,256]{1,0:T(8,128)(2,1)S(1)}) fusion(s32[256]{0:T(256)S(1)} %iota_add_fusion.1, s32[512]{0:T(512)S(1)} %iota_add_fusion), kind=kLoop, calls=%fused_computation.28 | loop fusion | flops 2490368 | bytes 527360 | tf_op jit(solution)/shard_map/convert
  117.8 0.7 collective-permute-done.6.refs_7_
  118.5 8.3 %collective-permute-done.14.refs_8_ = bf16[256,8,128]{2,1,0:T(8,128)(2,1)} collective-permute-done((bf16[256,8,128]{2,1,0:T(8,128)(2,1)}, bf16[256,8,128]{2,1,0:T(8,128)(2,1)}, u32[]{:S(2)}, u32[]{:S(2)}) %collective-permute-start.14) | collective-permute-done | bytes 524320 | tf_op jit(solution)/shard_map/ppermute | solution.py:136
  126.8 1.0 copy-done.1
  127.8 9.3 %shard_map.46 = bf16[1024,256]{1,0:T(8,128)(2,1)S(1)} custom-call(s32[2,1024]{1,0:T(2,128)S(1)} %bitcast.48, bf16[256,8,128]{2,1,0:T(8,128)(2,1)S(1)} %bitcast.46, bf16[256,8,128]{2,1,0:T(8,128)(2,1)S(1)} %collective-permute-done.refs_1_, bf16[256,8,128]{2,1,0:T(8,128)(2,1)S(1)} %collective-permute-done.1.refs_2_, ...), custom_call_target="tpu_custom_call" | custom-call | tf_op jit(solution)/shard_map/pallas_call | solution.py:112
  137.1 26.0 %all_to_all.16 = bf16[32,32,256]{2,1,0:T(8,128)(2,1)S(1)} all-to-all(bf16[32,32,256]{2,1,0:T(8,128)(2,1)S(1)} %bitcast.47), channel_id=1, replica_groups=mesh['z'=16,'x'=4,'y'=4,'c'=2] {'x','y','c'}, dimensions={0} | all-to-all | bytes 1048576 | tf_op jit(solution)/shard_map/all_to_all | solution.py:197
  163.1 0.1 convert_reduce_fusion
  163.2 0.6 broadcast_multiply_fusion
  (24 shorter events, 0.3 us)
Async XLA Ops:
  1.7 1.2 copy-start.2
  3.5 76.3 %copy-start.3 = (s32[4096]{0:T(1024)S(1)}, s32[4096]{0:T(1024)}, u32[]{:S(2)}) copy-start(s32[4096]{0:T(1024)} %param.6) | copy-start | bytes 49156
  3.5 76.3 %copy-start.4 = (s32[256,2]{0,1:T(2,128)S(1)}, s32[256,2]{0,1:T(2,128)}, u32[]{:S(2)}) copy-start(s32[256,2]{0,1:T(2,128)} %param.5) | copy-start | bytes 6148
  15.4 23.1 %collective-permute-start.7 = (bf16[256,8,128]{2,1,0:T(8,128)(2,1)S(1)}, bf16[256,8,128]{2,1,0:T(8,128)(2,1)S(1)}, u32[]{:S(2)}, u32[]{:S(2)}) collective-permute-start(bf16[256,8,128]{2,1,0:T(8,128)(2,1)S(1)} %bitcast.44), channel_id=1, source_target_pairs={{0,32},{32,64},{64,96},{96,128},{128,160},{160,192},{192,224},{224... | collective-permute-start | bytes 1572872 | tf_op jit(solution)/shard_map/ppermute | solution.py:136
  20.5 19.9 %collective-permute-start = (bf16[256,8,128]{2,1,0:T(8,128)(2,1)S(1)}, bf16[256,8,128]{2,1,0:T(8,128)(2,1)S(1)}, u32[]{:S(2)}, u32[]{:S(2)}) collective-permute-start(bf16[256,8,128]{2,1,0:T(8,128)(2,1)S(1)} %bitcast.45), channel_id=1, source_target_pairs={{0,480},{32,0},{64,32},{96,64},{128,96},{160,128},{192,160},{224,1... | collective-permute-start | bytes 1572872 | tf_op jit(solution)/shard_map/ppermute | solution.py:139
  38.5 14.0 %collective-permute-start.8 = (bf16[256,8,128]{2,1,0:T(8,128)(2,1)S(1)}, bf16[256,8,128]{2,1,0:T(8,128)(2,1)S(1)}, u32[]{:S(2)}, u32[]{:S(2)}) collective-permute-start(bf16[256,8,128]{2,1,0:T(8,128)(2,1)S(1)} %collective-permute-done.7.refs_15_), channel_id=1, source_target_pairs={{0,32},{32,64},{64,96},{96,128},{128,160},{160,192},{192,224},{224... | collective-permute-start | bytes 1572872 | tf_op jit(solution)/shard_map/ppermute | solution.py:136
  40.4 14.0 %collective-permute-start.1 = (bf16[256,8,128]{2,1,0:T(8,128)(2,1)S(1)}, bf16[256,8,128]{2,1,0:T(8,128)(2,1)S(1)}, u32[]{:S(2)}, u32[]{:S(2)}) collective-permute-start(bf16[256,8,128]{2,1,0:T(8,128)(2,1)S(1)} %collective-permute-done.refs_1_), channel_id=1, source_target_pairs={{0,480},{32,0},{64,32},{96,64},{128,96},{160,128},{192,160},{224,1... | collective-permute-start | bytes 1572872 | tf_op jit(solution)/shard_map/ppermute | solution.py:139
  52.5 13.1 %collective-permute-start.9 = (bf16[256,8,128]{2,1,0:T(8,128)(2,1)S(1)}, bf16[256,8,128]{2,1,0:T(8,128)(2,1)S(1)}, u32[]{:S(2)}, u32[]{:S(2)}) collective-permute-start(bf16[256,8,128]{2,1,0:T(8,128)(2,1)S(1)} %collective-permute-done.8.refs_14_), channel_id=1, source_target_pairs={{0,32},{32,64},{64,96},{96,128},{128,160},{160,192},{192,224},{224... | collective-permute-start | bytes 1572872 | tf_op jit(solution)/shard_map/ppermute | solution.py:136
  54.4 13.1 %collective-permute-start.2 = (bf16[256,8,128]{2,1,0:T(8,128)(2,1)S(1)}, bf16[256,8,128]{2,1,0:T(8,128)(2,1)}, u32[]{:S(2)}, u32[]{:S(2)}) collective-permute-start(bf16[256,8,128]{2,1,0:T(8,128)(2,1)S(1)} %collective-permute-done.1.refs_2_), channel_id=1, source_target_pairs={{0,480},{32,0},{64,32},{96,64},{128,96},{160,128},{192,160},{224,1... | collective-permute-start | bytes 1572872 | tf_op jit(solution)/shard_map/ppermute | solution.py:139
  65.6 52.1 %copy-start = (bf16[256,8,128]{2,1,0:T(8,128)(2,1)}, bf16[256,8,128]{2,1,0:T(8,128)(2,1)S(1)}, u32[]{:S(2)}) copy-start(bf16[256,8,128]{2,1,0:T(8,128)(2,1)S(1)} %collective-permute-done.9.refs_13_) | copy-start | bytes 1572868
  65.6 12.3 %collective-permute-start.10 = (bf16[256,8,128]{2,1,0:T(8,128)(2,1)S(1)}, bf16[256,8,128]{2,1,0:T(8,128)(2,1)}, u32[]{:S(2)}, u32[]{:S(2)}) collective-permute-start(bf16[256,8,128]{2,1,0:T(8,128)(2,1)S(1)} %collective-permute-done.9.refs_13_), channel_id=1, source_target_pairs={{0,32},{32,64},{64,96},{96,128},{128,160},{160,192},{192,224},{224... | collective-permute-start | bytes 1572872 | tf_op jit(solution)/shard_map/ppermute | solution.py:136
  67.5 12.4 %collective-permute-start.3 = (bf16[256,8,128]{2,1,0:T(8,128)(2,1)}, bf16[256,8,128]{2,1,0:T(8,128)(2,1)}, u32[]{:S(2)}, u32[]{:S(2)}) collective-permute-start(bf16[256,8,128]{2,1,0:T(8,128)(2,1)} %collective-permute-done.2.refs_3_), channel_id=1, source_target_pairs={{0,480},{32,0},{64,32},{96,64},{128,96},{160,128},{192,160},{224,1... | collective-permute-start | bytes 1572872 | tf_op jit(solution)/shard_map/ppermute | solution.py:139
  77.8 11.4 %collective-permute-start.11 = (bf16[256,8,128]{2,1,0:T(8,128)(2,1)}, bf16[256,8,128]{2,1,0:T(8,128)(2,1)}, u32[]{:S(2)}, u32[]{:S(2)}) collective-permute-start(bf16[256,8,128]{2,1,0:T(8,128)(2,1)} %collective-permute-done.10.refs_12_), channel_id=1, source_target_pairs={{0,32},{32,64},{64,96},{96,128},{128,160},{160,192},{192,224},{224... | collective-permute-start | bytes 1572872 | tf_op jit(solution)/shard_map/ppermute | solution.py:136
  79.9 11.7 %collective-permute-start.4 = (bf16[256,8,128]{2,1,0:T(8,128)(2,1)}, bf16[256,8,128]{2,1,0:T(8,128)(2,1)}, u32[]{:S(2)}, u32[]{:S(2)}) collective-permute-start(bf16[256,8,128]{2,1,0:T(8,128)(2,1)} %collective-permute-done.3.refs_4_), channel_id=1, source_target_pairs={{0,480},{32,0},{64,32},{96,64},{128,96},{160,128},{192,160},{224,1... | collective-permute-start | bytes 1572872 | tf_op jit(solution)/shard_map/ppermute | solution.py:139
  89.3 11.4 %collective-permute-start.12 = (bf16[256,8,128]{2,1,0:T(8,128)(2,1)}, bf16[256,8,128]{2,1,0:T(8,128)(2,1)}, u32[]{:S(2)}, u32[]{:S(2)}) collective-permute-start(bf16[256,8,128]{2,1,0:T(8,128)(2,1)} %collective-permute-done.11.refs_11_), channel_id=1, source_target_pairs={{0,32},{32,64},{64,96},{96,128},{128,160},{160,192},{192,224},{224... | collective-permute-start | bytes 1572872 | tf_op jit(solution)/shard_map/ppermute | solution.py:136
  91.6 15.9 %collective-permute-start.5 = (bf16[256,8,128]{2,1,0:T(8,128)(2,1)}, bf16[256,8,128]{2,1,0:T(8,128)(2,1)}, u32[]{:S(2)}, u32[]{:S(2)}) collective-permute-start(bf16[256,8,128]{2,1,0:T(8,128)(2,1)} %collective-permute-done.4.refs_5_), channel_id=1, source_target_pairs={{0,480},{32,0},{64,32},{96,64},{128,96},{160,128},{192,160},{224,1... | collective-permute-start | bytes 1572872 | tf_op jit(solution)/shard_map/ppermute | solution.py:139
  100.7 12.5 %collective-permute-start.13 = (bf16[256,8,128]{2,1,0:T(8,128)(2,1)}, bf16[256,8,128]{2,1,0:T(8,128)(2,1)}, u32[]{:S(2)}, u32[]{:S(2)}) collective-permute-start(bf16[256,8,128]{2,1,0:T(8,128)(2,1)} %collective-permute-done.12.refs_10_), channel_id=1, source_target_pairs={{0,32},{32,64},{64,96},{96,128},{128,160},{160,192},{192,224},{224... | collective-permute-start | bytes 1572872 | tf_op jit(solution)/shard_map/ppermute | solution.py:136
  104.2 13.5 %all-to-all-start = ((s32[4,4,128]{2,1,0:T(4,128)}), s32[4,4,128]{2,1,0:T(4,128)S(1)}, u32[]{:S(2)}, u32[]{:S(2)}) async-start(s32[4,4,128]{2,1,0:T(4,128)} %broadcast_in_dim.13), calls=%async_computation | async-start | bytes 16384 | tf_op jit(solution)/shard_map/all_to_all | solution.py:180
  107.5 11.0 %collective-permute-start.6 = (bf16[256,8,128]{2,1,0:T(8,128)(2,1)}, bf16[256,8,128]{2,1,0:T(8,128)(2,1)}, u32[]{:S(2)}, u32[]{:S(2)}) collective-permute-start(bf16[256,8,128]{2,1,0:T(8,128)(2,1)} %collective-permute-done.5.refs_6_), channel_id=1, source_target_pairs={{0,480},{32,0},{64,32},{96,64},{128,96},{160,128},{192,160},{224,1... | collective-permute-start | bytes 1572872 | tf_op jit(solution)/shard_map/ppermute | solution.py:139
  113.2 13.6 %collective-permute-start.14 = (bf16[256,8,128]{2,1,0:T(8,128)(2,1)}, bf16[256,8,128]{2,1,0:T(8,128)(2,1)}, u32[]{:S(2)}, u32[]{:S(2)}) collective-permute-start(bf16[256,8,128]{2,1,0:T(8,128)(2,1)} %collective-permute-done.13.refs_9_), channel_id=1, source_target_pairs={{0,32},{32,64},{64,96},{96,128},{128,160},{160,192},{192,224},{224... | collective-permute-start | bytes 1572872 | tf_op jit(solution)/shard_map/ppermute | solution.py:136
  126.8 1.0 copy-start.1

commit v2 on v1

--- a/solution.py
+++ b/solution.py
@@ -51,11 +51,13 @@
     )
 
 
-def correlate_kernel(count, index_ref, *refs):
+def correlate_kernel(count, index_ref, used_ref, *refs):
     blocks = refs[:count]
     basis_ref, out_ref, table, cross, sems = refs[count:]
     block_rows = blocks[0].shape[0]
-    pair_count = out_ref.shape[0]
+    slot_count = out_ref.shape[0]
+    columns = used_ref.shape[0]
+    slots = slot_count // columns
     copies = [
         pltpu.make_async_copy(
             blocks[k], table.at[pl.ds(k * block_rows, block_rows)], sems.at[k]
@@ -66,26 +68,35 @@
         copy.start()
     zero_rows = table.shape[0] - count * block_rows
     table[pl.ds(count * block_rows, zero_rows)] = jnp.zeros((zero_rows, 8, LANES), table.dtype)
+
+    def clear(i, carry):
+        cross[pl.ds(pl.multiple_of(i * 256, 256), 256), :] = jnp.zeros((256, LANES), jnp.float32)
+        return carry
+
+    lax.fori_loop(0, slot_count * 8 // 256, clear, 0)
     for copy in copies:
         copy.wait()
     low = lax.broadcasted_iota(jnp.int32, (8, LANES), 0) < 4
-
     group = 8
 
-    def one_group(g, carry):
-        for u in range(group):
-            p = g * group + u
-            a = table[index_ref[0, p]].astype(jnp.float32)
-            b = table[index_ref[1, p]].astype(jnp.float32)
-            straight = a * b
-            crossed = a * pltpu.roll(b, 4, 0)
-            real_cross = straight + pltpu.roll(straight, 4, 0)
-            imag_cross = crossed - pltpu.roll(crossed, 4, 0)
-            start = pl.multiple_of(p * 8, 8)
-            cross[pl.ds(start, 8), :] = jnp.where(low, real_cross, imag_cross)
+    def one_column(column, carry):
+        def one_group(g, inner):
+            for u in range(group):
+                p = column * slots + g * group + u
+                a = table[index_ref[0, p]].astype(jnp.float32)
+                b = table[index_ref[1, p]].astype(jnp.float32)
+                straight = a * b
+                crossed = a * pltpu.roll(b, 4, 0)
+                real_cross = straight + pltpu.roll(straight, 4, 0)
+                imag_cross = crossed - pltpu.roll(crossed, 4, 0)
+                start = pl.multiple_of(p * 8, 8)
+                cross[pl.ds(start, 8), :] = jnp.where(low, real_cross, imag_cross)
+            return inner
+
+        lax.fori_loop(0, (used_ref[column] + group - 1) // group, one_group, 0)
         return carry
 
-    lax.fori_loop(0, pair_count // group, one_group, 0)
+    lax.fori_loop(0, columns, one_column, 0)
     step = 256
 
     def one_dot(i, carry):
@@ -101,44 +112,59 @@
         out_ref[pl.ds(pl.multiple_of(i * step, step), step), :] = product.astype(out_ref.dtype)
         return carry
 
-    lax.fori_loop(0, pair_count // step, one_dot, 0)
-
-
-def correlate(index, blocks, basis):
+    lax.fori_loop(0, slot_count // step, one_dot, 0)
+
+
+def correlate(index, used, blocks, basis):
     count = len(blocks)
     block_rows = blocks[0].shape[0]
-    pair_count = index.shape[1]
+    slot_count = index.shape[1]
     vmem = pl.BlockSpec(memory_space=pltpu.VMEM)
+    smem = pl.BlockSpec(memory_space=pltpu.SMEM)
     return pl.pallas_call(
         functools.partial(correlate_kernel, count),
-        out_shape=jax.ShapeDtypeStruct((pair_count, LAGS), jnp.bfloat16),
-        in_specs=[pl.BlockSpec(memory_space=pltpu.SMEM)]
-        + [pl.BlockSpec(memory_space=pl.ANY)] * count
-        + [vmem],
+        out_shape=jax.ShapeDtypeStruct((slot_count, LAGS), jnp.bfloat16),
+        in_specs=[smem, smem] + [pl.BlockSpec(memory_space=pl.ANY)] * count + [vmem],
         out_specs=vmem,
         scratch_shapes=[
             pltpu.VMEM((count * block_rows + 8, 8, LANES), jnp.bfloat16),
-            pltpu.VMEM((pair_count * 8, LANES), jnp.float32),
+            pltpu.VMEM((slot_count * 8, LANES), jnp.float32),
             pltpu.SemaphoreType.DMA((count,)),
         ],
         compiler_params=pltpu.CompilerParams(vmem_limit_bytes=36 * 1024 * 1024),
-    )(index, *blocks, basis)
-
-
-def ring(block, axis):
-    size = lax.axis_size(axis)
+    )(index, used, *blocks, basis)
+
+
+def shifts(size):
     up = [(i, (i + 1) % size) for i in range(size)]
     down = [(i, (i - 1) % size) for i in range(size)]
-    gathered = [None] * size
-    gathered[0] = block
+    return up, down
+
+
+def near_ring(block, axis, reach):
+    up, down = shifts(lax.axis_size(axis))
+    below, above = [], []
     from_below = from_above = block
-    for step in range(1, size // 2 + 1):
+    for _ in range(reach):
         from_below = lax.ppermute(from_below, axis, up)
-        gathered[size - step] = from_below
+        from_above = lax.ppermute(from_above, axis, down)
+        below.append(from_below)
+        above.append(from_above)
+    return below[::-1] + [block] + above
+
+
+def far_ring(near, axis, reach):
+    size = lax.axis_size(axis)
+    up, down = shifts(size)
+    below, above = [], []
+    from_below, from_above = near[0], near[-1]
+    for step in range(reach + 1, size // 2 + 1):
+        from_below = lax.ppermute(from_below, axis, up)
+        below.append(from_below)
         if step < size - step:
             from_above = lax.ppermute(from_above, axis, down)
-            gathered[step] = from_above
-    return gathered
+            above.append(from_above)
+    return above + below[::-1]
 
 
 def pick(table, digits_high, digits_low):
@@ -152,19 +178,31 @@
     return (high * 64.0 + low).astype(jnp.int32)
 
 
+def exchange_and_add(partial, group):
+    columns = partial.reshape(group, -1, LAGS)
+    shares = lax.all_to_all(columns, ("x", "y", "c"), 0, 0, tiled=True)
+    return jnp.sum(shares.astype(jnp.float32), axis=0)
+
+
 def body(spectra, station_pairs, station_home, block_lists):
     xs, ys, cs, zs = (lax.axis_size(n) for n in ("x", "y", "c", "z"))
     z, x = lax.axis_index("z"), lax.axis_index("x")
     owner = z * xs + x
+    day = lax.axis_index("y") * cs + lax.axis_index("c")
+    days = ys * cs
+    column = x * days + day
+    columns = xs * days
     rows = spectra.shape[1]
     freqs = spectra.shape[2] // 2
     share = freqs // xs
-    day_count = spectra.shape[0] * ys * cs
+    scale = 1.0 / math.sqrt(spectra.shape[0] * days)
     pair_slots = station_pairs.shape[0]
-    station_count = station_home.shape[0]
+    own = pair_slots // days
+    plane_rows = rows * xs
+    reach = zs // 4
 
     ends = jnp.concatenate([station_pairs[:, 0], station_pairs[:, 1]], axis=0)
-    storage = pick(station_home.reshape(64, station_count // 64), ends // 64, ends % 64)
+    storage = pick(station_home.reshape(64, -1), ends // 64, ends % 64)
     source_block = storage // rows
     source_row = storage % rows
     wanted = lax.dynamic_index_in_dim(block_lists, owner, 0, keepdims=False)
@@ -173,12 +211,8 @@
     )
     candidates = jnp.dot(hot, wanted.astype(jnp.bfloat16), preferred_element_type=jnp.float32)
     listed = jnp.any(candidates == source_row.astype(jnp.float32)[:, None], axis=1)
-    plane_rows = rows * xs
-    ahead = jnp.mod(storage // plane_rows - z, zs)
-    place = jnp.where(listed, ahead * plane_rows + storage % plane_rows, zs * plane_rows)
-    place = jnp.broadcast_to(place.reshape(1, 4, LANES), (xs, 4, LANES))
-    places = lax.all_to_all(place, "x", 0, 0, tiled=True).reshape(xs, 2, pair_slots)
-    index = places.transpose(1, 0, 2).reshape(2, xs * pair_slots)
+    code = jnp.where(listed, storage, -1).reshape(1, 2 * pair_slots // LANES, LANES)
+    code = jnp.broadcast_to(code, (zs * xs,) + code.shape[1:])
 
     real_part, imag_part = whiten(spectra[0])
     outbound = jnp.concatenate(
@@ -189,15 +223,82 @@
         axis=2,
     ).transpose(1, 0, 2, 3)
     block = lax.all_to_all(outbound, "x", 0, 0, tiled=True).reshape(plane_rows, 8, LANES)
-    blocks = ring(block, "z")
-    partial = correlate(index, blocks, basis_slice(x * share, share, freqs))
-
-    group = xs * ys * cs
-    slots = xs * pair_slots // group
-    shares = lax.all_to_all(
-        partial.reshape(group, slots, LAGS), ("x", "y", "c"), 0, 0, tiled=True
-    )
-    return jnp.sum(shares.astype(jnp.float32), axis=0) / math.sqrt(day_count)
+    block, code = lax.optimization_barrier((block, code))
+    codes = lax.all_to_all(code, ("z", "x"), 0, 0, tiled=True)
+    near = near_ring(block, "z", reach)
+    codes, _, _ = lax.optimization_barrier((codes, near[reach - 2], near[reach + 2]))
+    basis = basis_slice(x * share, share, freqs)
+
+    codes = codes.reshape(zs, xs, 2, days, own).transpose(2, 1, 3, 0, 4)
+    first, second = codes.reshape(2, columns, zs * own)
+    valid = (first >= 0) & (second >= 0)
+    first_plane, second_plane = first // plane_rows, second // plane_rows
+    apart = jnp.mod(second_plane - first_plane, zs)
+    middle = jnp.where(
+        apart <= zs // 2,
+        first_plane + apart // 2,
+        second_plane + (zs - apart) // 2,
+    )
+    middle = jnp.where(valid, jnp.mod(middle, zs), -1)
+
+    planes = jnp.arange(zs, dtype=jnp.int32)
+    middle_by_owner = middle.reshape(columns, zs, own)
+    meets = jnp.sum(
+        (middle_by_owner[None] == planes[:, None, None, None]).astype(jnp.float32), axis=3
+    )
+    slots, returned = 2 * own, own // 2
+    crowded = (jnp.max(jnp.sum(meets, axis=2)) > slots) | (jnp.max(meets) > returned)
+
+    here = middle == z
+    order = jnp.arange(zs * own, dtype=jnp.int32)
+    earlier = (order[:, None] < order[None, :]).astype(jnp.bfloat16)
+    rank = jnp.dot(here.astype(jnp.bfloat16), earlier, preferred_element_type=jnp.float32)
+    rank = jnp.where(here, rank.astype(jnp.int32), -1)
+    first_at = jnp.mod(first_plane - z + reach, zs) * plane_rows + first % plane_rows
+    second_at = jnp.mod(second_plane - z + reach, zs) * plane_rows + second % plane_rows
+    packed = first_at * 4096 + second_at
+    slot_ids = jnp.arange(slots, dtype=jnp.int32)
+    taken = rank[:, None, :] == slot_ids[None, :, None]
+    chosen = jnp.sum(jnp.where(taken, packed[:, None, :], 0), axis=2).reshape(-1)
+    index = jnp.stack([chosen // 4096, chosen % 4096])
+    used = jnp.sum(here.astype(jnp.int32), axis=1)
+
+    mine = lax.dynamic_index_in_dim(meets, column, 1, keepdims=False)
+    sent = lax.dynamic_index_in_dim(mine, z, 0, keepdims=False)
+    begin = jnp.sum(jnp.where(planes[None, :] < planes[:, None], sent[None, :], 0.0), axis=1)
+    places = begin.astype(jnp.int32)[:, None] + jnp.arange(returned, dtype=jnp.int32)[None, :]
+    send = (places.reshape(-1)[:, None] == slot_ids[None, :]).astype(jnp.bfloat16)
+    own_column = lax.dynamic_index_in_dim(middle_by_owner, column, 0, keepdims=False)
+    own_middle = lax.dynamic_index_in_dim(own_column, z, 0, keepdims=False)
+    ids = jnp.arange(own, dtype=jnp.int32)
+    before = (own_middle[:, None] == own_middle[None, :]) & (ids[None, :] < ids[:, None])
+    own_at = own_middle * returned + jnp.sum(before.astype(jnp.int32), axis=1)
+    own_at = jnp.where(own_middle >= 0, own_at, -1)
+    take = (own_at[:, None] == jnp.arange(zs * returned, dtype=jnp.int32)[None, :]).astype(
+        jnp.bfloat16
+    )
+
+    plane_first = lax.dynamic_slice_in_dim(first, z * own, own, 1).reshape(-1)
+    plane_second = lax.dynamic_slice_in_dim(second, z * own, own, 1).reshape(-1)
+    plane_codes = jnp.stack([plane_first, plane_second])
+    plane_at = jnp.mod(plane_codes // plane_rows - z + reach, zs) * plane_rows
+    plane_at = plane_at + jnp.mod(plane_codes, plane_rows)
+    plane_index = jnp.where(plane_codes >= 0, plane_at, zs * plane_rows)
+
+    def by_middle(near):
+        added = exchange_and_add(correlate(index, used, near, basis), columns)
+        leaving = jnp.dot(send, added.astype(jnp.bfloat16), preferred_element_type=jnp.bfloat16)
+        arrived = lax.all_to_all(
+            leaving.reshape(zs, returned, LAGS), "z", 0, 0, tiled=True
+        ).reshape(zs * returned, LAGS)
+        return jnp.dot(take, arrived, preferred_element_type=jnp.float32) * scale
+
+    def by_owner(near):
+        blocks = near + far_ring(near, "z", reach)
+        every = jnp.full((columns,), own, jnp.int32)
+        return exchange_and_add(correlate(plane_index, every, blocks, basis), columns) * scale
+
+    return lax.cond(crowded, by_owner, by_middle, near)
 
 
 def solution(mesh):

time: 165 us -> 190 us (1.15)
  starting transfers between devices: 58.7 us -> 69.4 us
  blocking collectives: 37.6 us -> 27.3 us
  other arithmetic: 5.35 us -> 15.5 us
  waiting for transfers between devices: 47.7 us -> 57.1 us
  local copies, waits for them, and re-layouts: 2.71 us -> 5.45 us
    all_to_all x1 -> x2, waiting for transfers between devices: 0.01 us -> 11.6 us  [the longest x1 6.15 us: body(): codes = lax.all_to_all(code, ('z', 'x'), 0, 0, tiled=True)]
    all_to_all x1 -> x2, starting transfers between devices: 3.25 us -> 13.5 us  [the longest x1 8.68 us: body(): codes = lax.all_to_all(code, ('z', 'x'), 0, 0, tiled=True)]
    all_to_all x2 -> x1, blocking collectives: 37.6 us -> 27.3 us  [exchange_and_add(): shares = lax.all_to_all(columns, ('x', 'y', 'c'), 0, 0, tiled=True)]
    reduce_sum x1 -> x5, other arithmetic: 0.08 us -> 3.87 us  [the longest x1 1.99 us: body(): jnp.sum((middle_by_owner[None] == planes[:, None, None, None]).astype(jnp...]
    another operation x0 -> x8, local copies, waits for them, and re-layouts: none -> 2.67 us  [the longest x5 2.5 us: body(): first, second = codes.reshape(2, columns, zs * own)]
    convert_element_type x0 -> x4, other arithmetic: none -> 2.3 us  [the longest x1 0.87 us: body(): used = jnp.sum(here.astype(jnp.int32), axis=1)]
    ppermute x15, waiting for transfers between devices: 47.7 us -> 45.6 us  [the longest x4 26.2 us: far_ring(): from_below = lax.ppermute(from_below, axis, up)]
  transfers between devices with their start and end apart: 16 -> 17, of which waited for: 9 -> 11; matrix products, arithmetic and copies ran while one was open for 3% -> 3% of each run, Pallas kernels for 0% -> 0%
where the time goes in v2:
time: 190 us; the launch traced here: 189 us
  starting transfers between devices  69.4 us (37%)
  waiting for transfers between devices  57.1 us (30%)
  blocking collectives  27.3 us (14%)
  other arithmetic  15.5 us (8%)
  Pallas kernels  9.19 us (5%)
  local copies, waits for them, and re-layouts  5.45 us (3%)
  matrix products  3.2 us (2%)
    all_to_all x1, blocking collectives, exchange_and_add(): shares = lax.all_to_all(columns, ('x', 'y', 'c'), 0, 0, tiled=True)  27.3 us
    ppermute x4, starting transfers between devices, near_ring(): from_above = lax.ppermute(from_above, axis, down)  26.7 us
    ppermute x4, waiting for transfers between devices, far_ring(): from_below = lax.ppermute(from_below, axis, up)  26.2 us
    ppermute x4, waiting for transfers between devices, near_ring(): from_above = lax.ppermute(from_above, axis, down)  13.7 us
    ppermute x3, starting transfers between devices, far_ring(): from_above = lax.ppermute(from_above, axis, down)  13.7 us
    pallas_call x1, Pallas kernels, correlate(): pl.pallas_call(functools.partial(correlate_kernel, count), out_shape=jax....  9.19 us
    all_to_all x1, starting transfers between devices, body(): codes = lax.all_to_all(code, ('z', 'x'), 0, 0, tiled=True)  8.68 us
    ppermute x4, starting transfers between devices, near_ring(): from_below = lax.ppermute(from_below, axis, up)  7.86 us
  transfers between devices with their start and end apart: 17, of which 11 were waited for; matrix products, arithmetic and copies ran while one was open for 3% of the time, Pallas kernels for 0%

profile of v2, /device:TPU:1, one launch (start us, length us, event | category | flops | bytes accessed | tf_op | source)
XLA Modules:
  0.0 189.0 jit_solution(6789057512313012567)
XLA Ops:
  0.0 1.4 add_sqrt_fusion
  1.7 0.8 fusion.14
  3.5 1.1 copy_bitcast_fusion
  4.6 4.8 %all-to-all-start.3 = ((bf16[4,64,8,128]{3,2,1,0:T(8,128)(2,1)}), bf16[4,64,8,128]{3,2,1,0:T(8,128)(2,1)S(1)}, u32[]{:S(2)}, u32[]{:S(2)}) async-start(bf16[4,64,8,128]{3,2,1,0:T(8,128)(2,1)} %copy_bitcast_fusion), calls=%async_computation.3 | async-start | bytes 1048576 | tf_op jit(solution)/shard_map/all_to_all | solution.py:225
  10.0 1.0 fusion.18
  10.9 5.4 %all-to-all-done.3 = bf16[4,64,8,128]{3,2,1,0:T(8,128)(2,1)S(1)} async-done(((bf16[4,64,8,128]{3,2,1,0:T(8,128)(2,1)}), bf16[4,64,8,128]{3,2,1,0:T(8,128)(2,1)S(1)}, u32[]{:S(2)}, u32[]{:S(2)}) %all-to-all-start.3) | async-done | bytes 524320 | tf_op jit(solution)/shard_map/all_to_all | solution.py:225
  16.4 0.7 broadcast_in_dim.46
  17.0 12.4 %collective-permute-start.9 = (bf16[256,8,128]{2,1,0:T(8,128)(2,1)S(1)}, bf16[256,8,128]{2,1,0:T(8,128)(2,1)S(1)}, u32[]{:S(2)}, u32[]{:S(2)}) collective-permute-start(bf16[256,8,128]{2,1,0:T(8,128)(2,1)S(1)} %bitcast.51), channel_id=1, source_target_pairs={{0,480},{32,0},{64,32},{96,64},{128,96},{160,128},{192,160},{224,1... | collective-permute-start | bytes 1572872 | tf_op jit(solution)/shard_map/ppermute | solution.py:150
  29.5 1.9 %collective-permute-start.7 = (bf16[256,8,128]{2,1,0:T(8,128)(2,1)S(1)}, bf16[256,8,128]{2,1,0:T(8,128)(2,1)S(1)}, u32[]{:S(2)}, u32[]{:S(2)}) collective-permute-start(bf16[256,8,128]{2,1,0:T(8,128)(2,1)S(1)} %bitcast.52), channel_id=1, source_target_pairs={{0,32},{32,64},{64,96},{96,128},{128,160},{160,192},{192,224},{224... | collective-permute-start | bytes 1572872 | tf_op jit(solution)/shard_map/ppermute | solution.py:149
  31.4 8.7 %all-to-all-start.4 = ((s32[64,4,128]{2,1,0:T(4,128)}), s32[64,4,128]{2,1,0:T(4,128)S(1)}, u32[]{:S(2)}, u32[]{:S(2)}) async-start(s32[64,4,128]{2,1,0:T(4,128)} %broadcast_in_dim.46), calls=%async_computation.4 | async-start | bytes 262144 | tf_op jit(solution)/shard_map/all_to_all | solution.py:227
  40.1 4.4 %collective-permute-start.10 = (bf16[256,8,128]{2,1,0:T(8,128)(2,1)S(1)}, bf16[256,8,128]{2,1,0:T(8,128)(2,1)S(1)}, u32[]{:S(2)}, u32[]{:S(2)}) collective-permute-start(bf16[256,8,128]{2,1,0:T(8,128)(2,1)S(1)} %collective-permute-done.9), channel_id=1, source_target_pairs={{0,480},{32,0},{64,32},{96,64},{128,96},{160,128},{192,160},{224,1... | collective-permute-start | bytes 1572872 | tf_op jit(solution)/shard_map/ppermute | solution.py:150
  44.5 1.9 %collective-permute-start.8 = (bf16[256,8,128]{2,1,0:T(8,128)(2,1)S(1)}, bf16[256,8,128]{2,1,0:T(8,128)(2,1)}, u32[]{:S(2)}, u32[]{:S(2)}) collective-permute-start(bf16[256,8,128]{2,1,0:T(8,128)(2,1)S(1)} %collective-permute-done.7), channel_id=1, source_target_pairs={{0,32},{32,64},{64,96},{96,128},{128,160},{160,192},{192,224},{224... | collective-permute-start | bytes 1572872 | tf_op jit(solution)/shard_map/ppermute | solution.py:149
  46.5 2.5 %multiply_convert_fusion.1 = (bf16[512,256]{1,0:T(8,128)(2,1)S(1)}, bf16[512,256]{1,0:T(8,128)(2,1)S(1)}) fusion(s32[256]{0:T(256)S(1)} %iota_add_fusion.2, s32[512]{0:T(512)S(1)} %iota_add_fusion.1), kind=kLoop, calls=%fused_computation.52 | loop fusion | flops 2490368 | bytes 527360 | tf_op jit(solution)/shard_map/convert.1
  49.1 6.1 %all-to-all-done.4 = s32[64,4,128]{2,1,0:T(4,128)S(1)} async-done(((s32[64,4,128]{2,1,0:T(4,128)}), s32[64,4,128]{2,1,0:T(4,128)S(1)}, u32[]{:S(2)}, u32[]{:S(2)}) %all-to-all-start.4) | async-done | bytes 131104 | tf_op jit(solution)/shard_map/all_to_all | solution.py:227
  55.2 2.9 %collective-permute-done.10 = bf16[256,8,128]{2,1,0:T(8,128)(2,1)S(1)} collective-permute-done((bf16[256,8,128]{2,1,0:T(8,128)(2,1)S(1)}, bf16[256,8,128]{2,1,0:T(8,128)(2,1)S(1)}, u32[]{:S(2)}, u32[]{:S(2)}) %collective-permute-start.10) | collective-permute-done | bytes 524320 | tf_op jit(solution)/shard_map/ppermute | solution.py:150
  59.0 1.0 fusion.134
  60.2 1.1 copy.37
  61.5 0.8 fusion.79
  62.3 1.1 fusion.17
  63.4 1.0 fusion.33
  64.4 2.0 %convert_reduce_fusion.1 = (f32[16,32,16]{2,1,0:T(8,128)S(1)}, f32[16,32]{1,0:T(8,128)S(1)}) fusion(s32[32,16,32]{2,1,0:T(8,128)S(1)} %fusion.33), kind=kLoop, calls=%fused_computation.17 | loop fusion | flops 1039872 | bytes 100352 | tf_op jit(solution)/shard_map/reduce_sum | solution.py:246
  67.1 0.6 reduce_max.19
  67.8 0.7 reduce_max.18
  69.9 0.7 fusion.108
  70.6 0.7 fusion.63
  71.6 1.5 select_reduce_fusion
  73.3 4.5 %collective-permute-start.13 = (bf16[256,8,128]{2,1,0:T(8,128)(2,1)S(1)}, bf16[256,8,128]{2,1,0:T(8,128)(2,1)S(1)}, u32[]{:S(2)}, u32[]{:S(2)}) collective-permute-start(bf16[256,8,128]{2,1,0:T(8,128)(2,1)S(1)} %collective-permute-done.10), channel_id=1, source_target_pairs={{0,480},{32,0},{64,32},{96,64},{128,96},{160,128},{192,160},{224,1... | collective-permute-start | bytes 1572872 | tf_op jit(solution)/shard_map/ppermute | solution.py:150
  77.8 1.9 %collective-permute-start.11 = (bf16[256,8,128]{2,1,0:T(8,128)(2,1)}, bf16[256,8,128]{2,1,0:T(8,128)(2,1)S(1)}, u32[]{:S(2)}, u32[]{:S(2)}) collective-permute-start(bf16[256,8,128]{2,1,0:T(8,128)(2,1)} %collective-permute-done.8), channel_id=1, source_target_pairs={{0,32},{32,64},{64,96},{96,128},{128,160},{160,192},{192,224},{224... | collective-permute-start | bytes 1572872 | tf_op jit(solution)/shard_map/ppermute | solution.py:149
  79.8 6.4 %collective-permute-done.13 = bf16[256,8,128]{2,1,0:T(8,128)(2,1)S(1)} collective-permute-done((bf16[256,8,128]{2,1,0:T(8,128)(2,1)S(1)}, bf16[256,8,128]{2,1,0:T(8,128)(2,1)S(1)}, u32[]{:S(2)}, u32[]{:S(2)}) %collective-permute-start.13) | collective-permute-done | bytes 524320 | tf_op jit(solution)/shard_map/ppermute | solution.py:150
  86.2 5.3 %collective-permute-start.14 = (bf16[256,8,128]{2,1,0:T(8,128)(2,1)S(1)}, bf16[256,8,128]{2,1,0:T(8,128)(2,1)S(1)}, u32[]{:S(2)}, u32[]{:S(2)}) collective-permute-start(bf16[256,8,128]{2,1,0:T(8,128)(2,1)S(1)} %collective-permute-done.13), channel_id=1, source_target_pairs={{0,480},{32,0},{64,32},{96,64},{128,96},{160,128},{192,160},{224,1... | collective-permute-start | bytes 1572872 | tf_op jit(solution)/shard_map/ppermute | solution.py:150
  91.5 2.1 %collective-permute-start.12 = (bf16[256,8,128]{2,1,0:T(8,128)(2,1)S(1)}, bf16[256,8,128]{2,1,0:T(8,128)(2,1)S(1)}, u32[]{:S(2)}, u32[]{:S(2)}) collective-permute-start(bf16[256,8,128]{2,1,0:T(8,128)(2,1)S(1)} %collective-permute-done.11), channel_id=1, source_target_pairs={{0,32},{32,64},{64,96},{96,128},{128,160},{160,192},{192,224},{224... | collective-permute-start | bytes 1572872 | tf_op jit(solution)/shard_map/ppermute | solution.py:149
  93.6 0.9 fusion.54
  94.5 4.4 %collective-permute-done.14 = bf16[256,8,128]{2,1,0:T(8,128)(2,1)S(1)} collective-permute-done((bf16[256,8,128]{2,1,0:T(8,128)(2,1)S(1)}, bf16[256,8,128]{2,1,0:T(8,128)(2,1)S(1)}, u32[]{:S(2)}, u32[]{:S(2)}) %collective-permute-start.14) | collective-permute-done | bytes 524320 | tf_op jit(solution)/shard_map/ppermute | solution.py:150
  98.9 5.1 %collective-permute-done.12 = bf16[256,8,128]{2,1,0:T(8,128)(2,1)S(1)} collective-permute-done((bf16[256,8,128]{2,1,0:T(8,128)(2,1)S(1)}, bf16[256,8,128]{2,1,0:T(8,128)(2,1)S(1)}, u32[]{:S(2)}, u32[]{:S(2)}) %collective-permute-start.12) | collective-permute-done | bytes 524320 | tf_op jit(solution)/shard_map/ppermute | solution.py:149
  104.0 84.3 %conditional.1 = (f32[32,256]{1,0:T(8,128)S(1)}) conditional(s32[]{:T(128)} %convert_element_type.85, (s32[1,4,8,16,32]{4,2,0,1,3:T(8,128)S(1)}, s32[2,2048]{1,0:T(2,128)S(1)}, bf16[256,8,128]{2,1,0:T(8,128)(2,1)S(1)}, bf16[256,8,128]{2,1,0:T(8,128)(2,1)S(1)}, bf16[256,8,128]{2,1,0:T(8,128)(2,1)}, /*index=5*/bf16[256,8,128]{2,1,0:T(8,128)(2,1)S(1)}, ...), branch_computations={%region_10.13_spmd, %region_13.15_spmd} | conditional | flops 13115360 | bytes 24810020 | solution.py:301
  104.0 1.9 %collective-permute-start.3 = (bf16[256,8,128]{2,1,0:T(8,128)(2,1)S(1)}, bf16[256,8,128]{2,1,0:T(8,128)(2,1)S(1)}, u32[]{:S(2)}, u32[]{:S(2)}) collective-permute-start(bf16[256,8,128]{2,1,0:T(8,128)(2,1)S(1)} %get-tuple-element.128.refs_0_), channel_id=1, source_target_pairs={{0,32},{32,64},{64,96},{96,128},{128,160},{160,192},{192,224},{224... | collective-permute-start | bytes 1572872 | tf_op jit(solution)/shard_map/cond/branch_1_fun/ppermute | solution.py:162
  106.0 4.6 %collective-permute-start = (bf16[256,8,128]{2,1,0:T(8,128)(2,1)S(1)}, bf16[256,8,128]{2,1,0:T(8,128)(2,1)S(1)}, u32[]{:S(2)}, u32[]{:S(2)}) collective-permute-start(bf16[256,8,128]{2,1,0:T(8,128)(2,1)S(1)} %get-tuple-element.136.refs_8_), channel_id=1, source_target_pairs={{0,480},{32,0},{64,32},{96,64},{128,96},{160,128},{192,160},{224,1... | collective-permute-start | bytes 1572872 | tf_op jit(solution)/shard_map/cond/branch_1_fun/ppermute | solution.py:165
  110.5 5.1 %collective-permute-done.3.refs_15_ = bf16[256,8,128]{2,1,0:T(8,128)(2,1)S(1)} collective-permute-done((bf16[256,8,128]{2,1,0:T(8,128)(2,1)S(1)}, bf16[256,8,128]{2,1,0:T(8,128)(2,1)S(1)}, u32[]{:S(2)}, u32[]{:S(2)}) %collective-permute-start.3) | collective-permute-done | bytes 524320 | tf_op jit(solution)/shard_map/cond/branch_1_fun/ppermute | solution.py:162
  115.6 1.9 %collective-permute-start.4 = (bf16[256,8,128]{2,1,0:T(8,128)(2,1)S(1)}, bf16[256,8,128]{2,1,0:T(8,128)(2,1)S(1)}, u32[]{:S(2)}, u32[]{:S(2)}) collective-permute-start(bf16[256,8,128]{2,1,0:T(8,128)(2,1)S(1)} %collective-permute-done.3.refs_15_), channel_id=1, source_target_pairs={{0,32},{32,64},{64,96},{96,128},{128,160},{160,192},{192,224},{224... | collective-permute-start | bytes 1572872 | tf_op jit(solution)/shard_map/cond/branch_1_fun/ppermute | solution.py:162
  117.5 4.6 %collective-permute-start.1 = (bf16[256,8,128]{2,1,0:T(8,128)(2,1)S(1)}, bf16[256,8,128]{2,1,0:T(8,128)(2,1)S(1)}, u32[]{:S(2)}, u32[]{:S(2)}) collective-permute-start(bf16[256,8,128]{2,1,0:T(8,128)(2,1)S(1)} %collective-permute-done.refs_9_), channel_id=1, source_target_pairs={{0,480},{32,0},{64,32},{96,64},{128,96},{160,128},{192,160},{224,1... | collective-permute-start | bytes 1572872 | tf_op jit(solution)/shard_map/cond/branch_1_fun/ppermute | solution.py:165
  122.1 4.6 %collective-permute-done.4.refs_14_ = bf16[256,8,128]{2,1,0:T(8,128)(2,1)S(1)} collective-permute-done((bf16[256,8,128]{2,1,0:T(8,128)(2,1)S(1)}, bf16[256,8,128]{2,1,0:T(8,128)(2,1)S(1)}, u32[]{:S(2)}, u32[]{:S(2)}) %collective-permute-start.4) | collective-permute-done | bytes 524320 | tf_op jit(solution)/shard_map/cond/branch_1_fun/ppermute | solution.py:162
  126.7 1.9 %collective-permute-start.5 = (bf16[256,8,128]{2,1,0:T(8,128)(2,1)S(1)}, bf16[256,8,128]{2,1,0:T(8,128)(2,1)S(1)}, u32[]{:S(2)}, u32[]{:S(2)}) collective-permute-start(bf16[256,8,128]{2,1,0:T(8,128)(2,1)S(1)} %collective-permute-done.4.refs_14_), channel_id=1, source_target_pairs={{0,32},{32,64},{64,96},{96,128},{128,160},{160,192},{192,224},{224... | collective-permute-start | bytes 1572872 | tf_op jit(solution)/shard_map/cond/branch_1_fun/ppermute | solution.py:162
  128.7 4.6 %collective-permute-start.2 = (bf16[256,8,128]{2,1,0:T(8,128)(2,1)S(1)}, bf16[256,8,128]{2,1,0:T(8,128)(2,1)S(1)}, u32[]{:S(2)}, u32[]{:S(2)}) collective-permute-start(bf16[256,8,128]{2,1,0:T(8,128)(2,1)S(1)} %collective-permute-done.1.refs_10_), channel_id=1, source_target_pairs={{0,480},{32,0},{64,32},{96,64},{128,96},{160,128},{192,160},{224,1... | collective-permute-start | bytes 1572872 | tf_op jit(solution)/shard_map/cond/branch_1_fun/ppermute | solution.py:165
  133.2 5.4 %collective-permute-done.5.refs_13_ = bf16[256,8,128]{2,1,0:T(8,128)(2,1)S(1)} collective-permute-done((bf16[256,8,128]{2,1,0:T(8,128)(2,1)S(1)}, bf16[256,8,128]{2,1,0:T(8,128)(2,1)S(1)}, u32[]{:S(2)}, u32[]{:S(2)}) %collective-permute-start.5) | collective-permute-done | bytes 524320 | tf_op jit(solution)/shard_map/cond/branch_1_fun/ppermute | solution.py:162
  138.7 1.9 %collective-permute-start.6 = (bf16[256,8,128]{2,1,0:T(8,128)(2,1)S(1)}, bf16[256,8,128]{2,1,0:T(8,128)(2,1)S(1)}, u32[]{:S(2)}, u32[]{:S(2)}) collective-permute-start(bf16[256,8,128]{2,1,0:T(8,128)(2,1)S(1)} %collective-permute-done.5.refs_13_), channel_id=1, source_target_pairs={{0,32},{32,64},{64,96},{96,128},{128,160},{160,192},{192,224},{224... | collective-permute-start | bytes 1572872 | tf_op jit(solution)/shard_map/cond/branch_1_fun/ppermute | solution.py:162
  140.7 11.0 %collective-permute-done.6.refs_12_ = bf16[256,8,128]{2,1,0:T(8,128)(2,1)S(1)} collective-permute-done((bf16[256,8,128]{2,1,0:T(8,128)(2,1)S(1)}, bf16[256,8,128]{2,1,0:T(8,128)(2,1)S(1)}, u32[]{:S(2)}, u32[]{:S(2)}) %collective-permute-start.6) | collective-permute-done | bytes 524320 | tf_op jit(solution)/shard_map/cond/branch_1_fun/ppermute | solution.py:162
  151.7 9.2 %branch_1_fun.1 = bf16[1024,256]{1,0:T(8,128)(2,1)S(1)} custom-call(s32[2,1024]{1,0:T(2,128)S(1)} %compare_select_fusion.2.index_ref, s32[32]{0:T(128)S(1)} %broadcast_21_used_ref.0.used_ref, bf16[256,8,128]{2,1,0:T(8,128)(2,1)} %copy-done.8, bf16[256,8,128]{2,1,0:T(8,128)(2,1)} %copy-done.4, bf16[256,8,128]{2,1,0:T(8,128)(2,1)} %get-tuple-element.130.refs_2_, ...), custom_call_target="tpu_custom_call" | custom-call | tf_op jit(solution)/shard_map/cond/branch_1_fun/pallas_call | solution.py:124
  160.9 27.3 %all_to_all.24 = bf16[32,32,256]{2,1,0:T(8,128)(2,1)S(1)} all-to-all(bf16[32,32,256]{2,1,0:T(8,128)(2,1)S(1)} %bitcast.50), channel_id=1, replica_groups=mesh['z'=16,'x'=4,'y'=4,'c'=2] {'x','y','c'}, dimensions={0} | all-to-all | bytes 1048576 | tf_op jit(solution)/shard_map/cond/branch_1_fun/all_to_all | solution.py:183
  (73 shorter events, 5.3 us)
Async XLA Ops:
  1.6 1.2 copy-start
  3.5 5.9 %copy-start.14 = (s32[256,2]{0,1:T(2,128)S(1)}, s32[256,2]{0,1:T(2,128)}, u32[]{:S(2)}) copy-start(s32[256,2]{0,1:T(2,128)} %param.7) | copy-start | bytes 6148
  3.5 5.9 %copy-start.13 = (s32[4096]{0:T(1024)S(1)}, s32[4096]{0:T(1024)}, u32[]{:S(2)}) copy-start(s32[4096]{0:T(1024)} %param.8) | copy-start | bytes 49156
  4.6 11.8 %all-to-all-start.3 = ((bf16[4,64,8,128]{3,2,1,0:T(8,128)(2,1)}), bf16[4,64,8,128]{3,2,1,0:T(8,128)(2,1)S(1)}, u32[]{:S(2)}, u32[]{:S(2)}) async-start(bf16[4,64,8,128]{3,2,1,0:T(8,128)(2,1)} %copy_bitcast_fusion), calls=%async_computation.3 | async-start | bytes 1048576 | tf_op jit(solution)/shard_map/all_to_all | solution.py:225
  17.0 23.1 %collective-permute-start.9 = (bf16[256,8,128]{2,1,0:T(8,128)(2,1)S(1)}, bf16[256,8,128]{2,1,0:T(8,128)(2,1)S(1)}, u32[]{:S(2)}, u32[]{:S(2)}) collective-permute-start(bf16[256,8,128]{2,1,0:T(8,128)(2,1)S(1)} %bitcast.51), channel_id=1, source_target_pairs={{0,480},{32,0},{64,32},{96,64},{128,96},{160,128},{192,160},{224,1... | collective-permute-start | bytes 1572872 | tf_op jit(solution)/shard_map/ppermute | solution.py:150
  29.5 15.1 %collective-permute-start.7 = (bf16[256,8,128]{2,1,0:T(8,128)(2,1)S(1)}, bf16[256,8,128]{2,1,0:T(8,128)(2,1)S(1)}, u32[]{:S(2)}, u32[]{:S(2)}) collective-permute-start(bf16[256,8,128]{2,1,0:T(8,128)(2,1)S(1)} %bitcast.52), channel_id=1, source_target_pairs={{0,32},{32,64},{64,96},{96,128},{128,160},{160,192},{192,224},{224... | collective-permute-start | bytes 1572872 | tf_op jit(solution)/shard_map/ppermute | solution.py:149
  31.4 23.8 %all-to-all-start.4 = ((s32[64,4,128]{2,1,0:T(4,128)}), s32[64,4,128]{2,1,0:T(4,128)S(1)}, u32[]{:S(2)}, u32[]{:S(2)}) async-start(s32[64,4,128]{2,1,0:T(4,128)} %broadcast_in_dim.46), calls=%async_computation.4 | async-start | bytes 262144 | tf_op jit(solution)/shard_map/all_to_all | solution.py:227
  40.1 18.0 %collective-permute-start.10 = (bf16[256,8,128]{2,1,0:T(8,128)(2,1)S(1)}, bf16[256,8,128]{2,1,0:T(8,128)(2,1)S(1)}, u32[]{:S(2)}, u32[]{:S(2)}) collective-permute-start(bf16[256,8,128]{2,1,0:T(8,128)(2,1)S(1)} %collective-permute-done.9), channel_id=1, source_target_pairs={{0,480},{32,0},{64,32},{96,64},{128,96},{160,128},{192,160},{224,1... | collective-permute-start | bytes 1572872 | tf_op jit(solution)/shard_map/ppermute | solution.py:150
  44.5 14.2 %collective-permute-start.8 = (bf16[256,8,128]{2,1,0:T(8,128)(2,1)S(1)}, bf16[256,8,128]{2,1,0:T(8,128)(2,1)}, u32[]{:S(2)}, u32[]{:S(2)}) collective-permute-start(bf16[256,8,128]{2,1,0:T(8,128)(2,1)S(1)} %collective-permute-done.7), channel_id=1, source_target_pairs={{0,32},{32,64},{64,96},{96,128},{128,160},{160,192},{192,224},{224... | collective-permute-start | bytes 1572872 | tf_op jit(solution)/shard_map/ppermute | solution.py:149
  62.3 1.1 copy-start.9
  62.3 1.1 copy-start.10
  71.4 32.6 %copy-start.11 = (bf16[256,64]{1,0:T(8,128)(2,1)S(1)}, bf16[256,64]{1,0:T(8,128)(2,1)}, u32[]{:S(2)}) copy-start(bf16[256,64]{1,0:T(8,128)(2,1)} %fusion.63) | copy-start | bytes 98308
  73.3 12.9 %collective-permute-start.13 = (bf16[256,8,128]{2,1,0:T(8,128)(2,1)S(1)}, bf16[256,8,128]{2,1,0:T(8,128)(2,1)S(1)}, u32[]{:S(2)}, u32[]{:S(2)}) collective-permute-start(bf16[256,8,128]{2,1,0:T(8,128)(2,1)S(1)} %collective-permute-done.10), channel_id=1, source_target_pairs={{0,480},{32,0},{64,32},{96,64},{128,96},{160,128},{192,160},{224,1... | collective-permute-start | bytes 1572872 | tf_op jit(solution)/shard_map/ppermute | solution.py:150
  77.8 13.7 %collective-permute-start.11 = (bf16[256,8,128]{2,1,0:T(8,128)(2,1)}, bf16[256,8,128]{2,1,0:T(8,128)(2,1)S(1)}, u32[]{:S(2)}, u32[]{:S(2)}) collective-permute-start(bf16[256,8,128]{2,1,0:T(8,128)(2,1)} %collective-permute-done.8), channel_id=1, source_target_pairs={{0,32},{32,64},{64,96},{96,128},{128,160},{160,192},{192,224},{224... | collective-permute-start | bytes 1572872 | tf_op jit(solution)/shard_map/ppermute | solution.py:149
  86.2 12.8 %collective-permute-start.14 = (bf16[256,8,128]{2,1,0:T(8,128)(2,1)S(1)}, bf16[256,8,128]{2,1,0:T(8,128)(2,1)S(1)}, u32[]{:S(2)}, u32[]{:S(2)}) collective-permute-start(bf16[256,8,128]{2,1,0:T(8,128)(2,1)S(1)} %collective-permute-done.13), channel_id=1, source_target_pairs={{0,480},{32,0},{64,32},{96,64},{128,96},{160,128},{192,160},{224,1... | collective-permute-start | bytes 1572872 | tf_op jit(solution)/shard_map/ppermute | solution.py:150
  91.5 12.5 %collective-permute-start.12 = (bf16[256,8,128]{2,1,0:T(8,128)(2,1)S(1)}, bf16[256,8,128]{2,1,0:T(8,128)(2,1)S(1)}, u32[]{:S(2)}, u32[]{:S(2)}) collective-permute-start(bf16[256,8,128]{2,1,0:T(8,128)(2,1)S(1)} %collective-permute-done.11), channel_id=1, source_target_pairs={{0,32},{32,64},{64,96},{96,128},{128,160},{160,192},{192,224},{224... | collective-permute-start | bytes 1572872 | tf_op jit(solution)/shard_map/ppermute | solution.py:149
  104.0 47.7 %copy-start.2 = (bf16[256,8,128]{2,1,0:T(8,128)(2,1)}, bf16[256,8,128]{2,1,0:T(8,128)(2,1)S(1)}, u32[]{:S(2)}) copy-start(bf16[256,8,128]{2,1,0:T(8,128)(2,1)S(1)} %get-tuple-element.135.refs_7_) | copy-start | bytes 1572868 | tf_op jit(solution)/shard_map/cond
  104.0 47.7 %copy-start.4 = (bf16[256,8,128]{2,1,0:T(8,128)(2,1)}, bf16[256,8,128]{2,1,0:T(8,128)(2,1)S(1)}, u32[]{:S(2)}) copy-start(bf16[256,8,128]{2,1,0:T(8,128)(2,1)S(1)} %get-tuple-element.129.refs_1_) | copy-start | bytes 1572868 | tf_op jit(solution)/shard_map/cond
  104.0 47.7 %copy-start.6 = (bf16[256,8,128]{2,1,0:T(8,128)(2,1)}, bf16[256,8,128]{2,1,0:T(8,128)(2,1)S(1)}, u32[]{:S(2)}) copy-start(bf16[256,8,128]{2,1,0:T(8,128)(2,1)S(1)} %get-tuple-element.136.refs_8_) | copy-start | bytes 1572868 | tf_op jit(solution)/shard_map/cond
  104.0 47.7 %copy-start.8 = (bf16[256,8,128]{2,1,0:T(8,128)(2,1)}, bf16[256,8,128]{2,1,0:T(8,128)(2,1)S(1)}, u32[]{:S(2)}) copy-start(bf16[256,8,128]{2,1,0:T(8,128)(2,1)S(1)} %get-tuple-element.128.refs_0_) | copy-start | bytes 1572868 | tf_op jit(solution)/shard_map/cond
  104.0 11.6 %collective-permute-start.3 = (bf16[256,8,128]{2,1,0:T(8,128)(2,1)S(1)}, bf16[256,8,128]{2,1,0:T(8,128)(2,1)S(1)}, u32[]{:S(2)}, u32[]{:S(2)}) collective-permute-start(bf16[256,8,128]{2,1,0:T(8,128)(2,1)S(1)} %get-tuple-element.128.refs_0_), channel_id=1, source_target_pairs={{0,32},{32,64},{64,96},{96,128},{128,160},{160,192},{192,224},{224... | collective-permute-start | bytes 1572872 | tf_op jit(solution)/shard_map/cond/branch_1_fun/ppermute | solution.py:162
  106.0 11.6 %collective-permute-start = (bf16[256,8,128]{2,1,0:T(8,128)(2,1)S(1)}, bf16[256,8,128]{2,1,0:T(8,128)(2,1)S(1)}, u32[]{:S(2)}, u32[]{:S(2)}) collective-permute-start(bf16[256,8,128]{2,1,0:T(8,128)(2,1)S(1)} %get-tuple-element.136.refs_8_), channel_id=1, source_target_pairs={{0,480},{32,0},{64,32},{96,64},{128,96},{160,128},{192,160},{224,1... | collective-permute-start | bytes 1572872 | tf_op jit(solution)/shard_map/cond/branch_1_fun/ppermute | solution.py:165
  115.6 11.1 %collective-permute-start.4 = (bf16[256,8,128]{2,1,0:T(8,128)(2,1)S(1)}, bf16[256,8,128]{2,1,0:T(8,128)(2,1)S(1)}, u32[]{:S(2)}, u32[]{:S(2)}) collective-permute-start(bf16[256,8,128]{2,1,0:T(8,128)(2,1)S(1)} %collective-permute-done.3.refs_15_), channel_id=1, source_target_pairs={{0,32},{32,64},{64,96},{96,128},{128,160},{160,192},{192,224},{224... | collective-permute-start | bytes 1572872 | tf_op jit(solution)/shard_map/cond/branch_1_fun/ppermute | solution.py:162
  117.5 11.1 %collective-permute-start.1 = (bf16[256,8,128]{2,1,0:T(8,128)(2,1)S(1)}, bf16[256,8,128]{2,1,0:T(8,128)(2,1)S(1)}, u32[]{:S(2)}, u32[]{:S(2)}) collective-permute-start(bf16[256,8,128]{2,1,0:T(8,128)(2,1)S(1)} %collective-permute-done.refs_9_), channel_id=1, source_target_pairs={{0,480},{32,0},{64,32},{96,64},{128,96},{160,128},{192,160},{224,1... | collective-permute-start | bytes 1572872 | tf_op jit(solution)/shard_map/cond/branch_1_fun/ppermute | solution.py:165
  126.7 11.9 %collective-permute-start.5 = (bf16[256,8,128]{2,1,0:T(8,128)(2,1)S(1)}, bf16[256,8,128]{2,1,0:T(8,128)(2,1)S(1)}, u32[]{:S(2)}, u32[]{:S(2)}) collective-permute-start(bf16[256,8,128]{2,1,0:T(8,128)(2,1)S(1)} %collective-permute-done.4.refs_14_), channel_id=1, source_target_pairs={{0,32},{32,64},{64,96},{96,128},{128,160},{160,192},{192,224},{224... | collective-permute-start | bytes 1572872 | tf_op jit(solution)/shard_map/cond/branch_1_fun/ppermute | solution.py:162
  128.7 12.0 %collective-permute-start.2 = (bf16[256,8,128]{2,1,0:T(8,128)(2,1)S(1)}, bf16[256,8,128]{2,1,0:T(8,128)(2,1)S(1)}, u32[]{:S(2)}, u32[]{:S(2)}) collective-permute-start(bf16[256,8,128]{2,1,0:T(8,128)(2,1)S(1)} %collective-permute-done.1.refs_10_), channel_id=1, source_target_pairs={{0,480},{32,0},{64,32},{96,64},{128,96},{160,128},{192,160},{224,1... | collective-permute-start | bytes 1572872 | tf_op jit(solution)/shard_map/cond/branch_1_fun/ppermute | solution.py:165
  138.7 13.0 %collective-permute-start.6 = (bf16[256,8,128]{2,1,0:T(8,128)(2,1)S(1)}, bf16[256,8,128]{2,1,0:T(8,128)(2,1)S(1)}, u32[]{:S(2)}, u32[]{:S(2)}) collective-permute-start(bf16[256,8,128]{2,1,0:T(8,128)(2,1)S(1)} %collective-permute-done.5.refs_13_), channel_id=1, source_target_pairs={{0,32},{32,64},{64,96},{96,128},{128,160},{160,192},{192,224},{224... | collective-permute-start | bytes 1572872 | tf_op jit(solution)/shard_map/cond/branch_1_fun/ppermute | solution.py:162
  188.3 0.6 copy-start.12

commit v3 on v2

--- a/solution.py
+++ b/solution.py
@@ -141,16 +141,20 @@
     return up, down
 
 
-def near_ring(block, axis, reach):
+def near_ring(block, axis, reach, codes, basis):
     up, down = shifts(lax.axis_size(axis))
     below, above = [], []
     from_below = from_above = block
-    for _ in range(reach):
+    for step in range(reach):
+        if step == 2:
+            from_below, from_above, codes, basis = lax.optimization_barrier(
+                (from_below, from_above, codes, basis)
+            )
         from_below = lax.ppermute(from_below, axis, up)
         from_above = lax.ppermute(from_above, axis, down)
         below.append(from_below)
         above.append(from_above)
-    return below[::-1] + [block] + above
+    return below[::-1] + [block] + above, codes, basis
 
 
 def far_ring(near, axis, reach):
@@ -225,43 +229,56 @@
     block = lax.all_to_all(outbound, "x", 0, 0, tiled=True).reshape(plane_rows, 8, LANES)
     block, code = lax.optimization_barrier((block, code))
     codes = lax.all_to_all(code, ("z", "x"), 0, 0, tiled=True)
-    near = near_ring(block, "z", reach)
-    codes, _, _ = lax.optimization_barrier((codes, near[reach - 2], near[reach + 2]))
     basis = basis_slice(x * share, share, freqs)
-
-    codes = codes.reshape(zs, xs, 2, days, own).transpose(2, 1, 3, 0, 4)
-    first, second = codes.reshape(2, columns, zs * own)
-    valid = (first >= 0) & (second >= 0)
-    first_plane, second_plane = first // plane_rows, second // plane_rows
-    apart = jnp.mod(second_plane - first_plane, zs)
-    middle = jnp.where(
-        apart <= zs // 2,
-        first_plane + apart // 2,
-        second_plane + (zs - apart) // 2,
-    )
-    middle = jnp.where(valid, jnp.mod(middle, zs), -1)
+    near, codes, basis = near_ring(block, "z", reach, codes, basis)
 
     planes = jnp.arange(zs, dtype=jnp.int32)
+    slots, returned = 2 * own, own // 2
+    slot_ids = jnp.arange(slots, dtype=jnp.int32)
+
+    def bookkeeping(codes):
+        codes = codes.reshape(zs, xs, 2, days, own).transpose(2, 1, 3, 0, 4)
+        first, second = codes.reshape(2, columns, zs * own)
+        valid = (first >= 0) & (second >= 0)
+        first_plane, second_plane = first // plane_rows, second // plane_rows
+        apart = jnp.mod(second_plane - first_plane, zs)
+        middle = jnp.where(
+            apart <= zs // 2,
+            first_plane + apart // 2,
+            second_plane + (zs - apart) // 2,
+        )
+        middle = jnp.where(valid, jnp.mod(middle, zs), -1)
+
+        here = middle == z
+        order = jnp.arange(zs * own, dtype=jnp.int32)
+        earlier = (order[:, None] < order[None, :]).astype(jnp.bfloat16)
+        rank = jnp.dot(here.astype(jnp.bfloat16), earlier, preferred_element_type=jnp.float32)
+        rank = jnp.where(here, rank.astype(jnp.int32), -1)
+        first_at = jnp.mod(first_plane - z + reach, zs) * plane_rows + first % plane_rows
+        second_at = jnp.mod(second_plane - z + reach, zs) * plane_rows + second % plane_rows
+        packed = first_at * 4096 + second_at
+        taken = rank[:, None, :] == slot_ids[None, :, None]
+        chosen = jnp.sum(jnp.where(taken, packed[:, None, :], 0), axis=2).reshape(-1)
+        index = jnp.stack([chosen // 4096, chosen % 4096])
+        used = jnp.minimum(jnp.sum(here.astype(jnp.int32), axis=1), slots)
+        return index, used, middle
+
+    def nothing(codes):
+        return (
+            jnp.zeros((2, columns * slots), jnp.int32),
+            jnp.zeros((columns,), jnp.int32),
+            jnp.full((columns, zs * own), -1, jnp.int32),
+        )
+
+    index, used, middle = lax.cond(codes[0, 0, 0] >= -1, bookkeeping, nothing, codes)
+    partial = correlate(index, used, near, basis)
+    added = exchange_and_add(partial, columns)
+
     middle_by_owner = middle.reshape(columns, zs, own)
     meets = jnp.sum(
         (middle_by_owner[None] == planes[:, None, None, None]).astype(jnp.float32), axis=3
     )
-    slots, returned = 2 * own, own // 2
     crowded = (jnp.max(jnp.sum(meets, axis=2)) > slots) | (jnp.max(meets) > returned)
-
-    here = middle == z
-    order = jnp.arange(zs * own, dtype=jnp.int32)
-    earlier = (order[:, None] < order[None, :]).astype(jnp.bfloat16)
-    rank = jnp.dot(here.astype(jnp.bfloat16), earlier, preferred_element_type=jnp.float32)
-    rank = jnp.where(here, rank.astype(jnp.int32), -1)
-    first_at = jnp.mod(first_plane - z + reach, zs) * plane_rows + first % plane_rows
-    second_at = jnp.mod(second_plane - z + reach, zs) * plane_rows + second % plane_rows
-    packed = first_at * 4096 + second_at
-    slot_ids = jnp.arange(slots, dtype=jnp.int32)
-    taken = rank[:, None, :] == slot_ids[None, :, None]
-    chosen = jnp.sum(jnp.where(taken, packed[:, None, :], 0), axis=2).reshape(-1)
-    index = jnp.stack([chosen // 4096, chosen % 4096])
-    used = jnp.sum(here.astype(jnp.int32), axis=1)
 
     mine = lax.dynamic_index_in_dim(meets, column, 1, keepdims=False)
     sent = lax.dynamic_index_in_dim(mine, z, 0, keepdims=False)
@@ -277,28 +294,25 @@
     take = (own_at[:, None] == jnp.arange(zs * returned, dtype=jnp.int32)[None, :]).astype(
         jnp.bfloat16
     )
-
-    plane_first = lax.dynamic_slice_in_dim(first, z * own, own, 1).reshape(-1)
-    plane_second = lax.dynamic_slice_in_dim(second, z * own, own, 1).reshape(-1)
-    plane_codes = jnp.stack([plane_first, plane_second])
-    plane_at = jnp.mod(plane_codes // plane_rows - z + reach, zs) * plane_rows
-    plane_at = plane_at + jnp.mod(plane_codes, plane_rows)
-    plane_index = jnp.where(plane_codes >= 0, plane_at, zs * plane_rows)
-
-    def by_middle(near):
-        added = exchange_and_add(correlate(index, used, near, basis), columns)
-        leaving = jnp.dot(send, added.astype(jnp.bfloat16), preferred_element_type=jnp.bfloat16)
-        arrived = lax.all_to_all(
-            leaving.reshape(zs, returned, LAGS), "z", 0, 0, tiled=True
-        ).reshape(zs * returned, LAGS)
-        return jnp.dot(take, arrived, preferred_element_type=jnp.float32) * scale
-
-    def by_owner(near):
+    leaving = jnp.dot(send, added.astype(jnp.bfloat16), preferred_element_type=jnp.bfloat16)
+    arrived = lax.all_to_all(
+        leaving.reshape(zs, returned, LAGS), "z", 0, 0, tiled=True
+    ).reshape(zs * returned, LAGS)
+    by_middle = jnp.dot(take, arrived, preferred_element_type=jnp.float32) * scale
+
+    def by_owner(near, codes, by_middle):
+        plane = lax.dynamic_slice_in_dim(codes.reshape(zs, xs, 2, pair_slots), z, 1, 0)
+        plane_codes = plane[0].transpose(1, 0, 2).reshape(2, xs * pair_slots)
+        plane_at = jnp.mod(plane_codes // plane_rows - z + reach, zs) * plane_rows
+        plane_at = plane_at + jnp.mod(plane_codes, plane_rows)
+        plane_index = jnp.where(plane_codes >= 0, plane_at, zs * plane_rows)
         blocks = near + far_ring(near, "z", reach)
         every = jnp.full((columns,), own, jnp.int32)
         return exchange_and_add(correlate(plane_index, every, blocks, basis), columns) * scale
 
-    return lax.cond(crowded, by_owner, by_middle, near)
+    return lax.cond(
+        crowded, by_owner, lambda near, codes, by_middle: by_middle, near, codes, by_middle
+    )
 
 
 def solution(mesh):

time: 190 us -> 158 us (0.83)
  blocking collectives: 27.3 us -> 0 us
  waiting for transfers between devices: 57.1 us -> 42.3 us
  Pallas kernels: 9.19 us -> 12.2 us
  local copies, waits for them, and re-layouts: 5.45 us -> 7.97 us
  matrix products: 3.2 us -> 5.31 us
    all_to_all x1 -> x0, blocking collectives: 27.3 us -> none  [exchange_and_add(): shares = lax.all_to_all(columns, ('x', 'y', 'c'), 0, 0, tiled=True)]
    ppermute x7 -> x0, waiting for transfers between devices: 26.2 us -> none  [the longest x4 26.2 us: far_ring(): from_below = lax.ppermute(from_below, axis, up)]
    all_to_all x0 -> x2, waiting for transfers between devices: none -> 22.6 us  [the longest x1 14.1 us: exchange_and_add(): shares = lax.all_to_all(columns, ('x', 'y', 'c'), 0, 0, tiled=True)]
    all_to_all x0 -> x2, starting transfers between devices: none -> 22.5 us  [the longest x1 13.5 us: exchange_and_add(): shares = lax.all_to_all(columns, ('x', 'y', 'c'), 0, 0, tiled=True)]
    ppermute x7 -> x0, starting transfers between devices: 21.4 us -> none  [the longest x3 13.7 us: far_ring(): from_above = lax.ppermute(from_above, axis, down)]
    ppermute x4, waiting for transfers between devices: 13.7 us -> 2.83 us  [near_ring(): from_above = lax.ppermute(from_above, axis, down)]
    ppermute x4, starting transfers between devices: 7.86 us -> 11.9 us  [near_ring(): from_below = lax.ppermute(from_below, axis, up)]
    ppermute x4, starting transfers between devices: 26.7 us -> 23.3 us  [near_ring(): from_above = lax.ppermute(from_above, axis, down)]
  transfers between devices with their start and end apart: 17 -> 12, of which waited for: 11 -> 7; matrix products, arithmetic and copies ran while one was open for 3% -> 12% of each run, Pallas kernels for 0% -> 0%
where the time goes in v3:
time: 158 us; the launch traced here: 156 us
  starting transfers between devices  71.2 us (45%)
  waiting for transfers between devices  42.3 us (27%)
  other arithmetic  14.6 us (9%)
  Pallas kernels  12.2 us (8%)
  local copies, waits for them, and re-layouts  7.97 us (5%)
  matrix products  5.31 us (3%)
  between operations  2.27 us (1%)
    ppermute x4, starting transfers between devices, near_ring(): from_above = lax.ppermute(from_above, axis, down)  23.3 us
    all_to_all x1, waiting for transfers between devices, exchange_and_add(): shares = lax.all_to_all(columns, ('x', 'y', 'c'), 0, 0, tiled=True)  14.1 us
    all_to_all x1, starting transfers between devices, exchange_and_add(): shares = lax.all_to_all(columns, ('x', 'y', 'c'), 0, 0, tiled=True)  13.5 us
    pallas_call x1, Pallas kernels, correlate(): pl.pallas_call(functools.partial(correlate_kernel, count), out_shape=jax....  12.2 us
    ppermute x4, starting transfers between devices, near_ring(): from_below = lax.ppermute(from_below, axis, up)  11.9 us
    all_to_all x1, starting transfers between devices, body(): lax.all_to_all(leaving.reshape(zs, returned, LAGS), 'z', 0, 0, tiled=True)  9 us
    all_to_all x1, starting transfers between devices, body(): codes = lax.all_to_all(code, ('z', 'x'), 0, 0, tiled=True)  8.68 us
    all_to_all x1, waiting for transfers between devices, body(): lax.all_to_all(leaving.reshape(zs, returned, LAGS), 'z', 0, 0, tiled=True)  8.49 us
  transfers between devices with their start and end apart: 12, of which 7 were waited for; matrix products, arithmetic and copies ran while one was open for 12% of the time, Pallas kernels for 0%

profile of v3, /device:TPU:1, one launch (start us, length us, event | category | flops | bytes accessed | tf_op | source)
XLA Modules:
  0.0 155.9 jit_solution(15711496998439681812)
XLA Ops:
  0.0 1.4 add_sqrt_fusion
  1.7 0.8 fusion.93
  2.5 0.4 copy-done.2
  2.9 0.2 fusion.100
  3.5 1.1 copy_bitcast_fusion.2
  4.6 4.8 %all-to-all-start.1 = ((bf16[4,64,8,128]{3,2,1,0:T(8,128)(2,1)}), bf16[4,64,8,128]{3,2,1,0:T(8,128)(2,1)S(1)}, u32[]{:S(2)}, u32[]{:S(2)}) async-start(bf16[4,64,8,128]{3,2,1,0:T(8,128)(2,1)} %copy_bitcast_fusion.2), calls=%async_computation.1 | async-start | bytes 1048576 | tf_op jit(solution)/shard_map/all_to_all | solution.py:229
  9.6 0.3 fusion.102
  10.0 1.0 fusion.96
  10.9 5.4 %all-to-all-done.1 = bf16[4,64,8,128]{3,2,1,0:T(8,128)(2,1)S(1)} async-done(((bf16[4,64,8,128]{3,2,1,0:T(8,128)(2,1)}), bf16[4,64,8,128]{3,2,1,0:T(8,128)(2,1)S(1)}, u32[]{:S(2)}, u32[]{:S(2)}) %all-to-all-start.1) | async-done | bytes 524320 | tf_op jit(solution)/shard_map/all_to_all | solution.py:229
  16.4 0.7 broadcast_in_dim.50
  17.0 12.4 %collective-permute-start.9 = (bf16[256,8,128]{2,1,0:T(8,128)(2,1)S(1)}, bf16[256,8,128]{2,1,0:T(8,128)(2,1)S(1)}, u32[]{:S(2)}, u32[]{:S(2)}) collective-permute-start(bf16[256,8,128]{2,1,0:T(8,128)(2,1)S(1)} %bitcast.95), channel_id=1, source_target_pairs={{0,480},{32,0},{64,32},{96,64},{128,96},{160,128},{192,160},{224,1... | collective-permute-start | bytes 1572872 | tf_op jit(solution)/shard_map/ppermute | solution.py:154
  29.5 1.9 %collective-permute-start.7 = (bf16[256,8,128]{2,1,0:T(8,128)(2,1)S(1)}, bf16[256,8,128]{2,1,0:T(8,128)(2,1)S(1)}, u32[]{:S(2)}, u32[]{:S(2)}) collective-permute-start(bf16[256,8,128]{2,1,0:T(8,128)(2,1)S(1)} %bitcast.96), channel_id=1, source_target_pairs={{0,32},{32,64},{64,96},{96,128},{128,160},{160,192},{192,224},{224... | collective-permute-start | bytes 1572872 | tf_op jit(solution)/shard_map/ppermute | solution.py:153
  31.4 8.7 %all-to-all-start.2 = ((s32[64,4,128]{2,1,0:T(4,128)}), s32[64,4,128]{2,1,0:T(4,128)S(1)}, u32[]{:S(2)}, u32[]{:S(2)}) async-start(s32[64,4,128]{2,1,0:T(4,128)} %broadcast_in_dim.50), calls=%async_computation.2 | async-start | bytes 262144 | tf_op jit(solution)/shard_map/all_to_all | solution.py:231
  40.1 4.4 %collective-permute-start.10 = (bf16[256,8,128]{2,1,0:T(8,128)(2,1)S(1)}, bf16[256,8,128]{2,1,0:T(8,128)(2,1)S(1)}, u32[]{:S(2)}, u32[]{:S(2)}) collective-permute-start(bf16[256,8,128]{2,1,0:T(8,128)(2,1)S(1)} %collective-permute-done.9.refs_5_), channel_id=1, source_target_pairs={{0,480},{32,0},{64,32},{96,64},{128,96},{160,128},{192,160},{224,1... | collective-permute-start | bytes 1572872 | tf_op jit(solution)/shard_map/ppermute | solution.py:154
  44.6 1.9 %collective-permute-start.8 = (bf16[256,8,128]{2,1,0:T(8,128)(2,1)S(1)}, bf16[256,8,128]{2,1,0:T(8,128)(2,1)S(1)}, u32[]{:S(2)}, u32[]{:S(2)}) collective-permute-start(bf16[256,8,128]{2,1,0:T(8,128)(2,1)S(1)} %collective-permute-done.7.refs_3_), channel_id=1, source_target_pairs={{0,32},{32,64},{64,96},{96,128},{128,160},{160,192},{192,224},{224... | collective-permute-start | bytes 1572872 | tf_op jit(solution)/shard_map/ppermute | solution.py:153
  46.5 2.5 %multiply_convert_fusion.1 = (bf16[512,256]{1,0:T(8,128)(2,1)S(1)}, bf16[512,256]{1,0:T(8,128)(2,1)S(1)}) fusion(s32[256]{0:T(256)S(1)} %iota_add_fusion.2, s32[512]{0:T(512)S(1)} %iota_add_fusion.1), kind=kLoop, calls=%fused_computation.229 | loop fusion | flops 2490368 | bytes 527360 | tf_op jit(solution)/shard_map/convert.2
  49.1 6.2 %all-to-all-done.2 = s32[64,4,128]{2,1,0:T(4,128)S(1)} async-done(((s32[64,4,128]{2,1,0:T(4,128)}), s32[64,4,128]{2,1,0:T(4,128)S(1)}, u32[]{:S(2)}, u32[]{:S(2)}) %all-to-all-start.2) | async-done | bytes 131104 | tf_op jit(solution)/shard_map/all_to_all | solution.py:231
  55.2 2.8 %collective-permute-done.10.refs_6_ = bf16[256,8,128]{2,1,0:T(8,128)(2,1)S(1)} collective-permute-done((bf16[256,8,128]{2,1,0:T(8,128)(2,1)S(1)}, bf16[256,8,128]{2,1,0:T(8,128)(2,1)S(1)}, u32[]{:S(2)}, u32[]{:S(2)}) %collective-permute-start.10) | collective-permute-done | bytes 524320 | tf_op jit(solution)/shard_map/ppermute | solution.py:154
  58.1 0.6 collective-permute-done.8.refs_2_
  58.7 3.1 %collective-permute-start.11 = (bf16[256,8,128]{2,1,0:T(8,128)(2,1)S(1)}, bf16[256,8,128]{2,1,0:T(8,128)(2,1)}, u32[]{:S(2)}, u32[]{:S(2)}) collective-permute-start(bf16[256,8,128]{2,1,0:T(8,128)(2,1)S(1)} %collective-permute-done.8.refs_2_), channel_id=1, source_target_pairs={{0,32},{32,64},{64,96},{96,128},{128,160},{160,192},{192,224},{224... | collective-permute-start | bytes 1572872 | tf_op jit(solution)/shard_map/ppermute | solution.py:153
  61.8 3.4 %collective-permute-start.13 = (bf16[256,8,128]{2,1,0:T(8,128)(2,1)S(1)}, bf16[256,8,128]{2,1,0:T(8,128)(2,1)}, u32[]{:S(2)}, u32[]{:S(2)}) collective-permute-start(bf16[256,8,128]{2,1,0:T(8,128)(2,1)S(1)} %collective-permute-done.10.refs_6_), channel_id=1, source_target_pairs={{0,480},{32,0},{64,32},{96,64},{128,96},{160,128},{192,160},{224,1... | collective-permute-start | bytes 1572872 | tf_op jit(solution)/shard_map/ppermute | solution.py:154
  65.2 4.7 %collective-permute-done.11.refs_1_ = bf16[256,8,128]{2,1,0:T(8,128)(2,1)} collective-permute-done((bf16[256,8,128]{2,1,0:T(8,128)(2,1)S(1)}, bf16[256,8,128]{2,1,0:T(8,128)(2,1)}, u32[]{:S(2)}, u32[]{:S(2)}) %collective-permute-start.11) | collective-permute-done | bytes 524320 | tf_op jit(solution)/shard_map/ppermute | solution.py:153
  69.9 4.9 %collective-permute-start.12 = (bf16[256,8,128]{2,1,0:T(8,128)(2,1)}, bf16[256,8,128]{2,1,0:T(8,128)(2,1)}, u32[]{:S(2)}, u32[]{:S(2)}) collective-permute-start(bf16[256,8,128]{2,1,0:T(8,128)(2,1)} %collective-permute-done.11.refs_1_), channel_id=1, source_target_pairs={{0,32},{32,64},{64,96},{96,128},{128,160},{160,192},{192,224},{224... | collective-permute-start | bytes 1572872 | tf_op jit(solution)/shard_map/ppermute | solution.py:153
  74.8 3.0 %collective-permute-start.14 = (bf16[256,8,128]{2,1,0:T(8,128)(2,1)}, bf16[256,8,128]{2,1,0:T(8,128)(2,1)}, u32[]{:S(2)}, u32[]{:S(2)}) collective-permute-start(bf16[256,8,128]{2,1,0:T(8,128)(2,1)} %collective-permute-done.13.refs_7_), channel_id=1, source_target_pairs={{0,480},{32,0},{64,32},{96,64},{128,96},{160,128},{192,160},{224,1... | collective-permute-start | bytes 1572872 | tf_op jit(solution)/shard_map/ppermute | solution.py:154
  77.9 0.5 slice.49
  79.1 0.5 iota.63
  79.6 9.3 %conditional.2 = (s32[2,2048]{1,0:T(2,128)S(1)}, s32[32]{0:T(128)}, s32[32,16,32]{2,1,0:T(8,128)S(1)}) conditional(s32[]{:T(128)} %bitcast.14, () %tuple.27, (s32[64,4,128]{2,1,0:T(4,128)S(1)}, s32[]{:T(128)}, s32[64]{0:T(128)}) %tuple.28), branch_computations={%region_3.4_spmd, %region_4.7_spmd} | conditional | flops 27518976 | bytes 1869760 | solution.py:273
  79.6 1.0 reshape.495
  80.6 1.3 copy.28
  81.9 1.2 convert_reduce_fusion
  83.1 0.7 min.5
  83.8 0.8 unstack.13
  84.6 0.9 fusion.21
  85.6 1.0 fusion.48
  86.6 1.4 fusion
  88.0 0.7 select_reduce_fusion
  88.9 12.2 %shard_map.48 = bf16[2048,256]{1,0:T(8,128)(2,1)} custom-call(s32[2,2048]{1,0:T(2,128)S(1)} %get-tuple-element.72.index_ref, s32[32]{0:T(128)} %get-tuple-element.73.used_ref, bf16[256,8,128]{2,1,0:T(8,128)(2,1)} %collective-permute-done.12.refs_0_, bf16[256,8,128]{2,1,0:T(8,128)(2,1)} %collective-permute-done.11.refs_1_, bf16[256,8,128]{2,1,0:T(8,128)(2,1)} %copy-done.6, ...), custom_call_target="tpu_custom_call" | custom-call | tf_op jit(solution)/shard_map/pallas_call | solution.py:124
  101.1 13.5 %all-to-all-start.3 = ((bf16[32,64,256]{2,1,0:T(8,128)(2,1)}), bf16[32,64,256]{2,1,0:T(8,128)(2,1)S(1)}, u32[]{:S(2)}, u32[]{:S(2)}) async-start(bf16[32,64,256]{2,1,0:T(8,128)(2,1)} %bitcast.17), calls=%async_computation.3 | async-start | bytes 2097152 | tf_op jit(solution)/shard_map/all_to_all | solution.py:187
  114.6 2.0 %convert_reduce_fusion.2 = (f32[16,32,16]{2,1,0:T(8,128)S(1)}, f32[16,32]{1,0:T(8,128)S(1)}) fusion(s32[32,16,32]{2,1,0:T(8,128)S(1)} %get-tuple-element.71), kind=kLoop, calls=%fused_computation.199 | loop fusion | flops 1039872 | bytes 100352 | tf_op jit(solution)/shard_map/reduce_sum | solution.py:278
  116.8 0.5 copy-done.7
  117.4 14.1 %all-to-all-done.3 = bf16[32,64,256]{2,1,0:T(8,128)(2,1)S(1)} async-done(((bf16[32,64,256]{2,1,0:T(8,128)(2,1)}), bf16[32,64,256]{2,1,0:T(8,128)(2,1)S(1)}, u32[]{:S(2)}, u32[]{:S(2)}) %all-to-all-start.3) | async-done | bytes 1048608 | tf_op jit(solution)/shard_map/all_to_all | solution.py:187
  131.5 0.8 reduce_sum.99
  132.3 1.6 %fusion.109 = bf16[16,16,256]{2,1,0:T(8,128)(2,1)} fusion(s32[16,16]{1,0:T(8,128)S(1)} %iota_add_fusion, bf16[64,256]{1,0:T(8,128)(2,1)} %reduce_sum.99), kind=kOutput, calls=%fused_computation.244 | convolution fusion | flops 8404992 | bytes 164864 | tf_op jit(solution)/shard_map/dot_general | solution.py:297
  133.9 9.0 %all-to-all-start.4 = ((bf16[16,16,256]{2,1,0:T(8,128)(2,1)}), bf16[16,16,256]{2,1,0:T(8,128)(2,1)S(1)}, u32[]{:S(2)}, u32[]{:S(2)}) async-start(bf16[16,16,256]{2,1,0:T(8,128)(2,1)} %fusion.109), calls=%async_computation.4 | async-start | bytes 262144 | tf_op jit(solution)/shard_map/all_to_all | solution.py:298
  142.9 1.6 %reduce_max.19 = f32[]{:T(128)} reduce(f32[16,32,16]{2,1,0:T(8,128)} %copy-done.7, f32[]{:T(128)} %constant.359.clone.1), dimensions={0,1,2}, to_apply=%region_10.11 | reduce | flops 8191 | bytes 32776 | tf_op jit(solution)/shard_map/reduce_max | solution.py:281
  144.6 0.6 reduce_max.18
  146.6 8.5 %all-to-all-done.4 = bf16[16,16,256]{2,1,0:T(8,128)(2,1)S(1)} async-done(((bf16[16,16,256]{2,1,0:T(8,128)(2,1)}), bf16[16,16,256]{2,1,0:T(8,128)(2,1)S(1)}, u32[]{:S(2)}, u32[]{:S(2)}) %all-to-all-start.4) | async-done | bytes 131104 | tf_op jit(solution)/shard_map/all_to_all | solution.py:298
  155.3 0.6 copy-done.8
  (50 shorter events, 1.8 us)
Async XLA Ops:
  1.7 1.2 copy-start.2
  3.5 5.9 %copy-start.10 = (s32[256,2]{0,1:T(2,128)S(1)}, s32[256,2]{0,1:T(2,128)}, u32[]{:S(2)}) copy-start(s32[256,2]{0,1:T(2,128)} %param.9) | copy-start | bytes 6148
  3.5 5.9 %copy-start.9 = (s32[4096]{0:T(1024)S(1)}, s32[4096]{0:T(1024)}, u32[]{:S(2)}) copy-start(s32[4096]{0:T(1024)} %param.10) | copy-start | bytes 49156
  4.6 11.8 %all-to-all-start.1 = ((bf16[4,64,8,128]{3,2,1,0:T(8,128)(2,1)}), bf16[4,64,8,128]{3,2,1,0:T(8,128)(2,1)S(1)}, u32[]{:S(2)}, u32[]{:S(2)}) async-start(bf16[4,64,8,128]{3,2,1,0:T(8,128)(2,1)} %copy_bitcast_fusion.2), calls=%async_computation.1 | async-start | bytes 1048576 | tf_op jit(solution)/shard_map/all_to_all | solution.py:229
  17.0 23.1 %collective-permute-start.9 = (bf16[256,8,128]{2,1,0:T(8,128)(2,1)S(1)}, bf16[256,8,128]{2,1,0:T(8,128)(2,1)S(1)}, u32[]{:S(2)}, u32[]{:S(2)}) collective-permute-start(bf16[256,8,128]{2,1,0:T(8,128)(2,1)S(1)} %bitcast.95), channel_id=1, source_target_pairs={{0,480},{32,0},{64,32},{96,64},{128,96},{160,128},{192,160},{224,1... | collective-permute-start | bytes 1572872 | tf_op jit(solution)/shard_map/ppermute | solution.py:154
  29.5 15.1 %collective-permute-start.7 = (bf16[256,8,128]{2,1,0:T(8,128)(2,1)S(1)}, bf16[256,8,128]{2,1,0:T(8,128)(2,1)S(1)}, u32[]{:S(2)}, u32[]{:S(2)}) collective-permute-start(bf16[256,8,128]{2,1,0:T(8,128)(2,1)S(1)} %bitcast.96), channel_id=1, source_target_pairs={{0,32},{32,64},{64,96},{96,128},{128,160},{160,192},{192,224},{224... | collective-permute-start | bytes 1572872 | tf_op jit(solution)/shard_map/ppermute | solution.py:153
  31.4 23.8 %all-to-all-start.2 = ((s32[64,4,128]{2,1,0:T(4,128)}), s32[64,4,128]{2,1,0:T(4,128)S(1)}, u32[]{:S(2)}, u32[]{:S(2)}) async-start(s32[64,4,128]{2,1,0:T(4,128)} %broadcast_in_dim.50), calls=%async_computation.2 | async-start | bytes 262144 | tf_op jit(solution)/shard_map/all_to_all | solution.py:231
  40.1 48.8 %copy-start.3 = (bf16[256,8,128]{2,1,0:T(8,128)(2,1)}, bf16[256,8,128]{2,1,0:T(8,128)(2,1)S(1)}, u32[]{:S(2)}) copy-start(bf16[256,8,128]{2,1,0:T(8,128)(2,1)S(1)} %collective-permute-done.9.refs_5_) | copy-start | bytes 1572868
  40.1 17.9 %collective-permute-start.10 = (bf16[256,8,128]{2,1,0:T(8,128)(2,1)S(1)}, bf16[256,8,128]{2,1,0:T(8,128)(2,1)S(1)}, u32[]{:S(2)}, u32[]{:S(2)}) collective-permute-start(bf16[256,8,128]{2,1,0:T(8,128)(2,1)S(1)} %collective-permute-done.9.refs_5_), channel_id=1, source_target_pairs={{0,480},{32,0},{64,32},{96,64},{128,96},{160,128},{192,160},{224,1... | collective-permute-start | bytes 1572872 | tf_op jit(solution)/shard_map/ppermute | solution.py:154
  44.6 14.1 %collective-permute-start.8 = (bf16[256,8,128]{2,1,0:T(8,128)(2,1)S(1)}, bf16[256,8,128]{2,1,0:T(8,128)(2,1)S(1)}, u32[]{:S(2)}, u32[]{:S(2)}) collective-permute-start(bf16[256,8,128]{2,1,0:T(8,128)(2,1)S(1)} %collective-permute-done.7.refs_3_), channel_id=1, source_target_pairs={{0,32},{32,64},{64,96},{96,128},{128,160},{160,192},{192,224},{224... | collective-permute-start | bytes 1572872 | tf_op jit(solution)/shard_map/ppermute | solution.py:153
  58.7 20.9 %copy-start.6 = (bf16[256,8,128]{2,1,0:T(8,128)(2,1)}, bf16[256,8,128]{2,1,0:T(8,128)(2,1)S(1)}, u32[]{:S(2)}) copy-start(bf16[256,8,128]{2,1,0:T(8,128)(2,1)S(1)} %collective-permute-done.8.refs_2_) | copy-start | bytes 1572868
  58.7 11.2 %collective-permute-start.11 = (bf16[256,8,128]{2,1,0:T(8,128)(2,1)S(1)}, bf16[256,8,128]{2,1,0:T(8,128)(2,1)}, u32[]{:S(2)}, u32[]{:S(2)}) collective-permute-start(bf16[256,8,128]{2,1,0:T(8,128)(2,1)S(1)} %collective-permute-done.8.refs_2_), channel_id=1, source_target_pairs={{0,32},{32,64},{64,96},{96,128},{128,160},{160,192},{192,224},{224... | collective-permute-start | bytes 1572872 | tf_op jit(solution)/shard_map/ppermute | solution.py:153
  61.8 13.1 %collective-permute-start.13 = (bf16[256,8,128]{2,1,0:T(8,128)(2,1)S(1)}, bf16[256,8,128]{2,1,0:T(8,128)(2,1)}, u32[]{:S(2)}, u32[]{:S(2)}) collective-permute-start(bf16[256,8,128]{2,1,0:T(8,128)(2,1)S(1)} %collective-permute-done.10.refs_6_), channel_id=1, source_target_pairs={{0,480},{32,0},{64,32},{96,64},{128,96},{160,128},{192,160},{224,1... | collective-permute-start | bytes 1572872 | tf_op jit(solution)/shard_map/ppermute | solution.py:154
  69.9 19.0 %collective-permute-start.12 = (bf16[256,8,128]{2,1,0:T(8,128)(2,1)}, bf16[256,8,128]{2,1,0:T(8,128)(2,1)}, u32[]{:S(2)}, u32[]{:S(2)}) collective-permute-start(bf16[256,8,128]{2,1,0:T(8,128)(2,1)} %collective-permute-done.11.refs_1_), channel_id=1, source_target_pairs={{0,32},{32,64},{64,96},{96,128},{128,160},{160,192},{192,224},{224... | collective-permute-start | bytes 1572872 | tf_op jit(solution)/shard_map/ppermute | solution.py:153
  74.8 14.1 %collective-permute-start.14 = (bf16[256,8,128]{2,1,0:T(8,128)(2,1)}, bf16[256,8,128]{2,1,0:T(8,128)(2,1)}, u32[]{:S(2)}, u32[]{:S(2)}) collective-permute-start(bf16[256,8,128]{2,1,0:T(8,128)(2,1)} %collective-permute-done.13.refs_7_), channel_id=1, source_target_pairs={{0,480},{32,0},{64,32},{96,64},{128,96},{160,128},{192,160},{224,1... | collective-permute-start | bytes 1572872 | tf_op jit(solution)/shard_map/ppermute | solution.py:154
  86.6 1.4 copy-start.11
  101.1 30.4 %all-to-all-start.3 = ((bf16[32,64,256]{2,1,0:T(8,128)(2,1)}), bf16[32,64,256]{2,1,0:T(8,128)(2,1)S(1)}, u32[]{:S(2)}, u32[]{:S(2)}) async-start(bf16[32,64,256]{2,1,0:T(8,128)(2,1)} %bitcast.17), calls=%async_computation.3 | async-start | bytes 2097152 | tf_op jit(solution)/shard_map/all_to_all | solution.py:187
  116.6 0.7 copy-start.7
  133.9 21.2 %all-to-all-start.4 = ((bf16[16,16,256]{2,1,0:T(8,128)(2,1)}), bf16[16,16,256]{2,1,0:T(8,128)(2,1)S(1)}, u32[]{:S(2)}, u32[]{:S(2)}) async-start(bf16[16,16,256]{2,1,0:T(8,128)(2,1)} %fusion.109), calls=%async_computation.4 | async-start | bytes 262144 | tf_op jit(solution)/shard_map/all_to_all | solution.py:298
  155.3 0.6 copy-start.8

commit v4 on v3

--- a/solution.py
+++ b/solution.py
@@ -141,20 +141,81 @@
     return up, down
 
 
-def near_ring(block, axis, reach, codes, basis):
+def near_ring(block, axis, reach, codes, basis, place):
     up, down = shifts(lax.axis_size(axis))
     below, above = [], []
     from_below = from_above = block
+    placed = None
     for step in range(reach):
-        if step == 2:
+        if step == reach - 2:
             from_below, from_above, codes, basis = lax.optimization_barrier(
                 (from_below, from_above, codes, basis)
+            )
+        if step == reach - 1:
+            from_below, from_above, placed = lax.optimization_barrier(
+                (from_below, from_above, place(codes))
             )
         from_below = lax.ppermute(from_below, axis, up)
         from_above = lax.ppermute(from_above, axis, down)
         below.append(from_below)
         above.append(from_above)
-    return below[::-1] + [block] + above, codes, basis
+    return below[::-1] + [block] + above, codes, basis, placed
+
+
+def place_pairs(codes, zs, xs, days, own, plane_rows, z):
+    columns = xs * days
+    reach = zs // 4
+    codes = codes.reshape(zs, xs, 2, days, own).transpose(2, 1, 3, 0, 4)
+    first, second = codes.reshape(2, columns, zs * own)
+    valid = (first >= 0) & (second >= 0)
+    first_plane, second_plane = first // plane_rows, second // plane_rows
+    apart = jnp.mod(second_plane - first_plane, zs)
+    middle = jnp.where(
+        apart <= zs // 2,
+        first_plane + apart // 2,
+        second_plane + (zs - apart) // 2,
+    )
+    middle = jnp.where(valid, jnp.mod(middle, zs), -1)
+    loose = jnp.minimum(apart, zs - apart) <= 2 * reach - 2
+
+    planes = jnp.arange(zs, dtype=jnp.int32)
+    at = middle[None] == planes[:, None, None]
+    load = jnp.sum(at.astype(jnp.float32), axis=2)
+    total = jnp.sum(load, axis=0, keepdims=True)
+    upto = (planes[None, :] <= planes[:, None]).astype(jnp.float32)
+    excess = jnp.sum(upto[:, :, None] * (load * zs - total)[None], axis=1)
+    centre = (jnp.max(excess, axis=0) + jnp.min(excess, axis=0)) * 0.5
+    flow = jnp.floor((excess - centre) / zs + 0.5)
+    rising = jnp.maximum(flow, 0.0)[:, :, None]
+    falling = jnp.maximum(-jnp.roll(flow, 1, axis=0), 0.0)[:, :, None]
+
+    movable = (at & loose[None]).astype(jnp.bfloat16)
+    order = jnp.arange(zs * own, dtype=jnp.int32)
+    earlier = (order[:, None] < order[None, :]).astype(jnp.bfloat16)
+    rank = jnp.dot(
+        movable.reshape(zs * columns, zs * own), earlier, preferred_element_type=jnp.float32
+    ).reshape(zs, columns, zs * own)
+    step = jnp.where(rank < rising, 1.0, jnp.where(rank < rising + falling, -1.0, 0.0))
+    shift = jnp.sum(movable.astype(jnp.float32) * step, axis=0).astype(jnp.int32)
+    middle = jnp.where(valid, jnp.mod(middle + shift, zs), -1)
+
+    first_at = jnp.mod(first_plane - z + reach, zs) * plane_rows + jnp.mod(first, plane_rows)
+    second_at = jnp.mod(second_plane - z + reach, zs) * plane_rows + jnp.mod(second, plane_rows)
+    return middle, first_at * 4096 + second_at
+
+
+def fill_slots(middle, packed, slots, z):
+    here = middle == z
+    order = jnp.arange(middle.shape[1], dtype=jnp.int32)
+    earlier = (order[:, None] < order[None, :]).astype(jnp.bfloat16)
+    rank = jnp.dot(here.astype(jnp.bfloat16), earlier, preferred_element_type=jnp.float32)
+    rank = jnp.where(here, rank.astype(jnp.int32), -1)
+    slot_ids = jnp.arange(slots, dtype=jnp.int32)
+    taken = rank[:, None, :] == slot_ids[None, :, None]
+    chosen = jnp.sum(jnp.where(taken, packed[:, None, :], 0), axis=2).reshape(-1)
+    index = jnp.stack([chosen // 4096, chosen % 4096])
+    used = jnp.minimum(jnp.sum(here.astype(jnp.int32), axis=1), slots)
+    return index, used
 
 
 def far_ring(near, axis, reach):
@@ -230,47 +291,30 @@
     block, code = lax.optimization_barrier((block, code))
     codes = lax.all_to_all(code, ("z", "x"), 0, 0, tiled=True)
     basis = basis_slice(x * share, share, freqs)
-    near, codes, basis = near_ring(block, "z", reach, codes, basis)
-
     planes = jnp.arange(zs, dtype=jnp.int32)
-    slots, returned = 2 * own, own // 2
+    slots, returned = own + own // 4, own // 2
     slot_ids = jnp.arange(slots, dtype=jnp.int32)
 
-    def bookkeeping(codes):
-        codes = codes.reshape(zs, xs, 2, days, own).transpose(2, 1, 3, 0, 4)
-        first, second = codes.reshape(2, columns, zs * own)
-        valid = (first >= 0) & (second >= 0)
-        first_plane, second_plane = first // plane_rows, second // plane_rows
-        apart = jnp.mod(second_plane - first_plane, zs)
-        middle = jnp.where(
-            apart <= zs // 2,
-            first_plane + apart // 2,
-            second_plane + (zs - apart) // 2,
-        )
-        middle = jnp.where(valid, jnp.mod(middle, zs), -1)
-
-        here = middle == z
-        order = jnp.arange(zs * own, dtype=jnp.int32)
-        earlier = (order[:, None] < order[None, :]).astype(jnp.bfloat16)
-        rank = jnp.dot(here.astype(jnp.bfloat16), earlier, preferred_element_type=jnp.float32)
-        rank = jnp.where(here, rank.astype(jnp.int32), -1)
-        first_at = jnp.mod(first_plane - z + reach, zs) * plane_rows + first % plane_rows
-        second_at = jnp.mod(second_plane - z + reach, zs) * plane_rows + second % plane_rows
-        packed = first_at * 4096 + second_at
-        taken = rank[:, None, :] == slot_ids[None, :, None]
-        chosen = jnp.sum(jnp.where(taken, packed[:, None, :], 0), axis=2).reshape(-1)
-        index = jnp.stack([chosen // 4096, chosen % 4096])
-        used = jnp.minimum(jnp.sum(here.astype(jnp.int32), axis=1), slots)
-        return index, used, middle
-
-    def nothing(codes):
-        return (
-            jnp.zeros((2, columns * slots), jnp.int32),
-            jnp.zeros((columns,), jnp.int32),
-            jnp.full((columns, zs * own), -1, jnp.int32),
-        )
-
-    index, used, middle = lax.cond(codes[0, 0, 0] >= -1, bookkeeping, nothing, codes)
+    def place(codes):
+        def first_branch(codes):
+            return place_pairs(codes, zs, xs, days, own, plane_rows, z)
+
+        def second_branch(codes):
+            none = jnp.full((columns, zs * own), -1, jnp.int32)
+            return none, none
+
+        return lax.cond(codes[0, 0, 0] >= -1, first_branch, second_branch, codes)
+
+    near, codes, basis, placed = near_ring(block, "z", reach, codes, basis, place)
+    middle, packed = placed
+
+    def first_branch(middle, packed):
+        return fill_slots(middle, packed, slots, z)
+
+    def second_branch(middle, packed):
+        return jnp.zeros((2, columns * slots), jnp.int32), jnp.zeros((columns,), jnp.int32)
+
+    index, used = lax.cond(codes[0, 0, 0] >= -1, first_branch, second_branch, middle, packed)
     partial = correlate(index, used, near, basis)
     added = exchange_and_add(partial, columns)
 

time: 158 us -> 151 us (0.956)
  waiting for transfers between devices: 42.3 us -> 45.2 us
  local copies, waits for them, and re-layouts: 7.97 us -> 5.35 us
  starting transfers between devices: 71.2 us -> 68.6 us
  Pallas kernels: 12.2 us -> 10.4 us
    ppermute x4, waiting for transfers between devices: 2.83 us -> 10.4 us  [near_ring(): from_above = lax.ppermute(from_above, axis, down)]
    all_to_all x1, waiting for transfers between devices: 14.1 us -> 10.7 us  [exchange_and_add(): shares = lax.all_to_all(columns, ('x', 'y', 'c'), 0, 0, tiled=True)]
    ppermute x4, waiting for transfers between devices: 5.32 us -> 2.58 us  [near_ring(): from_below = lax.ppermute(from_below, axis, up)]
    all_to_all x1, starting transfers between devices: 13.5 us -> 11.1 us  [exchange_and_add(): shares = lax.all_to_all(columns, ('x', 'y', 'c'), 0, 0, tiled=True)]
    pallas_call x1, Pallas kernels: 12.2 us -> 10.4 us  [correlate(): pl.pallas_call(functools.partial(correlate_kernel, count), out_shape=jax....]
    reduce_sum x2 -> x5, other arithmetic: 1.85 us -> 3.21 us  [the longest x1 1.47 us: fill_slots(): jnp.sum(jnp.where(taken, packed[:, None, :], 0), axis=2).reshape(-1)]
  transfers between devices with their start and end apart: 12 -> 12, of which waited for: 7 -> 10; matrix products, arithmetic and copies ran while one was open for 12% -> 11% of each run, Pallas kernels for 0% -> 0%
where the time goes in v4:
time: 151 us; the launch traced here: 150 us
  starting transfers between devices  68.6 us (45%)
  waiting for transfers between devices  45.2 us (30%)
  other arithmetic  14.2 us (9%)
  Pallas kernels  10.4 us (7%)
  local copies, waits for them, and re-layouts  5.35 us (4%)
  matrix products  3.92 us (3%)
  between operations  2.37 us (2%)
    ppermute x4, starting transfers between devices, near_ring(): from_above = lax.ppermute(from_above, axis, down)  22.2 us
    ppermute x4, starting transfers between devices, near_ring(): from_below = lax.ppermute(from_below, axis, up)  12.1 us
    all_to_all x1, starting transfers between devices, exchange_and_add(): shares = lax.all_to_all(columns, ('x', 'y', 'c'), 0, 0, tiled=True)  11.1 us
    all_to_all x1, waiting for transfers between devices, exchange_and_add(): shares = lax.all_to_all(columns, ('x', 'y', 'c'), 0, 0, tiled=True)  10.7 us
    ppermute x4, waiting for transfers between devices, near_ring(): from_above = lax.ppermute(from_above, axis, down)  10.4 us
    pallas_call x1, Pallas kernels, correlate(): pl.pallas_call(functools.partial(correlate_kernel, count), out_shape=jax....  10.4 us
    all_to_all x1, waiting for transfers between devices, body(): lax.all_to_all(leaving.reshape(zs, returned, LAGS), 'z', 0, 0, tiled=True)  9.97 us
    all_to_all x1, starting transfers between devices, body(): lax.all_to_all(leaving.reshape(zs, returned, LAGS), 'z', 0, 0, tiled=True)  9.8 us
  transfers between devices with their start and end apart: 12, of which 10 were waited for; matrix products, arithmetic and copies ran while one was open for 11% of the time, Pallas kernels for 0%

profile of v4, /device:TPU:1, one launch (start us, length us, event | category | flops | bytes accessed | tf_op | source)
XLA Modules:
  0.0 150.3 jit_solution(6757918888203913132)
XLA Ops:
  0.0 1.4 add_sqrt_fusion
  1.7 0.8 fusion.52
  2.5 0.4 copy-done.2
  3.5 1.1 copy_bitcast_fusion.2
  4.6 4.8 %all-to-all-start.1 = ((bf16[4,64,8,128]{3,2,1,0:T(8,128)(2,1)}), bf16[4,64,8,128]{3,2,1,0:T(8,128)(2,1)S(1)}, u32[]{:S(2)}, u32[]{:S(2)}) async-start(bf16[4,64,8,128]{3,2,1,0:T(8,128)(2,1)} %copy_bitcast_fusion.2), calls=%async_computation.1 | async-start | bytes 1048576 | tf_op jit(solution)/shard_map/all_to_all | solution.py:290
  9.9 1.0 fusion.55
  10.9 5.4 %all-to-all-done.1 = bf16[4,64,8,128]{3,2,1,0:T(8,128)(2,1)S(1)} async-done(((bf16[4,64,8,128]{3,2,1,0:T(8,128)(2,1)}), bf16[4,64,8,128]{3,2,1,0:T(8,128)(2,1)S(1)}, u32[]{:S(2)}, u32[]{:S(2)}) %all-to-all-start.1) | async-done | bytes 524320 | tf_op jit(solution)/shard_map/all_to_all | solution.py:290
  16.3 0.7 broadcast_in_dim.74
  17.0 12.4 %collective-permute-start.9 = (bf16[256,8,128]{2,1,0:T(8,128)(2,1)S(1)}, bf16[256,8,128]{2,1,0:T(8,128)(2,1)S(1)}, u32[]{:S(2)}, u32[]{:S(2)}) collective-permute-start(bf16[256,8,128]{2,1,0:T(8,128)(2,1)S(1)} %bitcast.58), channel_id=1, source_target_pairs={{0,480},{32,0},{64,32},{96,64},{128,96},{160,128},{192,160},{224,1... | collective-permute-start | bytes 1572872 | tf_op jit(solution)/shard_map/ppermute | solution.py:159
  29.5 1.9 %collective-permute-start.7 = (bf16[256,8,128]{2,1,0:T(8,128)(2,1)S(1)}, bf16[256,8,128]{2,1,0:T(8,128)(2,1)S(1)}, u32[]{:S(2)}, u32[]{:S(2)}) collective-permute-start(bf16[256,8,128]{2,1,0:T(8,128)(2,1)S(1)} %bitcast.59), channel_id=1, source_target_pairs={{0,32},{32,64},{64,96},{96,128},{128,160},{160,192},{192,224},{224... | collective-permute-start | bytes 1572872 | tf_op jit(solution)/shard_map/ppermute | solution.py:158
  31.4 8.7 %all-to-all-start.2 = ((s32[64,4,128]{2,1,0:T(4,128)}), s32[64,4,128]{2,1,0:T(4,128)S(1)}, u32[]{:S(2)}, u32[]{:S(2)}) async-start(s32[64,4,128]{2,1,0:T(4,128)} %broadcast_in_dim.74), calls=%async_computation.2 | async-start | bytes 262144 | tf_op jit(solution)/shard_map/all_to_all | solution.py:292
  40.1 4.4 %collective-permute-start.10 = (bf16[256,8,128]{2,1,0:T(8,128)(2,1)S(1)}, bf16[256,8,128]{2,1,0:T(8,128)(2,1)S(1)}, u32[]{:S(2)}, u32[]{:S(2)}) collective-permute-start(bf16[256,8,128]{2,1,0:T(8,128)(2,1)S(1)} %collective-permute-done.9.refs_5_), channel_id=1, source_target_pairs={{0,480},{32,0},{64,32},{96,64},{128,96},{160,128},{192,160},{224,1... | collective-permute-start | bytes 1572872 | tf_op jit(solution)/shard_map/ppermute | solution.py:159
  44.5 1.9 %collective-permute-start.8 = (bf16[256,8,128]{2,1,0:T(8,128)(2,1)S(1)}, bf16[256,8,128]{2,1,0:T(8,128)(2,1)}, u32[]{:S(2)}, u32[]{:S(2)}) collective-permute-start(bf16[256,8,128]{2,1,0:T(8,128)(2,1)S(1)} %collective-permute-done.7.refs_3_), channel_id=1, source_target_pairs={{0,32},{32,64},{64,96},{96,128},{128,160},{160,192},{192,224},{224... | collective-permute-start | bytes 1572872 | tf_op jit(solution)/shard_map/ppermute | solution.py:158
  46.5 2.5 %multiply_convert_fusion.1 = (bf16[512,256]{1,0:T(8,128)(2,1)S(1)}, bf16[512,256]{1,0:T(8,128)(2,1)S(1)}) fusion(s32[256]{0:T(256)S(1)} %iota_add_fusion.2, s32[512]{0:T(512)S(1)} %iota_add_fusion.1), kind=kLoop, calls=%fused_computation.156 | loop fusion | flops 2490368 | bytes 527360 | tf_op jit(solution)/shard_map/convert.2
  49.1 6.2 %all-to-all-done.2 = s32[64,4,128]{2,1,0:T(4,128)S(1)} async-done(((s32[64,4,128]{2,1,0:T(4,128)}), s32[64,4,128]{2,1,0:T(4,128)S(1)}, u32[]{:S(2)}, u32[]{:S(2)}) %all-to-all-start.2) | async-done | bytes 131104 | tf_op jit(solution)/shard_map/all_to_all | solution.py:292
  55.2 2.9 %collective-permute-done.10.refs_6_ = bf16[256,8,128]{2,1,0:T(8,128)(2,1)S(1)} collective-permute-done((bf16[256,8,128]{2,1,0:T(8,128)(2,1)S(1)}, bf16[256,8,128]{2,1,0:T(8,128)(2,1)S(1)}, u32[]{:S(2)}, u32[]{:S(2)}) %collective-permute-start.10) | collective-permute-done | bytes 524320 | tf_op jit(solution)/shard_map/ppermute | solution.py:159
  58.2 0.6 collective-permute-done.8.refs_2_
  58.7 3.1 %collective-permute-start.11 = (bf16[256,8,128]{2,1,0:T(8,128)(2,1)}, bf16[256,8,128]{2,1,0:T(8,128)(2,1)}, u32[]{:S(2)}, u32[]{:S(2)}) collective-permute-start(bf16[256,8,128]{2,1,0:T(8,128)(2,1)} %collective-permute-done.8.refs_2_), channel_id=1, source_target_pairs={{0,32},{32,64},{64,96},{96,128},{128,160},{160,192},{192,224},{224... | collective-permute-start | bytes 1572872 | tf_op jit(solution)/shard_map/ppermute | solution.py:158
  61.9 3.4 %collective-permute-start.12 = (bf16[256,8,128]{2,1,0:T(8,128)(2,1)S(1)}, bf16[256,8,128]{2,1,0:T(8,128)(2,1)}, u32[]{:S(2)}, u32[]{:S(2)}) collective-permute-start(bf16[256,8,128]{2,1,0:T(8,128)(2,1)S(1)} %collective-permute-done.10.refs_6_), channel_id=1, source_target_pairs={{0,480},{32,0},{64,32},{96,64},{128,96},{160,128},{192,160},{224,1... | collective-permute-start | bytes 1572872 | tf_op jit(solution)/shard_map/ppermute | solution.py:159
  65.2 0.5 slice.58
  66.4 2.9 %conditional.3 = (s32[32,512]{1,0:T(8,128)S(1)}, s32[32,512]{1,0:T(8,128)S(1)}) conditional(s32[]{:T(128)} %bitcast.13, () %tuple.34, (s32[64,4,128]{2,1,0:T(4,128)S(1)}, s32[]{:T(128)}) %tuple.35), branch_computations={%region_3.4_spmd, %region_4.11_spmd} | conditional | flops 279927264 | bytes 2145556 | solution.py:306
  66.6 0.3 copy.28
  67.4 0.3 fusion.23
  68.2 0.6 fusion.10
  68.8 0.4 multiply_reduce_fusion
  69.3 0.9 collective-permute-done.11.refs_1_
  70.2 3.6 %collective-permute-done.12.refs_7_ = bf16[256,8,128]{2,1,0:T(8,128)(2,1)} collective-permute-done((bf16[256,8,128]{2,1,0:T(8,128)(2,1)S(1)}, bf16[256,8,128]{2,1,0:T(8,128)(2,1)}, u32[]{:S(2)}, u32[]{:S(2)}) %collective-permute-start.12) | collective-permute-done | bytes 524320 | tf_op jit(solution)/shard_map/ppermute | solution.py:159
  73.8 5.1 %collective-permute-start.13 = (bf16[256,8,128]{2,1,0:T(8,128)(2,1)}, bf16[256,8,128]{2,1,0:T(8,128)(2,1)S(1)}, u32[]{:S(2)}, u32[]{:S(2)}) collective-permute-start(bf16[256,8,128]{2,1,0:T(8,128)(2,1)} %collective-permute-done.11.refs_1_), channel_id=1, source_target_pairs={{0,32},{32,64},{64,96},{96,128},{128,160},{160,192},{192,224},{224... | collective-permute-start | bytes 1572872 | tf_op jit(solution)/shard_map/ppermute | solution.py:158
  79.0 1.9 %collective-permute-start.14 = (bf16[256,8,128]{2,1,0:T(8,128)(2,1)}, bf16[256,8,128]{2,1,0:T(8,128)(2,1)}, u32[]{:S(2)}, u32[]{:S(2)}) collective-permute-start(bf16[256,8,128]{2,1,0:T(8,128)(2,1)} %collective-permute-done.12.refs_7_), channel_id=1, source_target_pairs={{0,480},{32,0},{64,32},{96,64},{128,96},{160,128},{192,160},{224,1... | collective-permute-start | bytes 1572872 | tf_op jit(solution)/shard_map/ppermute | solution.py:159
  80.9 1.0 eq.167
  81.9 4.6 %conditional.4 = (s32[2,1280]{1,0:T(2,128)S(1)}, s32[32]{0:T(128)}) conditional(s32[]{:T(128)} %bitcast.13, () %tuple.37, (s32[]{:T(128)}, s32[32,512]{1,0:T(8,128)}, s32[32,512]{1,0:T(8,128)}) %tuple.72), branch_computations={%region_17.18_spmd, %region_18.21_spmd} | conditional | flops 19114240 | bytes 356756 | solution.py:317
  81.9 1.0 convert_reduce_fusion
  82.9 0.5 broadcast_minimum_fusion
  83.6 1.5 select_reduce_fusion
  85.1 0.7 reshape.607
  85.8 0.7 and_select_fusion.1
  86.5 1.1 collective-permute-done.13.refs_0_
  87.7 3.8 %collective-permute-done.14.refs_8_ = bf16[256,8,128]{2,1,0:T(8,128)(2,1)} collective-permute-done((bf16[256,8,128]{2,1,0:T(8,128)(2,1)}, bf16[256,8,128]{2,1,0:T(8,128)(2,1)}, u32[]{:S(2)}, u32[]{:S(2)}) %collective-permute-start.14) | collective-permute-done | bytes 524320 | tf_op jit(solution)/shard_map/ppermute | solution.py:159
  91.5 10.4 %shard_map.48 = bf16[1280,256]{1,0:T(8,128)(2,1)} custom-call(s32[2,1280]{1,0:T(2,128)} %copy-done.9, s32[32]{0:T(128)} %get-tuple-element.88.used_ref, bf16[256,8,128]{2,1,0:T(8,128)(2,1)S(1)} %collective-permute-done.13.refs_0_, bf16[256,8,128]{2,1,0:T(8,128)(2,1)} %collective-permute-done.11.refs_1_, bf16[256,8,128]{2,1,0:T(8,128)(2,1)} %collective-permute-done.8.refs_2_, ...), custom_call_target="tpu_custom_call" | custom-call | tf_op jit(solution)/shard_map/pallas_call | solution.py:124
  101.9 11.1 %all-to-all-start.3 = ((bf16[32,40,256]{2,1,0:T(8,128)(2,1)}), bf16[32,40,256]{2,1,0:T(8,128)(2,1)S(1)}, u32[]{:S(2)}, u32[]{:S(2)}) async-start(bf16[32,40,256]{2,1,0:T(8,128)(2,1)} %bitcast.16), calls=%async_computation.3 | async-start | bytes 1310720 | tf_op jit(solution)/shard_map/all_to_all | solution.py:248
  112.9 2.0 %convert_reduce_fusion.4 = (f32[16,32,16]{2,1,0:T(8,128)S(1)}, f32[16,32]{1,0:T(8,128)S(1)}) fusion(s32[32,16,32]{2,1,0:T(8,128)S(1)} %eq.167), kind=kLoop, calls=%fused_computation.126 | loop fusion | flops 1039872 | bytes 100352 | tf_op jit(solution)/shard_map/reduce_sum | solution.py:322
  115.1 10.7 %all-to-all-done.3 = bf16[32,40,256]{2,1,0:T(8,128)(2,1)S(1)} async-done(((bf16[32,40,256]{2,1,0:T(8,128)(2,1)}), bf16[32,40,256]{2,1,0:T(8,128)(2,1)S(1)}, u32[]{:S(2)}, u32[]{:S(2)}) %all-to-all-start.3) | async-done | bytes 655392 | tf_op jit(solution)/shard_map/all_to_all | solution.py:248
  126.0 0.9 fusion.68
  126.8 9.8 %all-to-all-start.4 = ((bf16[16,16,256]{2,1,0:T(8,128)(2,1)}), bf16[16,16,256]{2,1,0:T(8,128)(2,1)S(1)}, u32[]{:S(2)}, u32[]{:S(2)}) async-start(bf16[16,16,256]{2,1,0:T(8,128)(2,1)} %fusion.68), calls=%async_computation.4 | async-start | bytes 262144 | tf_op jit(solution)/shard_map/all_to_all | solution.py:342
  136.7 0.7 reduce_max.28
  137.3 0.6 reduce_max.27
  139.5 10.0 %all-to-all-done.4 = bf16[16,16,256]{2,1,0:T(8,128)(2,1)S(1)} async-done(((bf16[16,16,256]{2,1,0:T(8,128)(2,1)}), bf16[16,16,256]{2,1,0:T(8,128)(2,1)S(1)}, u32[]{:S(2)}, u32[]{:S(2)}) %all-to-all-start.4) | async-done | bytes 131104 | tf_op jit(solution)/shard_map/all_to_all | solution.py:342
  149.7 0.6 copy-done.10
  (65 shorter events, 3.5 us)
Async XLA Ops:
  1.7 1.2 copy-start.2
  3.5 5.9 %copy-start.12 = (s32[256,2]{0,1:T(2,128)S(1)}, s32[256,2]{0,1:T(2,128)}, u32[]{:S(2)}) copy-start(s32[256,2]{0,1:T(2,128)} %param.11) | copy-start | bytes 6148
  3.5 5.9 %copy-start.11 = (s32[4096]{0:T(1024)S(1)}, s32[4096]{0:T(1024)}, u32[]{:S(2)}) copy-start(s32[4096]{0:T(1024)} %param.12) | copy-start | bytes 49156
  4.6 11.8 %all-to-all-start.1 = ((bf16[4,64,8,128]{3,2,1,0:T(8,128)(2,1)}), bf16[4,64,8,128]{3,2,1,0:T(8,128)(2,1)S(1)}, u32[]{:S(2)}, u32[]{:S(2)}) async-start(bf16[4,64,8,128]{3,2,1,0:T(8,128)(2,1)} %copy_bitcast_fusion.2), calls=%async_computation.1 | async-start | bytes 1048576 | tf_op jit(solution)/shard_map/all_to_all | solution.py:290
  17.0 23.1 %collective-permute-start.9 = (bf16[256,8,128]{2,1,0:T(8,128)(2,1)S(1)}, bf16[256,8,128]{2,1,0:T(8,128)(2,1)S(1)}, u32[]{:S(2)}, u32[]{:S(2)}) collective-permute-start(bf16[256,8,128]{2,1,0:T(8,128)(2,1)S(1)} %bitcast.58), channel_id=1, source_target_pairs={{0,480},{32,0},{64,32},{96,64},{128,96},{160,128},{192,160},{224,1... | collective-permute-start | bytes 1572872 | tf_op jit(solution)/shard_map/ppermute | solution.py:159
  29.5 15.1 %collective-permute-start.7 = (bf16[256,8,128]{2,1,0:T(8,128)(2,1)S(1)}, bf16[256,8,128]{2,1,0:T(8,128)(2,1)S(1)}, u32[]{:S(2)}, u32[]{:S(2)}) collective-permute-start(bf16[256,8,128]{2,1,0:T(8,128)(2,1)S(1)} %bitcast.59), channel_id=1, source_target_pairs={{0,32},{32,64},{64,96},{96,128},{128,160},{160,192},{192,224},{224... | collective-permute-start | bytes 1572872 | tf_op jit(solution)/shard_map/ppermute | solution.py:158
  31.4 23.8 %all-to-all-start.2 = ((s32[64,4,128]{2,1,0:T(4,128)}), s32[64,4,128]{2,1,0:T(4,128)S(1)}, u32[]{:S(2)}, u32[]{:S(2)}) async-start(s32[64,4,128]{2,1,0:T(4,128)} %broadcast_in_dim.74), calls=%async_computation.2 | async-start | bytes 262144 | tf_op jit(solution)/shard_map/all_to_all | solution.py:292
  40.1 51.4 %copy-start.3 = (bf16[256,8,128]{2,1,0:T(8,128)(2,1)}, bf16[256,8,128]{2,1,0:T(8,128)(2,1)S(1)}, u32[]{:S(2)}) copy-start(bf16[256,8,128]{2,1,0:T(8,128)(2,1)S(1)} %collective-permute-done.9.refs_5_) | copy-start | bytes 1572868
  40.1 18.0 %collective-permute-start.10 = (bf16[256,8,128]{2,1,0:T(8,128)(2,1)S(1)}, bf16[256,8,128]{2,1,0:T(8,128)(2,1)S(1)}, u32[]{:S(2)}, u32[]{:S(2)}) collective-permute-start(bf16[256,8,128]{2,1,0:T(8,128)(2,1)S(1)} %collective-permute-done.9.refs_5_), channel_id=1, source_target_pairs={{0,480},{32,0},{64,32},{96,64},{128,96},{160,128},{192,160},{224,1... | collective-permute-start | bytes 1572872 | tf_op jit(solution)/shard_map/ppermute | solution.py:159
  44.5 14.2 %collective-permute-start.8 = (bf16[256,8,128]{2,1,0:T(8,128)(2,1)S(1)}, bf16[256,8,128]{2,1,0:T(8,128)(2,1)}, u32[]{:S(2)}, u32[]{:S(2)}) collective-permute-start(bf16[256,8,128]{2,1,0:T(8,128)(2,1)S(1)} %collective-permute-done.7.refs_3_), channel_id=1, source_target_pairs={{0,32},{32,64},{64,96},{96,128},{128,160},{160,192},{192,224},{224... | collective-permute-start | bytes 1572872 | tf_op jit(solution)/shard_map/ppermute | solution.py:158
  58.7 11.4 %collective-permute-start.11 = (bf16[256,8,128]{2,1,0:T(8,128)(2,1)}, bf16[256,8,128]{2,1,0:T(8,128)(2,1)}, u32[]{:S(2)}, u32[]{:S(2)}) collective-permute-start(bf16[256,8,128]{2,1,0:T(8,128)(2,1)} %collective-permute-done.8.refs_2_), channel_id=1, source_target_pairs={{0,32},{32,64},{64,96},{96,128},{128,160},{160,192},{192,224},{224... | collective-permute-start | bytes 1572872 | tf_op jit(solution)/shard_map/ppermute | solution.py:158
  61.9 12.0 %collective-permute-start.12 = (bf16[256,8,128]{2,1,0:T(8,128)(2,1)S(1)}, bf16[256,8,128]{2,1,0:T(8,128)(2,1)}, u32[]{:S(2)}, u32[]{:S(2)}) collective-permute-start(bf16[256,8,128]{2,1,0:T(8,128)(2,1)S(1)} %collective-permute-done.10.refs_6_), channel_id=1, source_target_pairs={{0,480},{32,0},{64,32},{96,64},{128,96},{160,128},{192,160},{224,1... | collective-permute-start | bytes 1572872 | tf_op jit(solution)/shard_map/ppermute | solution.py:159
  69.3 11.6 %copy-start.7 = (s32[32,512]{1,0:T(8,128)}, s32[32,512]{1,0:T(8,128)S(1)}, u32[]{:S(2)}) copy-start(s32[32,512]{1,0:T(8,128)S(1)} %get-tuple-element.85) | copy-start | bytes 196612
  69.3 11.6 %copy-start.8 = (s32[32,512]{1,0:T(8,128)}, s32[32,512]{1,0:T(8,128)S(1)}, u32[]{:S(2)}) copy-start(s32[32,512]{1,0:T(8,128)S(1)} %get-tuple-element.86) | copy-start | bytes 196612
  73.8 13.8 %collective-permute-start.13 = (bf16[256,8,128]{2,1,0:T(8,128)(2,1)}, bf16[256,8,128]{2,1,0:T(8,128)(2,1)S(1)}, u32[]{:S(2)}, u32[]{:S(2)}) collective-permute-start(bf16[256,8,128]{2,1,0:T(8,128)(2,1)} %collective-permute-done.11.refs_1_), channel_id=1, source_target_pairs={{0,32},{32,64},{64,96},{96,128},{128,160},{160,192},{192,224},{224... | collective-permute-start | bytes 1572872 | tf_op jit(solution)/shard_map/ppermute | solution.py:158
  79.0 12.5 %collective-permute-start.14 = (bf16[256,8,128]{2,1,0:T(8,128)(2,1)}, bf16[256,8,128]{2,1,0:T(8,128)(2,1)}, u32[]{:S(2)}, u32[]{:S(2)}) collective-permute-start(bf16[256,8,128]{2,1,0:T(8,128)(2,1)} %collective-permute-done.12.refs_7_), channel_id=1, source_target_pairs={{0,480},{32,0},{64,32},{96,64},{128,96},{160,128},{192,160},{224,1... | collective-permute-start | bytes 1572872 | tf_op jit(solution)/shard_map/ppermute | solution.py:159
  86.5 1.1 copy-start.9
  87.7 14.2 %copy-start.6 = (bf16[256,8,128]{2,1,0:T(8,128)(2,1)}, bf16[256,8,128]{2,1,0:T(8,128)(2,1)S(1)}, u32[]{:S(2)}) copy-start(bf16[256,8,128]{2,1,0:T(8,128)(2,1)S(1)} %collective-permute-done.13.refs_0_) | copy-start | bytes 1572868
  101.9 24.0 %all-to-all-start.3 = ((bf16[32,40,256]{2,1,0:T(8,128)(2,1)}), bf16[32,40,256]{2,1,0:T(8,128)(2,1)S(1)}, u32[]{:S(2)}, u32[]{:S(2)}) async-start(bf16[32,40,256]{2,1,0:T(8,128)(2,1)} %bitcast.16), calls=%async_computation.3 | async-start | bytes 1310720 | tf_op jit(solution)/shard_map/all_to_all | solution.py:248
  126.8 22.6 %all-to-all-start.4 = ((bf16[16,16,256]{2,1,0:T(8,128)(2,1)}), bf16[16,16,256]{2,1,0:T(8,128)(2,1)S(1)}, u32[]{:S(2)}, u32[]{:S(2)}) async-start(bf16[16,16,256]{2,1,0:T(8,128)(2,1)} %fusion.68), calls=%async_computation.4 | async-start | bytes 262144 | tf_op jit(solution)/shard_map/all_to_all | solution.py:342
  149.6 0.6 copy-start.10

commit v5 on v4

--- a/solution.py
+++ b/solution.py
@@ -78,22 +78,30 @@
         copy.wait()
     low = lax.broadcasted_iota(jnp.int32, (8, LANES), 0) < 4
     group = 8
+    whole = slots // 32 * 32
+
+    def one_pair(p):
+        a = table[index_ref[0, p]].astype(jnp.float32)
+        b = table[index_ref[1, p]].astype(jnp.float32)
+        swapped_a = pltpu.roll(a, 4, 0)
+        swapped_b = pltpu.roll(b, 4, 0)
+        real_b = jnp.where(low, b, swapped_b)
+        imag_b = jnp.where(low, swapped_b, -b)
+        start = pl.multiple_of(p * 8, 8)
+        cross[pl.ds(start, 8), :] = a * real_b + swapped_a * imag_b
 
     def one_column(column, carry):
+        base = column * slots
+        for u in range(whole):
+            one_pair(base + u)
+
         def one_group(g, inner):
             for u in range(group):
-                p = column * slots + g * group + u
-                a = table[index_ref[0, p]].astype(jnp.float32)
-                b = table[index_ref[1, p]].astype(jnp.float32)
-                straight = a * b
-                crossed = a * pltpu.roll(b, 4, 0)
-                real_cross = straight + pltpu.roll(straight, 4, 0)
-                imag_cross = crossed - pltpu.roll(crossed, 4, 0)
-                start = pl.multiple_of(p * 8, 8)
-                cross[pl.ds(start, 8), :] = jnp.where(low, real_cross, imag_cross)
+                one_pair(base + whole + g * group + u)
             return inner
 
-        lax.fori_loop(0, (used_ref[column] + group - 1) // group, one_group, 0)
+        extra = jnp.maximum(used_ref[column] - whole + group - 1, 0) // group
+        lax.fori_loop(0, extra, one_group, 0)
         return carry
 
     lax.fori_loop(0, columns, one_column, 0)
@@ -288,7 +296,6 @@
         axis=2,
     ).transpose(1, 0, 2, 3)
     block = lax.all_to_all(outbound, "x", 0, 0, tiled=True).reshape(plane_rows, 8, LANES)
-    block, code = lax.optimization_barrier((block, code))
     codes = lax.all_to_all(code, ("z", "x"), 0, 0, tiled=True)
     basis = basis_slice(x * share, share, freqs)
     planes = jnp.arange(zs, dtype=jnp.int32)

time: 151 us -> 151 us (level)
    ppermute x4, waiting for transfers between devices: 2.58 us -> 5.31 us  [near_ring(): from_below = lax.ppermute(from_below, axis, up)]
    ppermute x4, waiting for transfers between devices: 10.4 us -> 8.16 us  [near_ring(): from_above = lax.ppermute(from_above, axis, down)]
where the time goes in v5:
time: 151 us; the launch traced here: 150 us
  starting transfers between devices  68.2 us (45%)
  waiting for transfers between devices  46.6 us (31%)
  other arithmetic  14.2 us (9%)
  Pallas kernels  8.99 us (6%)
  local copies, waits for them, and re-layouts  5.35 us (4%)
  matrix products  3.92 us (3%)
  between operations  2.37 us (2%)
    ppermute x4, starting transfers between devices, near_ring(): from_above = lax.ppermute(from_above, axis, down)  23.2 us
    all_to_all x1, starting transfers between devices, exchange_and_add(): shares = lax.all_to_all(columns, ('x', 'y', 'c'), 0, 0, tiled=True)  11.1 us
    all_to_all x1, waiting for transfers between devices, exchange_and_add(): shares = lax.all_to_all(columns, ('x', 'y', 'c'), 0, 0, tiled=True)  10.7 us
    ppermute x4, starting transfers between devices, near_ring(): from_below = lax.ppermute(from_below, axis, up)  10.6 us
    all_to_all x1, waiting for transfers between devices, body(): lax.all_to_all(leaving.reshape(zs, returned, LAGS), 'z', 0, 0, tiled=True)  9.96 us
    all_to_all x1, starting transfers between devices, body(): lax.all_to_all(leaving.reshape(zs, returned, LAGS), 'z', 0, 0, tiled=True)  9.8 us
    pallas_call x1, Pallas kernels, correlate(): pl.pallas_call(functools.partial(correlate_kernel, count), out_shape=jax....  8.99 us
    all_to_all x1, starting transfers between devices, body(): codes = lax.all_to_all(code, ('z', 'x'), 0, 0, tiled=True)  8.66 us
  transfers between devices with their start and end apart: 12, of which 10 were waited for; matrix products, arithmetic and copies ran while one was open for 11% of the time, Pallas kernels for 0%

profile of v5, /device:TPU:1, one launch (start us, length us, event | category | flops | bytes accessed | tf_op | source)
XLA Modules:
  0.0 149.9 jit_solution(4060617014635620217)
XLA Ops:
  0.0 1.4 add_sqrt_fusion
  1.7 0.8 fusion.52
  2.5 0.4 copy-done.2
  3.5 1.1 copy_bitcast_fusion.2
  4.6 4.8 %all-to-all-start.1 = ((bf16[4,64,8,128]{3,2,1,0:T(8,128)(2,1)}), bf16[4,64,8,128]{3,2,1,0:T(8,128)(2,1)S(1)}, u32[]{:S(2)}, u32[]{:S(2)}) async-start(bf16[4,64,8,128]{3,2,1,0:T(8,128)(2,1)} %copy_bitcast_fusion.2), calls=%async_computation.1 | async-start | bytes 1048576 | tf_op jit(solution)/shard_map/all_to_all | solution.py:298
  9.9 6.4 %all-to-all-done.1 = bf16[4,64,8,128]{3,2,1,0:T(8,128)(2,1)S(1)} async-done(((bf16[4,64,8,128]{3,2,1,0:T(8,128)(2,1)}), bf16[4,64,8,128]{3,2,1,0:T(8,128)(2,1)S(1)}, u32[]{:S(2)}, u32[]{:S(2)}) %all-to-all-start.1) | async-done | bytes 524320 | tf_op jit(solution)/shard_map/all_to_all | solution.py:298
  16.3 12.4 %collective-permute-start.9 = (bf16[256,8,128]{2,1,0:T(8,128)(2,1)S(1)}, bf16[256,8,128]{2,1,0:T(8,128)(2,1)S(1)}, u32[]{:S(2)}, u32[]{:S(2)}) collective-permute-start(bf16[256,8,128]{2,1,0:T(8,128)(2,1)S(1)} %bitcast.58), channel_id=1, source_target_pairs={{0,480},{32,0},{64,32},{96,64},{128,96},{160,128},{192,160},{224,1... | collective-permute-start | bytes 1572872 | tf_op jit(solution)/shard_map/ppermute | solution.py:167
  28.8 1.9 %collective-permute-start.7 = (bf16[256,8,128]{2,1,0:T(8,128)(2,1)S(1)}, bf16[256,8,128]{2,1,0:T(8,128)(2,1)S(1)}, u32[]{:S(2)}, u32[]{:S(2)}) collective-permute-start(bf16[256,8,128]{2,1,0:T(8,128)(2,1)S(1)} %bitcast.59), channel_id=1, source_target_pairs={{0,32},{32,64},{64,96},{96,128},{128,160},{160,192},{192,224},{224... | collective-permute-start | bytes 1572872 | tf_op jit(solution)/shard_map/ppermute | solution.py:166
  30.8 1.0 fusion.55
  31.7 0.7 broadcast_in_dim.74
  32.4 8.7 %all-to-all-start.2 = ((s32[64,4,128]{2,1,0:T(4,128)}), s32[64,4,128]{2,1,0:T(4,128)S(1)}, u32[]{:S(2)}, u32[]{:S(2)}) async-start(s32[64,4,128]{2,1,0:T(4,128)} %broadcast_in_dim.74), calls=%async_computation.2 | async-start | bytes 262144 | tf_op jit(solution)/shard_map/all_to_all | solution.py:299
  41.1 4.4 %collective-permute-start.10 = (bf16[256,8,128]{2,1,0:T(8,128)(2,1)S(1)}, bf16[256,8,128]{2,1,0:T(8,128)(2,1)S(1)}, u32[]{:S(2)}, u32[]{:S(2)}) collective-permute-start(bf16[256,8,128]{2,1,0:T(8,128)(2,1)S(1)} %collective-permute-done.9.refs_5_), channel_id=1, source_target_pairs={{0,480},{32,0},{64,32},{96,64},{128,96},{160,128},{192,160},{224,1... | collective-permute-start | bytes 1572872 | tf_op jit(solution)/shard_map/ppermute | solution.py:167
  45.5 1.9 %collective-permute-start.8 = (bf16[256,8,128]{2,1,0:T(8,128)(2,1)S(1)}, bf16[256,8,128]{2,1,0:T(8,128)(2,1)}, u32[]{:S(2)}, u32[]{:S(2)}) collective-permute-start(bf16[256,8,128]{2,1,0:T(8,128)(2,1)S(1)} %collective-permute-done.7.refs_3_), channel_id=1, source_target_pairs={{0,32},{32,64},{64,96},{96,128},{128,160},{160,192},{192,224},{224... | collective-permute-start | bytes 1572872 | tf_op jit(solution)/shard_map/ppermute | solution.py:166
  47.5 2.5 %multiply_convert_fusion.1 = (bf16[512,256]{1,0:T(8,128)(2,1)S(1)}, bf16[512,256]{1,0:T(8,128)(2,1)S(1)}) fusion(s32[256]{0:T(256)S(1)} %iota_add_fusion.2, s32[512]{0:T(512)S(1)} %iota_add_fusion.1), kind=kLoop, calls=%fused_computation.156 | loop fusion | flops 2490368 | bytes 527360 | tf_op jit(solution)/shard_map/convert.2
  50.1 6.0 %all-to-all-done.2 = s32[64,4,128]{2,1,0:T(4,128)S(1)} async-done(((s32[64,4,128]{2,1,0:T(4,128)}), s32[64,4,128]{2,1,0:T(4,128)S(1)}, u32[]{:S(2)}, u32[]{:S(2)}) %all-to-all-start.2) | async-done | bytes 131104 | tf_op jit(solution)/shard_map/all_to_all | solution.py:299
  56.1 3.1 %collective-permute-done.10.refs_6_ = bf16[256,8,128]{2,1,0:T(8,128)(2,1)S(1)} collective-permute-done((bf16[256,8,128]{2,1,0:T(8,128)(2,1)S(1)}, bf16[256,8,128]{2,1,0:T(8,128)(2,1)S(1)}, u32[]{:S(2)}, u32[]{:S(2)}) %collective-permute-start.10) | collective-permute-done | bytes 524320 | tf_op jit(solution)/shard_map/ppermute | solution.py:167
  59.2 1.6 %collective-permute-done.8.refs_2_ = bf16[256,8,128]{2,1,0:T(8,128)(2,1)} collective-permute-done((bf16[256,8,128]{2,1,0:T(8,128)(2,1)S(1)}, bf16[256,8,128]{2,1,0:T(8,128)(2,1)}, u32[]{:S(2)}, u32[]{:S(2)}) %collective-permute-start.8) | collective-permute-done | bytes 524320 | tf_op jit(solution)/shard_map/ppermute | solution.py:166
  60.8 2.3 %collective-permute-start.11 = (bf16[256,8,128]{2,1,0:T(8,128)(2,1)}, bf16[256,8,128]{2,1,0:T(8,128)(2,1)}, u32[]{:S(2)}, u32[]{:S(2)}) collective-permute-start(bf16[256,8,128]{2,1,0:T(8,128)(2,1)} %collective-permute-done.8.refs_2_), channel_id=1, source_target_pairs={{0,32},{32,64},{64,96},{96,128},{128,160},{160,192},{192,224},{224... | collective-permute-start | bytes 1572872 | tf_op jit(solution)/shard_map/ppermute | solution.py:166
  63.1 4.2 %collective-permute-start.12 = (bf16[256,8,128]{2,1,0:T(8,128)(2,1)S(1)}, bf16[256,8,128]{2,1,0:T(8,128)(2,1)}, u32[]{:S(2)}, u32[]{:S(2)}) collective-permute-start(bf16[256,8,128]{2,1,0:T(8,128)(2,1)S(1)} %collective-permute-done.10.refs_6_), channel_id=1, source_target_pairs={{0,480},{32,0},{64,32},{96,64},{128,96},{160,128},{192,160},{224,1... | collective-permute-start | bytes 1572872 | tf_op jit(solution)/shard_map/ppermute | solution.py:167
  67.3 0.5 slice.58
  68.5 2.9 %conditional.3 = (s32[32,512]{1,0:T(8,128)S(1)}, s32[32,512]{1,0:T(8,128)S(1)}) conditional(s32[]{:T(128)} %bitcast.13, () %tuple.32, (s32[64,4,128]{2,1,0:T(4,128)S(1)}, s32[]{:T(128)}) %tuple.33), branch_computations={%region_3.4_spmd, %region_4.11_spmd} | conditional | flops 279927264 | bytes 2145556 | solution.py:313
  68.7 0.3 copy.28
  69.5 0.3 fusion.23
  70.3 0.6 fusion.10
  70.9 0.4 multiply_reduce_fusion
  71.4 2.8 %collective-permute-done.11.refs_1_ = bf16[256,8,128]{2,1,0:T(8,128)(2,1)} collective-permute-done((bf16[256,8,128]{2,1,0:T(8,128)(2,1)}, bf16[256,8,128]{2,1,0:T(8,128)(2,1)}, u32[]{:S(2)}, u32[]{:S(2)}) %collective-permute-start.11) | collective-permute-done | bytes 524320 | tf_op jit(solution)/shard_map/ppermute | solution.py:166
  74.2 1.2 collective-permute-done.12.refs_7_
  75.4 4.5 %collective-permute-start.13 = (bf16[256,8,128]{2,1,0:T(8,128)(2,1)}, bf16[256,8,128]{2,1,0:T(8,128)(2,1)S(1)}, u32[]{:S(2)}, u32[]{:S(2)}) collective-permute-start(bf16[256,8,128]{2,1,0:T(8,128)(2,1)} %collective-permute-done.11.refs_1_), channel_id=1, source_target_pairs={{0,32},{32,64},{64,96},{96,128},{128,160},{160,192},{192,224},{224... | collective-permute-start | bytes 1572872 | tf_op jit(solution)/shard_map/ppermute | solution.py:166
  80.0 2.2 %collective-permute-start.14 = (bf16[256,8,128]{2,1,0:T(8,128)(2,1)}, bf16[256,8,128]{2,1,0:T(8,128)(2,1)}, u32[]{:S(2)}, u32[]{:S(2)}) collective-permute-start(bf16[256,8,128]{2,1,0:T(8,128)(2,1)} %collective-permute-done.12.refs_7_), channel_id=1, source_target_pairs={{0,480},{32,0},{64,32},{96,64},{128,96},{160,128},{192,160},{224,1... | collective-permute-start | bytes 1572872 | tf_op jit(solution)/shard_map/ppermute | solution.py:167
  82.2 1.0 eq.167
  83.1 4.6 %conditional.4 = (s32[2,1280]{1,0:T(2,128)S(1)}, s32[32]{0:T(128)}) conditional(s32[]{:T(128)} %bitcast.13, () %tuple.35, (s32[]{:T(128)}, s32[32,512]{1,0:T(8,128)}, s32[32,512]{1,0:T(8,128)}) %tuple.70), branch_computations={%region_17.18_spmd, %region_18.21_spmd} | conditional | flops 19114240 | bytes 356756 | solution.py:324
  83.1 1.0 convert_reduce_fusion
  84.1 0.5 broadcast_minimum_fusion
  84.8 1.5 select_reduce_fusion
  86.3 0.7 reshape.607
  87.0 0.7 and_select_fusion.1
  87.8 0.9 collective-permute-done.13.refs_0_
  88.6 3.8 %collective-permute-done.14.refs_8_ = bf16[256,8,128]{2,1,0:T(8,128)(2,1)} collective-permute-done((bf16[256,8,128]{2,1,0:T(8,128)(2,1)}, bf16[256,8,128]{2,1,0:T(8,128)(2,1)}, u32[]{:S(2)}, u32[]{:S(2)}) %collective-permute-start.14) | collective-permute-done | bytes 524320 | tf_op jit(solution)/shard_map/ppermute | solution.py:167
  92.5 9.0 %shard_map.48 = bf16[1280,256]{1,0:T(8,128)(2,1)} custom-call(s32[2,1280]{1,0:T(2,128)} %copy-done.9, s32[32]{0:T(128)} %get-tuple-element.84.used_ref, bf16[256,8,128]{2,1,0:T(8,128)(2,1)S(1)} %collective-permute-done.13.refs_0_, bf16[256,8,128]{2,1,0:T(8,128)(2,1)} %collective-permute-done.11.refs_1_, bf16[256,8,128]{2,1,0:T(8,128)(2,1)} %collective-permute-done.8.refs_2_, ...), custom_call_target="tpu_custom_call" | custom-call | tf_op jit(solution)/shard_map/pallas_call | solution.py:132
  101.5 11.1 %all-to-all-start.3 = ((bf16[32,40,256]{2,1,0:T(8,128)(2,1)}), bf16[32,40,256]{2,1,0:T(8,128)(2,1)S(1)}, u32[]{:S(2)}, u32[]{:S(2)}) async-start(bf16[32,40,256]{2,1,0:T(8,128)(2,1)} %bitcast.16), calls=%async_computation.3 | async-start | bytes 1310720 | tf_op jit(solution)/shard_map/all_to_all | solution.py:256
  112.5 2.0 %convert_reduce_fusion.4 = (f32[16,32,16]{2,1,0:T(8,128)S(1)}, f32[16,32]{1,0:T(8,128)S(1)}) fusion(s32[32,16,32]{2,1,0:T(8,128)S(1)} %eq.167), kind=kLoop, calls=%fused_computation.126 | loop fusion | flops 1039872 | bytes 100352 | tf_op jit(solution)/shard_map/reduce_sum | solution.py:329
  114.8 10.7 %all-to-all-done.3 = bf16[32,40,256]{2,1,0:T(8,128)(2,1)S(1)} async-done(((bf16[32,40,256]{2,1,0:T(8,128)(2,1)}), bf16[32,40,256]{2,1,0:T(8,128)(2,1)S(1)}, u32[]{:S(2)}, u32[]{:S(2)}) %all-to-all-start.3) | async-done | bytes 655392 | tf_op jit(solution)/shard_map/all_to_all | solution.py:256
  125.6 0.9 fusion.68
  126.5 9.8 %all-to-all-start.4 = ((bf16[16,16,256]{2,1,0:T(8,128)(2,1)}), bf16[16,16,256]{2,1,0:T(8,128)(2,1)S(1)}, u32[]{:S(2)}, u32[]{:S(2)}) async-start(bf16[16,16,256]{2,1,0:T(8,128)(2,1)} %fusion.68), calls=%async_computation.4 | async-start | bytes 262144 | tf_op jit(solution)/shard_map/all_to_all | solution.py:349
  136.3 0.7 reduce_max.28
  137.0 0.6 reduce_max.27
  139.1 10.0 %all-to-all-done.4 = bf16[16,16,256]{2,1,0:T(8,128)(2,1)S(1)} async-done(((bf16[16,16,256]{2,1,0:T(8,128)(2,1)}), bf16[16,16,256]{2,1,0:T(8,128)(2,1)S(1)}, u32[]{:S(2)}, u32[]{:S(2)}) %all-to-all-start.4) | async-done | bytes 131104 | tf_op jit(solution)/shard_map/all_to_all | solution.py:349
  149.3 0.6 copy-done.10
  (65 shorter events, 3.5 us)
Async XLA Ops:
  1.7 1.2 copy-start.2
  3.5 5.9 %copy-start.12 = (s32[256,2]{0,1:T(2,128)S(1)}, s32[256,2]{0,1:T(2,128)}, u32[]{:S(2)}) copy-start(s32[256,2]{0,1:T(2,128)} %param.11) | copy-start | bytes 6148
  3.5 5.9 %copy-start.11 = (s32[4096]{0:T(1024)S(1)}, s32[4096]{0:T(1024)}, u32[]{:S(2)}) copy-start(s32[4096]{0:T(1024)} %param.12) | copy-start | bytes 49156
  4.6 11.8 %all-to-all-start.1 = ((bf16[4,64,8,128]{3,2,1,0:T(8,128)(2,1)}), bf16[4,64,8,128]{3,2,1,0:T(8,128)(2,1)S(1)}, u32[]{:S(2)}, u32[]{:S(2)}) async-start(bf16[4,64,8,128]{3,2,1,0:T(8,128)(2,1)} %copy_bitcast_fusion.2), calls=%async_computation.1 | async-start | bytes 1048576 | tf_op jit(solution)/shard_map/all_to_all | solution.py:298
  16.3 24.7 %collective-permute-start.9 = (bf16[256,8,128]{2,1,0:T(8,128)(2,1)S(1)}, bf16[256,8,128]{2,1,0:T(8,128)(2,1)S(1)}, u32[]{:S(2)}, u32[]{:S(2)}) collective-permute-start(bf16[256,8,128]{2,1,0:T(8,128)(2,1)S(1)} %bitcast.58), channel_id=1, source_target_pairs={{0,480},{32,0},{64,32},{96,64},{128,96},{160,128},{192,160},{224,1... | collective-permute-start | bytes 1572872 | tf_op jit(solution)/shard_map/ppermute | solution.py:167
  28.8 16.7 %collective-permute-start.7 = (bf16[256,8,128]{2,1,0:T(8,128)(2,1)S(1)}, bf16[256,8,128]{2,1,0:T(8,128)(2,1)S(1)}, u32[]{:S(2)}, u32[]{:S(2)}) collective-permute-start(bf16[256,8,128]{2,1,0:T(8,128)(2,1)S(1)} %bitcast.59), channel_id=1, source_target_pairs={{0,32},{32,64},{64,96},{96,128},{128,160},{160,192},{192,224},{224... | collective-permute-start | bytes 1572872 | tf_op jit(solution)/shard_map/ppermute | solution.py:166
  32.4 23.7 %all-to-all-start.2 = ((s32[64,4,128]{2,1,0:T(4,128)}), s32[64,4,128]{2,1,0:T(4,128)S(1)}, u32[]{:S(2)}, u32[]{:S(2)}) async-start(s32[64,4,128]{2,1,0:T(4,128)} %broadcast_in_dim.74), calls=%async_computation.2 | async-start | bytes 262144 | tf_op jit(solution)/shard_map/all_to_all | solution.py:299
  41.1 51.4 %copy-start.3 = (bf16[256,8,128]{2,1,0:T(8,128)(2,1)}, bf16[256,8,128]{2,1,0:T(8,128)(2,1)S(1)}, u32[]{:S(2)}) copy-start(bf16[256,8,128]{2,1,0:T(8,128)(2,1)S(1)} %collective-permute-done.9.refs_5_) | copy-start | bytes 1572868
  41.1 18.1 %collective-permute-start.10 = (bf16[256,8,128]{2,1,0:T(8,128)(2,1)S(1)}, bf16[256,8,128]{2,1,0:T(8,128)(2,1)S(1)}, u32[]{:S(2)}, u32[]{:S(2)}) collective-permute-start(bf16[256,8,128]{2,1,0:T(8,128)(2,1)S(1)} %collective-permute-done.9.refs_5_), channel_id=1, source_target_pairs={{0,480},{32,0},{64,32},{96,64},{128,96},{160,128},{192,160},{224,1... | collective-permute-start | bytes 1572872 | tf_op jit(solution)/shard_map/ppermute | solution.py:167
  45.5 15.3 %collective-permute-start.8 = (bf16[256,8,128]{2,1,0:T(8,128)(2,1)S(1)}, bf16[256,8,128]{2,1,0:T(8,128)(2,1)}, u32[]{:S(2)}, u32[]{:S(2)}) collective-permute-start(bf16[256,8,128]{2,1,0:T(8,128)(2,1)S(1)} %collective-permute-done.7.refs_3_), channel_id=1, source_target_pairs={{0,32},{32,64},{64,96},{96,128},{128,160},{160,192},{192,224},{224... | collective-permute-start | bytes 1572872 | tf_op jit(solution)/shard_map/ppermute | solution.py:166
  60.8 13.4 %collective-permute-start.11 = (bf16[256,8,128]{2,1,0:T(8,128)(2,1)}, bf16[256,8,128]{2,1,0:T(8,128)(2,1)}, u32[]{:S(2)}, u32[]{:S(2)}) collective-permute-start(bf16[256,8,128]{2,1,0:T(8,128)(2,1)} %collective-permute-done.8.refs_2_), channel_id=1, source_target_pairs={{0,32},{32,64},{64,96},{96,128},{128,160},{160,192},{192,224},{224... | collective-permute-start | bytes 1572872 | tf_op jit(solution)/shard_map/ppermute | solution.py:166
  63.1 12.3 %collective-permute-start.12 = (bf16[256,8,128]{2,1,0:T(8,128)(2,1)S(1)}, bf16[256,8,128]{2,1,0:T(8,128)(2,1)}, u32[]{:S(2)}, u32[]{:S(2)}) collective-permute-start(bf16[256,8,128]{2,1,0:T(8,128)(2,1)S(1)} %collective-permute-done.10.refs_6_), channel_id=1, source_target_pairs={{0,480},{32,0},{64,32},{96,64},{128,96},{160,128},{192,160},{224,1... | collective-permute-start | bytes 1572872 | tf_op jit(solution)/shard_map/ppermute | solution.py:167
  71.3 10.8 %copy-start.7 = (s32[32,512]{1,0:T(8,128)}, s32[32,512]{1,0:T(8,128)S(1)}, u32[]{:S(2)}) copy-start(s32[32,512]{1,0:T(8,128)S(1)} %get-tuple-element.81) | copy-start | bytes 196612
  71.4 10.8 %copy-start.8 = (s32[32,512]{1,0:T(8,128)}, s32[32,512]{1,0:T(8,128)S(1)}, u32[]{:S(2)}) copy-start(s32[32,512]{1,0:T(8,128)S(1)} %get-tuple-element.82) | copy-start | bytes 196612
  75.4 13.2 %collective-permute-start.13 = (bf16[256,8,128]{2,1,0:T(8,128)(2,1)}, bf16[256,8,128]{2,1,0:T(8,128)(2,1)S(1)}, u32[]{:S(2)}, u32[]{:S(2)}) collective-permute-start(bf16[256,8,128]{2,1,0:T(8,128)(2,1)} %collective-permute-done.11.refs_1_), channel_id=1, source_target_pairs={{0,32},{32,64},{64,96},{96,128},{128,160},{160,192},{192,224},{224... | collective-permute-start | bytes 1572872 | tf_op jit(solution)/shard_map/ppermute | solution.py:166
  80.0 12.5 %collective-permute-start.14 = (bf16[256,8,128]{2,1,0:T(8,128)(2,1)}, bf16[256,8,128]{2,1,0:T(8,128)(2,1)}, u32[]{:S(2)}, u32[]{:S(2)}) collective-permute-start(bf16[256,8,128]{2,1,0:T(8,128)(2,1)} %collective-permute-done.12.refs_7_), channel_id=1, source_target_pairs={{0,480},{32,0},{64,32},{96,64},{128,96},{160,128},{192,160},{224,1... | collective-permute-start | bytes 1572872 | tf_op jit(solution)/shard_map/ppermute | solution.py:167
  87.7 0.9 copy-start.9
  88.6 12.8 %copy-start.6 = (bf16[256,8,128]{2,1,0:T(8,128)(2,1)}, bf16[256,8,128]{2,1,0:T(8,128)(2,1)S(1)}, u32[]{:S(2)}) copy-start(bf16[256,8,128]{2,1,0:T(8,128)(2,1)S(1)} %collective-permute-done.13.refs_0_) | copy-start | bytes 1572868
  101.5 24.0 %all-to-all-start.3 = ((bf16[32,40,256]{2,1,0:T(8,128)(2,1)}), bf16[32,40,256]{2,1,0:T(8,128)(2,1)S(1)}, u32[]{:S(2)}, u32[]{:S(2)}) async-start(bf16[32,40,256]{2,1,0:T(8,128)(2,1)} %bitcast.16), calls=%async_computation.3 | async-start | bytes 1310720 | tf_op jit(solution)/shard_map/all_to_all | solution.py:256
  126.5 22.6 %all-to-all-start.4 = ((bf16[16,16,256]{2,1,0:T(8,128)(2,1)}), bf16[16,16,256]{2,1,0:T(8,128)(2,1)S(1)}, u32[]{:S(2)}, u32[]{:S(2)}) async-start(bf16[16,16,256]{2,1,0:T(8,128)(2,1)} %fusion.68), calls=%async_computation.4 | async-start | bytes 262144 | tf_op jit(solution)/shard_map/all_to_all | solution.py:349
  149.2 0.6 copy-start.10

commit v6 on v5

--- a/solution.py
+++ b/solution.py
@@ -51,13 +51,8 @@
     )
 
 
-def correlate_kernel(count, index_ref, used_ref, *refs):
-    blocks = refs[:count]
-    basis_ref, out_ref, table, cross, sems = refs[count:]
-    block_rows = blocks[0].shape[0]
-    slot_count = out_ref.shape[0]
-    columns = used_ref.shape[0]
-    slots = slot_count // columns
+def load_table(blocks, table, sems):
+    count, block_rows = len(blocks), blocks[0].shape[0]
     copies = [
         pltpu.make_async_copy(
             blocks[k], table.at[pl.ds(k * block_rows, block_rows)], sems.at[k]
@@ -68,14 +63,36 @@
         copy.start()
     zero_rows = table.shape[0] - count * block_rows
     table[pl.ds(count * block_rows, zero_rows)] = jnp.zeros((zero_rows, 8, LANES), table.dtype)
-
+    return copies
+
+
+def loading_kernel(count, index_ref, used_ref, *refs):
+    blocks = refs[:count]
+    basis_ref, out_ref, table, cross, sems = refs[count:]
+    copies = load_table(blocks, table, sems)
+    clear_rows(cross)
+    for copy in copies:
+        copy.wait()
+    cross_and_contract(index_ref, used_ref, table, basis_ref, out_ref, cross)
+
+
+def reusing_kernel(index_ref, used_ref, table, basis_ref, out_ref, cross):
+    clear_rows(cross)
+    cross_and_contract(index_ref, used_ref, table, basis_ref, out_ref, cross)
+
+
+def clear_rows(cross):
     def clear(i, carry):
         cross[pl.ds(pl.multiple_of(i * 256, 256), 256), :] = jnp.zeros((256, LANES), jnp.float32)
         return carry
 
-    lax.fori_loop(0, slot_count * 8 // 256, clear, 0)
-    for copy in copies:
-        copy.wait()
+    lax.fori_loop(0, cross.shape[0] // 256, clear, 0)
+
+
+def cross_and_contract(index_ref, used_ref, table, basis_ref, out_ref, cross):
+    slot_count = out_ref.shape[0]
+    columns = used_ref.shape[0]
+    slots = slot_count // columns
     low = lax.broadcasted_iota(jnp.int32, (8, LANES), 0) < 4
     group = 8
     whole = slots // 32 * 32
@@ -105,7 +122,7 @@
         return carry
 
     lax.fori_loop(0, columns, one_column, 0)
-    step = 256
+    step = 128
 
     def one_dot(i, carry):
         start = pl.multiple_of(i * step * 8, step * 8)
@@ -130,17 +147,36 @@
     vmem = pl.BlockSpec(memory_space=pltpu.VMEM)
     smem = pl.BlockSpec(memory_space=pltpu.SMEM)
     return pl.pallas_call(
-        functools.partial(correlate_kernel, count),
-        out_shape=jax.ShapeDtypeStruct((slot_count, LAGS), jnp.bfloat16),
+        functools.partial(loading_kernel, count),
+        out_shape=[
+            jax.ShapeDtypeStruct((slot_count, LAGS), jnp.bfloat16),
+            jax.ShapeDtypeStruct((count * block_rows + 8, 8, LANES), jnp.bfloat16),
+        ],
         in_specs=[smem, smem] + [pl.BlockSpec(memory_space=pl.ANY)] * count + [vmem],
-        out_specs=vmem,
+        out_specs=[vmem, vmem],
         scratch_shapes=[
-            pltpu.VMEM((count * block_rows + 8, 8, LANES), jnp.bfloat16),
             pltpu.VMEM((slot_count * 8, LANES), jnp.float32),
             pltpu.SemaphoreType.DMA((count,)),
         ],
-        compiler_params=pltpu.CompilerParams(vmem_limit_bytes=36 * 1024 * 1024),
+        compiler_params=pltpu.CompilerParams(vmem_limit_bytes=40 * 1024 * 1024),
     )(index, used, *blocks, basis)
+
+
+def correlate_again(index, used, table, basis):
+    slot_count = index.shape[1]
+    vmem = pl.BlockSpec(memory_space=pltpu.VMEM)
+    smem = pl.BlockSpec(memory_space=pltpu.SMEM)
+    return pl.pallas_call(
+        reusing_kernel,
+        out_shape=jax.ShapeDtypeStruct((slot_count, LAGS), jnp.bfloat16),
+        in_specs=[smem, smem, vmem, vmem],
+        out_specs=vmem,
+        scratch_shapes=[pltpu.VMEM((slot_count * 8, LANES), jnp.float32)],
+        compiler_params=pltpu.CompilerParams(vmem_limit_bytes=32 * 1024 * 1024),
+        cost_estimate=pl.CostEstimate(
+            flops=2 * slot_count * 8 * LANES * LAGS, bytes_accessed=8 << 20, transcendentals=0
+        ),
+    )(index, used, table, basis)
 
 
 def shifts(size):
@@ -296,6 +332,7 @@
         axis=2,
     ).transpose(1, 0, 2, 3)
     block = lax.all_to_all(outbound, "x", 0, 0, tiled=True).reshape(plane_rows, 8, LANES)
+    block, code = lax.optimization_barrier((block, code))
     codes = lax.all_to_all(code, ("z", "x"), 0, 0, tiled=True)
     basis = basis_slice(x * share, share, freqs)
     planes = jnp.arange(zs, dtype=jnp.int32)
@@ -322,8 +359,22 @@
         return jnp.zeros((2, columns * slots), jnp.int32), jnp.zeros((columns,), jnp.int32)
 
     index, used = lax.cond(codes[0, 0, 0] >= -1, first_branch, second_branch, middle, packed)
-    partial = correlate(index, used, near, basis)
-    added = exchange_and_add(partial, columns)
+    core = lax.axis_index("c")
+    by_core = index.reshape(2, columns // cs, cs, slots)
+    used_by_core = used.reshape(columns // cs, cs)
+
+    def of_core(k):
+        some = lax.dynamic_index_in_dim(by_core, k, 2, keepdims=False).reshape(2, -1)
+        return some, lax.dynamic_index_in_dim(used_by_core, k, 1, keepdims=False)
+
+    other_index, other_used = of_core(1 - core)
+    own_index, own_used = of_core(core)
+    for_other, table = correlate(other_index, other_used, near, basis)
+    from_other = lax.ppermute(for_other, "c", [(0, 1), (1, 0)])
+    for_own = correlate_again(own_index, own_used, table, basis)
+    both = (for_own.astype(jnp.float32) + from_other.astype(jnp.float32)).astype(jnp.bfloat16)
+    shares = lax.all_to_all(both.reshape(xs * ys, slots, LAGS), ("x", "y"), 0, 0, tiled=True)
+    added = jnp.sum(shares.astype(jnp.float32), axis=0)
 
     middle_by_owner = middle.reshape(columns, zs, own)
     meets = jnp.sum(
@@ -359,7 +410,7 @@
         plane_index = jnp.where(plane_codes >= 0, plane_at, zs * plane_rows)
         blocks = near + far_ring(near, "z", reach)
         every = jnp.full((columns,), own, jnp.int32)
-        return exchange_and_add(correlate(plane_index, every, blocks, basis), columns) * scale
+        return exchange_and_add(correlate(plane_index, every, blocks, basis)[0], columns) * scale
 
     return lax.cond(
         crowded, by_owner, lambda near, codes, by_middle: by_middle, near, codes, by_middle

time: 151 us -> 151 us (level)
  waiting for transfers between devices: 46.6 us -> 42.3 us
  starting transfers between devices: 68.2 us -> 70.4 us
    ppermute x0 -> x1, starting transfers between devices: none -> 6.13 us  [body(): from_other = lax.ppermute(for_other, 'c', [(0, 1), (1, 0)])]
    all_to_all x1, starting transfers between devices: 11.1 us -> 6.75 us  [body(): lax.all_to_all(both.reshape(xs * ys, slots, LAGS), ('x', 'y'), 0, 0, tile...]
    all_to_all x1, waiting for transfers between devices: 10.7 us -> 8.3 us  [body(): lax.all_to_all(both.reshape(xs * ys, slots, LAGS), ('x', 'y'), 0, 0, tile...]
    ppermute x4, waiting for transfers between devices: 8.16 us -> 10.4 us  [near_ring(): from_above = lax.ppermute(from_above, axis, down)]
    all_to_all x1, waiting for transfers between devices: 9.96 us -> 8.31 us  [body(): lax.all_to_all(leaving.reshape(zs, returned, LAGS), 'z', 0, 0, tiled=True)]
    ppermute x4, waiting for transfers between devices: 5.31 us -> 3.77 us  [near_ring(): from_below = lax.ppermute(from_below, axis, up)]
    pallas_call x1 -> x2, Pallas kernels: 8.99 us -> 9.71 us  [the longest x1 5.65 us: correlate(): pl.pallas_call(functools.partial(loading_kernel, count), out_shape=[jax.S...]
  transfers between devices with their start and end apart: 12 -> 13, of which waited for: 10 -> 10; matrix products, arithmetic and copies ran while one was open for 11% -> 11% of each run, Pallas kernels for 0% -> 3%
where the time goes in v6:
time: 151 us; the launch traced here: 149 us
  starting transfers between devices  70.4 us (47%)
  waiting for transfers between devices  42.3 us (28%)
  other arithmetic  14.8 us (10%)
  Pallas kernels  9.71 us (6%)
  local copies, waits for them, and re-layouts  5.14 us (3%)
  matrix products  3.93 us (3%)
  between operations  2.38 us (2%)
    ppermute x4, starting transfers between devices, near_ring(): from_above = lax.ppermute(from_above, axis, down)  22.2 us
    ppermute x4, starting transfers between devices, near_ring(): from_below = lax.ppermute(from_below, axis, up)  12.1 us
    ppermute x4, waiting for transfers between devices, near_ring(): from_above = lax.ppermute(from_above, axis, down)  10.4 us
    all_to_all x1, starting transfers between devices, body(): lax.all_to_all(leaving.reshape(zs, returned, LAGS), 'z', 0, 0, tiled=True)  9.73 us
    all_to_all x1, starting transfers between devices, body(): codes = lax.all_to_all(code, ('z', 'x'), 0, 0, tiled=True)  8.68 us
    all_to_all x1, waiting for transfers between devices, body(): lax.all_to_all(leaving.reshape(zs, returned, LAGS), 'z', 0, 0, tiled=True)  8.31 us
    all_to_all x1, waiting for transfers between devices, body(): lax.all_to_all(both.reshape(xs * ys, slots, LAGS), ('x', 'y'), 0, 0, tile...  8.3 us
    all_to_all x1, starting transfers between devices, body(): lax.all_to_all(both.reshape(xs * ys, slots, LAGS), ('x', 'y'), 0, 0, tile...  6.75 us
  transfers between devices with their start and end apart: 13, of which 10 were waited for; matrix products, arithmetic and copies ran while one was open for 11% of the time, Pallas kernels for 3%

profile of v6, /device:TPU:1, one launch (start us, length us, event | category | flops | bytes accessed | tf_op | source)
XLA Modules:
  0.0 148.9 jit_solution(8533575139489997606)
XLA Ops:
  0.0 1.4 add_sqrt_fusion
  1.7 0.8 fusion.52
  3.4 1.1 copy_bitcast_fusion.2
  4.5 4.8 %all-to-all-start.1 = ((bf16[4,64,8,128]{3,2,1,0:T(8,128)(2,1)}), bf16[4,64,8,128]{3,2,1,0:T(8,128)(2,1)S(1)}, u32[]{:S(2)}, u32[]{:S(2)}) async-start(bf16[4,64,8,128]{3,2,1,0:T(8,128)(2,1)} %copy_bitcast_fusion.2), calls=%async_computation.1 | async-start | bytes 1048576 | tf_op jit(solution)/shard_map/all_to_all | solution.py:334
  9.5 0.3 fusion.61
  9.8 1.0 fusion.55
  10.8 5.4 %all-to-all-done.1 = bf16[4,64,8,128]{3,2,1,0:T(8,128)(2,1)S(1)} async-done(((bf16[4,64,8,128]{3,2,1,0:T(8,128)(2,1)}), bf16[4,64,8,128]{3,2,1,0:T(8,128)(2,1)S(1)}, u32[]{:S(2)}, u32[]{:S(2)}) %all-to-all-start.1) | async-done | bytes 524320 | tf_op jit(solution)/shard_map/all_to_all | solution.py:334
  16.2 0.7 broadcast_in_dim.74
  16.9 12.4 %collective-permute-start.9 = (bf16[256,8,128]{2,1,0:T(8,128)(2,1)S(1)}, bf16[256,8,128]{2,1,0:T(8,128)(2,1)S(1)}, u32[]{:S(2)}, u32[]{:S(2)}) collective-permute-start(bf16[256,8,128]{2,1,0:T(8,128)(2,1)S(1)} %bitcast.59), channel_id=1, source_target_pairs={{0,480},{32,0},{64,32},{96,64},{128,96},{160,128},{192,160},{224,1... | collective-permute-start | bytes 1572872 | tf_op jit(solution)/shard_map/ppermute | solution.py:203
  29.4 1.9 %collective-permute-start.7 = (bf16[256,8,128]{2,1,0:T(8,128)(2,1)S(1)}, bf16[256,8,128]{2,1,0:T(8,128)(2,1)S(1)}, u32[]{:S(2)}, u32[]{:S(2)}) collective-permute-start(bf16[256,8,128]{2,1,0:T(8,128)(2,1)S(1)} %bitcast.60), channel_id=1, source_target_pairs={{0,32},{32,64},{64,96},{96,128},{128,160},{160,192},{192,224},{224... | collective-permute-start | bytes 1572872 | tf_op jit(solution)/shard_map/ppermute | solution.py:202
  31.3 8.7 %all-to-all-start.2 = ((s32[64,4,128]{2,1,0:T(4,128)}), s32[64,4,128]{2,1,0:T(4,128)S(1)}, u32[]{:S(2)}, u32[]{:S(2)}) async-start(s32[64,4,128]{2,1,0:T(4,128)} %broadcast_in_dim.74), calls=%async_computation.2 | async-start | bytes 262144 | tf_op jit(solution)/shard_map/all_to_all | solution.py:336
  40.0 4.4 %collective-permute-start.10 = (bf16[256,8,128]{2,1,0:T(8,128)(2,1)S(1)}, bf16[256,8,128]{2,1,0:T(8,128)(2,1)S(1)}, u32[]{:S(2)}, u32[]{:S(2)}) collective-permute-start(bf16[256,8,128]{2,1,0:T(8,128)(2,1)S(1)} %collective-permute-done.9.refs_5_), channel_id=1, source_target_pairs={{0,480},{32,0},{64,32},{96,64},{128,96},{160,128},{192,160},{224,1... | collective-permute-start | bytes 1572872 | tf_op jit(solution)/shard_map/ppermute | solution.py:203
  44.4 1.9 %collective-permute-start.8 = (bf16[256,8,128]{2,1,0:T(8,128)(2,1)S(1)}, bf16[256,8,128]{2,1,0:T(8,128)(2,1)}, u32[]{:S(2)}, u32[]{:S(2)}) collective-permute-start(bf16[256,8,128]{2,1,0:T(8,128)(2,1)S(1)} %collective-permute-done.7.refs_3_), channel_id=1, source_target_pairs={{0,32},{32,64},{64,96},{96,128},{128,160},{160,192},{192,224},{224... | collective-permute-start | bytes 1572872 | tf_op jit(solution)/shard_map/ppermute | solution.py:202
  46.4 2.5 %multiply_convert_fusion.1 = (bf16[512,256]{1,0:T(8,128)(2,1)S(1)}, bf16[512,256]{1,0:T(8,128)(2,1)S(1)}) fusion(s32[256]{0:T(256)S(1)} %iota_add_fusion.2, s32[512]{0:T(512)S(1)} %iota_add_fusion.1), kind=kLoop, calls=%fused_computation.159 | loop fusion | flops 2490368 | bytes 527360 | tf_op jit(solution)/shard_map/convert.2
  49.0 6.2 %all-to-all-done.2 = s32[64,4,128]{2,1,0:T(4,128)S(1)} async-done(((s32[64,4,128]{2,1,0:T(4,128)}), s32[64,4,128]{2,1,0:T(4,128)S(1)}, u32[]{:S(2)}, u32[]{:S(2)}) %all-to-all-start.2) | async-done | bytes 131104 | tf_op jit(solution)/shard_map/all_to_all | solution.py:336
  55.1 2.9 %collective-permute-done.10.refs_6_ = bf16[256,8,128]{2,1,0:T(8,128)(2,1)S(1)} collective-permute-done((bf16[256,8,128]{2,1,0:T(8,128)(2,1)S(1)}, bf16[256,8,128]{2,1,0:T(8,128)(2,1)S(1)}, u32[]{:S(2)}, u32[]{:S(2)}) %collective-permute-start.10) | collective-permute-done | bytes 524320 | tf_op jit(solution)/shard_map/ppermute | solution.py:203
  58.0 0.6 collective-permute-done.8.refs_2_
  58.6 3.1 %collective-permute-start.11 = (bf16[256,8,128]{2,1,0:T(8,128)(2,1)}, bf16[256,8,128]{2,1,0:T(8,128)(2,1)}, u32[]{:S(2)}, u32[]{:S(2)}) collective-permute-start(bf16[256,8,128]{2,1,0:T(8,128)(2,1)} %collective-permute-done.8.refs_2_), channel_id=1, source_target_pairs={{0,32},{32,64},{64,96},{96,128},{128,160},{160,192},{192,224},{224... | collective-permute-start | bytes 1572872 | tf_op jit(solution)/shard_map/ppermute | solution.py:202
  61.7 3.4 %collective-permute-start.12 = (bf16[256,8,128]{2,1,0:T(8,128)(2,1)S(1)}, bf16[256,8,128]{2,1,0:T(8,128)(2,1)}, u32[]{:S(2)}, u32[]{:S(2)}) collective-permute-start(bf16[256,8,128]{2,1,0:T(8,128)(2,1)S(1)} %collective-permute-done.10.refs_6_), channel_id=1, source_target_pairs={{0,480},{32,0},{64,32},{96,64},{128,96},{160,128},{192,160},{224,1... | collective-permute-start | bytes 1572872 | tf_op jit(solution)/shard_map/ppermute | solution.py:203
  65.1 0.6 slice.58
  66.4 2.9 %conditional.3 = (s32[32,512]{1,0:T(8,128)S(1)}, s32[32,512]{1,0:T(8,128)S(1)}) conditional(s32[]{:T(128)} %bitcast.14, () %tuple.38, (s32[64,4,128]{2,1,0:T(4,128)S(1)}, s32[]{:T(128)}) %tuple.39), branch_computations={%region_3.4_spmd, %region_4.11_spmd} | conditional | flops 279927264 | bytes 2145556 | solution.py:350
  66.6 0.3 copy.28
  67.4 0.3 fusion.23
  68.2 0.6 fusion.10
  68.8 0.4 multiply_reduce_fusion
  69.3 0.8 collective-permute-done.11.refs_1_
  70.1 3.6 %collective-permute-done.12.refs_7_ = bf16[256,8,128]{2,1,0:T(8,128)(2,1)} collective-permute-done((bf16[256,8,128]{2,1,0:T(8,128)(2,1)S(1)}, bf16[256,8,128]{2,1,0:T(8,128)(2,1)}, u32[]{:S(2)}, u32[]{:S(2)}) %collective-permute-start.12) | collective-permute-done | bytes 524320 | tf_op jit(solution)/shard_map/ppermute | solution.py:203
  73.7 5.1 %collective-permute-start.13 = (bf16[256,8,128]{2,1,0:T(8,128)(2,1)}, bf16[256,8,128]{2,1,0:T(8,128)(2,1)}, u32[]{:S(2)}, u32[]{:S(2)}) collective-permute-start(bf16[256,8,128]{2,1,0:T(8,128)(2,1)} %collective-permute-done.11.refs_1_), channel_id=1, source_target_pairs={{0,32},{32,64},{64,96},{96,128},{128,160},{160,192},{192,224},{224... | collective-permute-start | bytes 1572872 | tf_op jit(solution)/shard_map/ppermute | solution.py:202
  78.8 1.9 %collective-permute-start.14 = (bf16[256,8,128]{2,1,0:T(8,128)(2,1)}, bf16[256,8,128]{2,1,0:T(8,128)(2,1)}, u32[]{:S(2)}, u32[]{:S(2)}) collective-permute-start(bf16[256,8,128]{2,1,0:T(8,128)(2,1)} %collective-permute-done.12.refs_7_), channel_id=1, source_target_pairs={{0,480},{32,0},{64,32},{96,64},{128,96},{160,128},{192,160},{224,1... | collective-permute-start | bytes 1572872 | tf_op jit(solution)/shard_map/ppermute | solution.py:203
  80.8 1.0 eq.167
  81.8 2.9 %conditional.4 = (s32[2,16,2,40]{3,2,1,0:T(2,128)S(1)}, s32[16,2]{1,0:T(8,128)S(1)}) conditional(s32[]{:T(128)} %bitcast.14, () %tuple.41, (s32[]{:T(128)}, s32[32,512]{1,0:T(8,128)}, s32[32,512]{1,0:T(8,128)}) %tuple.76), branch_computations={%region_17.18_spmd, %region_18.21_spmd} | conditional | flops 19112960 | bytes 336532 | solution.py:361
  81.8 1.0 convert_reduce_fusion
  83.1 1.5 select_reduce_fusion
  85.1 2.4 %collective-permute-done.13.refs_0_ = bf16[256,8,128]{2,1,0:T(8,128)(2,1)} collective-permute-done((bf16[256,8,128]{2,1,0:T(8,128)(2,1)}, bf16[256,8,128]{2,1,0:T(8,128)(2,1)}, u32[]{:S(2)}, u32[]{:S(2)}) %collective-permute-start.13) | collective-permute-done | bytes 524320 | tf_op jit(solution)/shard_map/ppermute | solution.py:202
  87.5 3.8 %collective-permute-done.14.refs_8_ = bf16[256,8,128]{2,1,0:T(8,128)(2,1)} collective-permute-done((bf16[256,8,128]{2,1,0:T(8,128)(2,1)}, bf16[256,8,128]{2,1,0:T(8,128)(2,1)}, u32[]{:S(2)}, u32[]{:S(2)}) %collective-permute-start.14) | collective-permute-done | bytes 524320 | tf_op jit(solution)/shard_map/ppermute | solution.py:203
  91.3 5.6 %shard_map.48 = (bf16[640,256]{1,0:T(8,128)(2,1)S(1)}, bf16[2312,8,128]{2,1,0:T(8,128)(2,1)S(1)}) custom-call(s32[2,640]{1,0:T(2,128)S(1)} %reshape.654.index_ref, s32[16]{0:T(128)S(1)} %get-tuple-element.113.used_ref, bf16[256,8,128]{2,1,0:T(8,128)(2,1)} %collective-permute-done.13.refs_0_, bf16[256,8,128]{2,1,0:T(8,128)(2,1)} %collective-permute-done.11.refs_1_, ...), custom_call_target="tpu_custom_call" | custom-call | tf_op jit(solution)/shard_map/pallas_call | solution.py:149
  97.0 6.1 %collective-permute-start.15 = (bf16[640,256]{1,0:T(8,128)(2,1)S(1)}, bf16[640,256]{1,0:T(8,128)(2,1)S(1)}, u32[]{:S(2)}, u32[]{:S(2)}) collective-permute-start(bf16[640,256]{1,0:T(8,128)(2,1)S(1)} %get-tuple-element.98), channel_id=1, source_target_pairs={{0,1},{1,0},{2,3},{3,2},{4,5},{5,4},{6,7},{7,6},{8,9},{9,8},{10,11... | collective-permute-start | bytes 983048 | tf_op jit(solution)/shard_map/ppermute | solution.py:373
  103.1 2.0 %convert_reduce_fusion.4 = (f32[16,32,16]{2,1,0:T(8,128)S(1)}, f32[16,32]{1,0:T(8,128)S(1)}) fusion(s32[32,16,32]{2,1,0:T(8,128)S(1)} %eq.167), kind=kLoop, calls=%fused_computation.128 | loop fusion | flops 1039872 | bytes 100352 | tf_op jit(solution)/shard_map/reduce_sum | solution.py:380
  105.2 4.1 %shard_map.49 = bf16[640,256]{1,0:T(8,128)(2,1)S(1)} custom-call(s32[2,640]{1,0:T(2,128)S(1)} %reshape.653.index_ref, s32[16]{0:T(128)S(1)} %get-tuple-element.112.used_ref, bf16[2312,8,128]{2,1,0:T(8,128)(2,1)S(1)} %get-tuple-element.97.table, bf16[1024,256]{1,0:T(8,128)(2,1)S(1)} %pad_maximum_fusion.2.refs_9_.basis_ref), custom_call_target="tpu_custom_call" | custom-call | flops 335544320 | bytes 8388608 | tf_op jit(solution)/shard_map/pallas_call | solution.py:169
  109.3 0.8 add_convert_fusion
  110.1 6.7 %all-to-all-start.3 = ((bf16[16,40,256]{2,1,0:T(8,128)(2,1)}), bf16[16,40,256]{2,1,0:T(8,128)(2,1)S(1)}, u32[]{:S(2)}, u32[]{:S(2)}) async-start(bf16[16,40,256]{2,1,0:T(8,128)(2,1)} %bitcast.17), calls=%async_computation.3 | async-start | bytes 655360 | tf_op jit(solution)/shard_map/all_to_all | solution.py:376
  117.0 8.3 %all-to-all-done.3 = bf16[16,40,256]{2,1,0:T(8,128)(2,1)S(1)} async-done(((bf16[16,40,256]{2,1,0:T(8,128)(2,1)}), bf16[16,40,256]{2,1,0:T(8,128)(2,1)S(1)}, u32[]{:S(2)}, u32[]{:S(2)}) %all-to-all-start.3) | async-done | bytes 327712 | tf_op jit(solution)/shard_map/all_to_all | solution.py:376
  125.4 0.9 fusion.68
  126.2 9.7 %all-to-all-start.4 = ((bf16[16,16,256]{2,1,0:T(8,128)(2,1)}), bf16[16,16,256]{2,1,0:T(8,128)(2,1)S(1)}, u32[]{:S(2)}, u32[]{:S(2)}) async-start(bf16[16,16,256]{2,1,0:T(8,128)(2,1)} %fusion.68), calls=%async_computation.4 | async-start | bytes 262144 | tf_op jit(solution)/shard_map/all_to_all | solution.py:400
  136.0 1.6 %reduce_max.28 = f32[]{:T(128)} reduce(f32[16,32,16]{2,1,0:T(8,128)} %copy-done.6, f32[]{:T(128)} %constant.403.clone.1), dimensions={0,1,2}, to_apply=%region_14.15 | reduce | flops 8191 | bytes 32776 | tf_op jit(solution)/shard_map/reduce_max | solution.py:383
  137.6 0.7 reduce_max.27
  139.7 8.3 %all-to-all-done.4 = bf16[16,16,256]{2,1,0:T(8,128)(2,1)S(1)} async-done(((bf16[16,16,256]{2,1,0:T(8,128)(2,1)}), bf16[16,16,256]{2,1,0:T(8,128)(2,1)S(1)}, u32[]{:S(2)}, u32[]{:S(2)}) %all-to-all-start.4) | async-done | bytes 131104 | tf_op jit(solution)/shard_map/all_to_all | solution.py:400
  148.3 0.6 copy-done.9
  (68 shorter events, 4.1 us)
Async XLA Ops:
  1.5 1.2 copy-start.2
  2.8 6.5 %copy-start.11 = (s32[256,2]{0,1:T(2,128)S(1)}, s32[256,2]{0,1:T(2,128)}, u32[]{:S(2)}) copy-start(s32[256,2]{0,1:T(2,128)} %param.11) | copy-start | bytes 6148
  2.8 6.6 %copy-start.10 = (s32[4096]{0:T(1024)S(1)}, s32[4096]{0:T(1024)}, u32[]{:S(2)}) copy-start(s32[4096]{0:T(1024)} %param.12) | copy-start | bytes 49156
  4.5 11.8 %all-to-all-start.1 = ((bf16[4,64,8,128]{3,2,1,0:T(8,128)(2,1)}), bf16[4,64,8,128]{3,2,1,0:T(8,128)(2,1)S(1)}, u32[]{:S(2)}, u32[]{:S(2)}) async-start(bf16[4,64,8,128]{3,2,1,0:T(8,128)(2,1)} %copy_bitcast_fusion.2), calls=%async_computation.1 | async-start | bytes 1048576 | tf_op jit(solution)/shard_map/all_to_all | solution.py:334
  16.9 23.1 %collective-permute-start.9 = (bf16[256,8,128]{2,1,0:T(8,128)(2,1)S(1)}, bf16[256,8,128]{2,1,0:T(8,128)(2,1)S(1)}, u32[]{:S(2)}, u32[]{:S(2)}) collective-permute-start(bf16[256,8,128]{2,1,0:T(8,128)(2,1)S(1)} %bitcast.59), channel_id=1, source_target_pairs={{0,480},{32,0},{64,32},{96,64},{128,96},{160,128},{192,160},{224,1... | collective-permute-start | bytes 1572872 | tf_op jit(solution)/shard_map/ppermute | solution.py:203
  29.4 15.1 %collective-permute-start.7 = (bf16[256,8,128]{2,1,0:T(8,128)(2,1)S(1)}, bf16[256,8,128]{2,1,0:T(8,128)(2,1)S(1)}, u32[]{:S(2)}, u32[]{:S(2)}) collective-permute-start(bf16[256,8,128]{2,1,0:T(8,128)(2,1)S(1)} %bitcast.60), channel_id=1, source_target_pairs={{0,32},{32,64},{64,96},{96,128},{128,160},{160,192},{192,224},{224... | collective-permute-start | bytes 1572872 | tf_op jit(solution)/shard_map/ppermute | solution.py:202
  31.3 23.8 %all-to-all-start.2 = ((s32[64,4,128]{2,1,0:T(4,128)}), s32[64,4,128]{2,1,0:T(4,128)S(1)}, u32[]{:S(2)}, u32[]{:S(2)}) async-start(s32[64,4,128]{2,1,0:T(4,128)} %broadcast_in_dim.74), calls=%async_computation.2 | async-start | bytes 262144 | tf_op jit(solution)/shard_map/all_to_all | solution.py:336
  40.0 18.0 %collective-permute-start.10 = (bf16[256,8,128]{2,1,0:T(8,128)(2,1)S(1)}, bf16[256,8,128]{2,1,0:T(8,128)(2,1)S(1)}, u32[]{:S(2)}, u32[]{:S(2)}) collective-permute-start(bf16[256,8,128]{2,1,0:T(8,128)(2,1)S(1)} %collective-permute-done.9.refs_5_), channel_id=1, source_target_pairs={{0,480},{32,0},{64,32},{96,64},{128,96},{160,128},{192,160},{224,1... | collective-permute-start | bytes 1572872 | tf_op jit(solution)/shard_map/ppermute | solution.py:203
  44.4 14.2 %collective-permute-start.8 = (bf16[256,8,128]{2,1,0:T(8,128)(2,1)S(1)}, bf16[256,8,128]{2,1,0:T(8,128)(2,1)}, u32[]{:S(2)}, u32[]{:S(2)}) collective-permute-start(bf16[256,8,128]{2,1,0:T(8,128)(2,1)S(1)} %collective-permute-done.7.refs_3_), channel_id=1, source_target_pairs={{0,32},{32,64},{64,96},{96,128},{128,160},{160,192},{192,224},{224... | collective-permute-start | bytes 1572872 | tf_op jit(solution)/shard_map/ppermute | solution.py:202
  58.6 11.4 %collective-permute-start.11 = (bf16[256,8,128]{2,1,0:T(8,128)(2,1)}, bf16[256,8,128]{2,1,0:T(8,128)(2,1)}, u32[]{:S(2)}, u32[]{:S(2)}) collective-permute-start(bf16[256,8,128]{2,1,0:T(8,128)(2,1)} %collective-permute-done.8.refs_2_), channel_id=1, source_target_pairs={{0,32},{32,64},{64,96},{96,128},{128,160},{160,192},{192,224},{224... | collective-permute-start | bytes 1572872 | tf_op jit(solution)/shard_map/ppermute | solution.py:202
  61.7 12.0 %collective-permute-start.12 = (bf16[256,8,128]{2,1,0:T(8,128)(2,1)S(1)}, bf16[256,8,128]{2,1,0:T(8,128)(2,1)}, u32[]{:S(2)}, u32[]{:S(2)}) collective-permute-start(bf16[256,8,128]{2,1,0:T(8,128)(2,1)S(1)} %collective-permute-done.10.refs_6_), channel_id=1, source_target_pairs={{0,480},{32,0},{64,32},{96,64},{128,96},{160,128},{192,160},{224,1... | collective-permute-start | bytes 1572872 | tf_op jit(solution)/shard_map/ppermute | solution.py:203
  69.3 11.5 %copy-start.7 = (s32[32,512]{1,0:T(8,128)}, s32[32,512]{1,0:T(8,128)S(1)}, u32[]{:S(2)}) copy-start(s32[32,512]{1,0:T(8,128)S(1)} %get-tuple-element.90) | copy-start | bytes 196612
  69.3 11.5 %copy-start.8 = (s32[32,512]{1,0:T(8,128)}, s32[32,512]{1,0:T(8,128)S(1)}, u32[]{:S(2)}) copy-start(s32[32,512]{1,0:T(8,128)S(1)} %get-tuple-element.91) | copy-start | bytes 196612
  73.7 13.8 %collective-permute-start.13 = (bf16[256,8,128]{2,1,0:T(8,128)(2,1)}, bf16[256,8,128]{2,1,0:T(8,128)(2,1)}, u32[]{:S(2)}, u32[]{:S(2)}) collective-permute-start(bf16[256,8,128]{2,1,0:T(8,128)(2,1)} %collective-permute-done.11.refs_1_), channel_id=1, source_target_pairs={{0,32},{32,64},{64,96},{96,128},{128,160},{160,192},{192,224},{224... | collective-permute-start | bytes 1572872 | tf_op jit(solution)/shard_map/ppermute | solution.py:202
  78.8 12.5 %collective-permute-start.14 = (bf16[256,8,128]{2,1,0:T(8,128)(2,1)}, bf16[256,8,128]{2,1,0:T(8,128)(2,1)}, u32[]{:S(2)}, u32[]{:S(2)}) collective-permute-start(bf16[256,8,128]{2,1,0:T(8,128)(2,1)} %collective-permute-done.12.refs_7_), channel_id=1, source_target_pairs={{0,480},{32,0},{64,32},{96,64},{128,96},{160,128},{192,160},{224,1... | collective-permute-start | bytes 1572872 | tf_op jit(solution)/shard_map/ppermute | solution.py:203
  97.0 12.3 %collective-permute-start.15 = (bf16[640,256]{1,0:T(8,128)(2,1)S(1)}, bf16[640,256]{1,0:T(8,128)(2,1)S(1)}, u32[]{:S(2)}, u32[]{:S(2)}) collective-permute-start(bf16[640,256]{1,0:T(8,128)(2,1)S(1)} %get-tuple-element.98), channel_id=1, source_target_pairs={{0,1},{1,0},{2,3},{3,2},{4,5},{5,4},{6,7},{7,6},{8,9},{9,8},{10,11... | collective-permute-start | bytes 983048 | tf_op jit(solution)/shard_map/ppermute | solution.py:373
  105.1 4.1 %copy-start.6 = (f32[16,32,16]{2,1,0:T(8,128)}, f32[16,32,16]{2,1,0:T(8,128)S(1)}, u32[]{:S(2)}) copy-start(f32[16,32,16]{2,1,0:T(8,128)S(1)} %get-tuple-element.108) | copy-start | bytes 98308
  110.1 15.2 %all-to-all-start.3 = ((bf16[16,40,256]{2,1,0:T(8,128)(2,1)}), bf16[16,40,256]{2,1,0:T(8,128)(2,1)S(1)}, u32[]{:S(2)}, u32[]{:S(2)}) async-start(bf16[16,40,256]{2,1,0:T(8,128)(2,1)} %bitcast.17), calls=%async_computation.3 | async-start | bytes 655360 | tf_op jit(solution)/shard_map/all_to_all | solution.py:376
  126.2 21.8 %all-to-all-start.4 = ((bf16[16,16,256]{2,1,0:T(8,128)(2,1)}), bf16[16,16,256]{2,1,0:T(8,128)(2,1)S(1)}, u32[]{:S(2)}, u32[]{:S(2)}) async-start(bf16[16,16,256]{2,1,0:T(8,128)(2,1)} %fusion.68), calls=%async_computation.4 | async-start | bytes 262144 | tf_op jit(solution)/shard_map/all_to_all | solution.py:400
  148.3 0.6 copy-start.9

commit v7 on v6

--- a/solution.py
+++ b/solution.py
@@ -373,6 +373,7 @@
     from_other = lax.ppermute(for_other, "c", [(0, 1), (1, 0)])
     for_own = correlate_again(own_index, own_used, table, basis)
     both = (for_own.astype(jnp.float32) + from_other.astype(jnp.float32)).astype(jnp.bfloat16)
+    both, middle = lax.optimization_barrier((both, middle))
     shares = lax.all_to_all(both.reshape(xs * ys, slots, LAGS), ("x", "y"), 0, 0, tiled=True)
     added = jnp.sum(shares.astype(jnp.float32), axis=0)
 

time: 151 us -> 154 us (1.020)
  local copies, waits for them, and re-layouts: 5.14 us -> 10.1 us
  waiting for transfers between devices: 42.3 us -> 40.1 us
    unnamed x14, local copies, waits for them, and re-layouts: 0.9 us -> 5.88 us
    all_to_all x1, waiting for transfers between devices: 8.3 us -> 4.76 us  [body(): lax.all_to_all(both.reshape(xs * ys, slots, LAGS), ('x', 'y'), 0, 0, tile...]
where the time goes in v7:
time: 154 us; the launch traced here: 152 us
  starting transfers between devices  70.2 us (46%)
  waiting for transfers between devices  40.1 us (26%)
  other arithmetic  15.6 us (10%)
  local copies, waits for them, and re-layouts  10.1 us (7%)
  Pallas kernels  9.71 us (6%)
  matrix products  3.93 us (3%)
  between operations  2.36 us (2%)
    ppermute x4, starting transfers between devices, near_ring(): from_above = lax.ppermute(from_above, axis, down)  22.2 us
    ppermute x4, starting transfers between devices, near_ring(): from_below = lax.ppermute(from_below, axis, up)  12.1 us
    ppermute x4, waiting for transfers between devices, near_ring(): from_above = lax.ppermute(from_above, axis, down)  10.4 us
    all_to_all x1, starting transfers between devices, body(): lax.all_to_all(leaving.reshape(zs, returned, LAGS), 'z', 0, 0, tiled=True)  9.73 us
    all_to_all x1, starting transfers between devices, body(): codes = lax.all_to_all(code, ('z', 'x'), 0, 0, tiled=True)  8.68 us
    all_to_all x1, waiting for transfers between devices, body(): lax.all_to_all(leaving.reshape(zs, returned, LAGS), 'z', 0, 0, tiled=True)  8.32 us
    all_to_all x1, starting transfers between devices, body(): lax.all_to_all(both.reshape(xs * ys, slots, LAGS), ('x', 'y'), 0, 0, tile...  6.75 us
    all_to_all x1, waiting for transfers between devices, body(): codes = lax.all_to_all(code, ('z', 'x'), 0, 0, tiled=True)  6.16 us
  transfers between devices with their start and end apart: 13, of which 10 were waited for; matrix products, arithmetic and copies ran while one was open for 11% of the time, Pallas kernels for 3%

profile of v7, /device:TPU:1, one launch (start us, length us, event | category | flops | bytes accessed | tf_op | source)
XLA Modules:
  0.0 152.2 jit_solution(14753613454636233552)
XLA Ops:
  0.0 1.4 add_sqrt_fusion
  1.7 0.8 fusion.52
  3.4 1.1 copy_bitcast_fusion.2
  4.5 4.8 %all-to-all-start.1 = ((bf16[4,64,8,128]{3,2,1,0:T(8,128)(2,1)}), bf16[4,64,8,128]{3,2,1,0:T(8,128)(2,1)S(1)}, u32[]{:S(2)}, u32[]{:S(2)}) async-start(bf16[4,64,8,128]{3,2,1,0:T(8,128)(2,1)} %copy_bitcast_fusion.2), calls=%async_computation.1 | async-start | bytes 1048576 | tf_op jit(solution)/shard_map/all_to_all | solution.py:334
  9.8 1.0 fusion.55
  10.8 5.4 %all-to-all-done.1 = bf16[4,64,8,128]{3,2,1,0:T(8,128)(2,1)S(1)} async-done(((bf16[4,64,8,128]{3,2,1,0:T(8,128)(2,1)}), bf16[4,64,8,128]{3,2,1,0:T(8,128)(2,1)S(1)}, u32[]{:S(2)}, u32[]{:S(2)}) %all-to-all-start.1) | async-done | bytes 524320 | tf_op jit(solution)/shard_map/all_to_all | solution.py:334
  16.2 0.7 broadcast_in_dim.74
  16.9 12.4 %collective-permute-start.9 = (bf16[256,8,128]{2,1,0:T(8,128)(2,1)S(1)}, bf16[256,8,128]{2,1,0:T(8,128)(2,1)S(1)}, u32[]{:S(2)}, u32[]{:S(2)}) collective-permute-start(bf16[256,8,128]{2,1,0:T(8,128)(2,1)S(1)} %bitcast.59), channel_id=1, source_target_pairs={{0,480},{32,0},{64,32},{96,64},{128,96},{160,128},{192,160},{224,1... | collective-permute-start | bytes 1572872 | tf_op jit(solution)/shard_map/ppermute | solution.py:203
  29.4 1.9 %collective-permute-start.7 = (bf16[256,8,128]{2,1,0:T(8,128)(2,1)S(1)}, bf16[256,8,128]{2,1,0:T(8,128)(2,1)S(1)}, u32[]{:S(2)}, u32[]{:S(2)}) collective-permute-start(bf16[256,8,128]{2,1,0:T(8,128)(2,1)S(1)} %bitcast.60), channel_id=1, source_target_pairs={{0,32},{32,64},{64,96},{96,128},{128,160},{160,192},{192,224},{224... | collective-permute-start | bytes 1572872 | tf_op jit(solution)/shard_map/ppermute | solution.py:202
  31.3 8.7 %all-to-all-start.2 = ((s32[64,4,128]{2,1,0:T(4,128)}), s32[64,4,128]{2,1,0:T(4,128)S(1)}, u32[]{:S(2)}, u32[]{:S(2)}) async-start(s32[64,4,128]{2,1,0:T(4,128)} %broadcast_in_dim.74), calls=%async_computation.2 | async-start | bytes 262144 | tf_op jit(solution)/shard_map/all_to_all | solution.py:336
  40.0 4.4 %collective-permute-start.10 = (bf16[256,8,128]{2,1,0:T(8,128)(2,1)S(1)}, bf16[256,8,128]{2,1,0:T(8,128)(2,1)S(1)}, u32[]{:S(2)}, u32[]{:S(2)}) collective-permute-start(bf16[256,8,128]{2,1,0:T(8,128)(2,1)S(1)} %collective-permute-done.9.refs_5_), channel_id=1, source_target_pairs={{0,480},{32,0},{64,32},{96,64},{128,96},{160,128},{192,160},{224,1... | collective-permute-start | bytes 1572872 | tf_op jit(solution)/shard_map/ppermute | solution.py:203
  44.4 1.9 %collective-permute-start.8 = (bf16[256,8,128]{2,1,0:T(8,128)(2,1)S(1)}, bf16[256,8,128]{2,1,0:T(8,128)(2,1)}, u32[]{:S(2)}, u32[]{:S(2)}) collective-permute-start(bf16[256,8,128]{2,1,0:T(8,128)(2,1)S(1)} %collective-permute-done.7.refs_3_), channel_id=1, source_target_pairs={{0,32},{32,64},{64,96},{96,128},{128,160},{160,192},{192,224},{224... | collective-permute-start | bytes 1572872 | tf_op jit(solution)/shard_map/ppermute | solution.py:202
  46.4 2.5 %multiply_convert_fusion.1 = (bf16[512,256]{1,0:T(8,128)(2,1)S(1)}, bf16[512,256]{1,0:T(8,128)(2,1)S(1)}) fusion(s32[256]{0:T(256)S(1)} %iota_add_fusion.2, s32[512]{0:T(512)S(1)} %iota_add_fusion.1), kind=kLoop, calls=%fused_computation.159 | loop fusion | flops 2490368 | bytes 527360 | tf_op jit(solution)/shard_map/convert.2
  49.0 6.2 %all-to-all-done.2 = s32[64,4,128]{2,1,0:T(4,128)S(1)} async-done(((s32[64,4,128]{2,1,0:T(4,128)}), s32[64,4,128]{2,1,0:T(4,128)S(1)}, u32[]{:S(2)}, u32[]{:S(2)}) %all-to-all-start.2) | async-done | bytes 131104 | tf_op jit(solution)/shard_map/all_to_all | solution.py:336
  55.1 2.9 %collective-permute-done.10.refs_6_ = bf16[256,8,128]{2,1,0:T(8,128)(2,1)S(1)} collective-permute-done((bf16[256,8,128]{2,1,0:T(8,128)(2,1)S(1)}, bf16[256,8,128]{2,1,0:T(8,128)(2,1)S(1)}, u32[]{:S(2)}, u32[]{:S(2)}) %collective-permute-start.10) | collective-permute-done | bytes 524320 | tf_op jit(solution)/shard_map/ppermute | solution.py:203
  58.0 0.6 collective-permute-done.8.refs_2_
  58.6 3.1 %collective-permute-start.11 = (bf16[256,8,128]{2,1,0:T(8,128)(2,1)}, bf16[256,8,128]{2,1,0:T(8,128)(2,1)}, u32[]{:S(2)}, u32[]{:S(2)}) collective-permute-start(bf16[256,8,128]{2,1,0:T(8,128)(2,1)} %collective-permute-done.8.refs_2_), channel_id=1, source_target_pairs={{0,32},{32,64},{64,96},{96,128},{128,160},{160,192},{192,224},{224... | collective-permute-start | bytes 1572872 | tf_op jit(solution)/shard_map/ppermute | solution.py:202
  61.7 3.4 %collective-permute-start.12 = (bf16[256,8,128]{2,1,0:T(8,128)(2,1)S(1)}, bf16[256,8,128]{2,1,0:T(8,128)(2,1)}, u32[]{:S(2)}, u32[]{:S(2)}) collective-permute-start(bf16[256,8,128]{2,1,0:T(8,128)(2,1)S(1)} %collective-permute-done.10.refs_6_), channel_id=1, source_target_pairs={{0,480},{32,0},{64,32},{96,64},{128,96},{160,128},{192,160},{224,1... | collective-permute-start | bytes 1572872 | tf_op jit(solution)/shard_map/ppermute | solution.py:203
  65.1 0.6 slice.58
  66.4 3.5 %conditional.3 = (s32[32,512]{1,0:T(8,128)}, s32[32,512]{1,0:T(8,128)S(1)}) conditional(s32[]{:T(128)} %bitcast.14, () %tuple.40, (s32[64,4,128]{2,1,0:T(4,128)S(1)}, s32[]{:T(128)}) %tuple.41), branch_computations={%region_3.4_spmd, %region_4.11_spmd} | conditional | flops 279927264 | bytes 2145556 | solution.py:350
  68.2 0.6 fusion.10
  68.8 0.4 multiply_reduce_fusion
  69.2 0.7 fusion.25
  70.1 3.6 %collective-permute-done.12.refs_7_ = bf16[256,8,128]{2,1,0:T(8,128)(2,1)} collective-permute-done((bf16[256,8,128]{2,1,0:T(8,128)(2,1)S(1)}, bf16[256,8,128]{2,1,0:T(8,128)(2,1)}, u32[]{:S(2)}, u32[]{:S(2)}) %collective-permute-start.12) | collective-permute-done | bytes 524320 | tf_op jit(solution)/shard_map/ppermute | solution.py:203
  73.7 5.1 %collective-permute-start.13 = (bf16[256,8,128]{2,1,0:T(8,128)(2,1)}, bf16[256,8,128]{2,1,0:T(8,128)(2,1)}, u32[]{:S(2)}, u32[]{:S(2)}) collective-permute-start(bf16[256,8,128]{2,1,0:T(8,128)(2,1)} %collective-permute-done.11.refs_1_), channel_id=1, source_target_pairs={{0,32},{32,64},{64,96},{96,128},{128,160},{160,192},{192,224},{224... | collective-permute-start | bytes 1572872 | tf_op jit(solution)/shard_map/ppermute | solution.py:202
  78.8 1.9 %collective-permute-start.14 = (bf16[256,8,128]{2,1,0:T(8,128)(2,1)}, bf16[256,8,128]{2,1,0:T(8,128)(2,1)}, u32[]{:S(2)}, u32[]{:S(2)}) collective-permute-start(bf16[256,8,128]{2,1,0:T(8,128)(2,1)} %collective-permute-done.12.refs_7_), channel_id=1, source_target_pairs={{0,480},{32,0},{64,32},{96,64},{128,96},{160,128},{192,160},{224,1... | collective-permute-start | bytes 1572872 | tf_op jit(solution)/shard_map/ppermute | solution.py:203
  80.8 2.0 %conditional.4 = (s32[2,16,2,40]{3,2,1,0:T(2,128)S(1)}, s32[16,2]{1,0:T(8,128)S(1)}) conditional(s32[]{:T(128)} %bitcast.14, () %tuple.39, (s32[]{:T(128)}, s32[32,512]{1,0:T(8,128)}, s32[32,512]{1,0:T(8,128)S(1)}) %tuple.43), branch_computations={%region_11.12_spmd, %region_12.15_spmd} | conditional | flops 19112960 | bytes 336532 | solution.py:361
  80.8 1.0 convert_reduce_fusion
  82.1 0.6 select_reduce_fusion
  83.2 4.3 %collective-permute-done.13.refs_0_ = bf16[256,8,128]{2,1,0:T(8,128)(2,1)} collective-permute-done((bf16[256,8,128]{2,1,0:T(8,128)(2,1)}, bf16[256,8,128]{2,1,0:T(8,128)(2,1)}, u32[]{:S(2)}, u32[]{:S(2)}) %collective-permute-start.13) | collective-permute-done | bytes 524320 | tf_op jit(solution)/shard_map/ppermute | solution.py:202
  87.5 3.8 %collective-permute-done.14.refs_8_ = bf16[256,8,128]{2,1,0:T(8,128)(2,1)} collective-permute-done((bf16[256,8,128]{2,1,0:T(8,128)(2,1)}, bf16[256,8,128]{2,1,0:T(8,128)(2,1)}, u32[]{:S(2)}, u32[]{:S(2)}) %collective-permute-start.14) | collective-permute-done | bytes 524320 | tf_op jit(solution)/shard_map/ppermute | solution.py:203
  91.3 5.6 %shard_map.48 = (bf16[640,256]{1,0:T(8,128)(2,1)S(1)}, bf16[2312,8,128]{2,1,0:T(8,128)(2,1)S(1)}) custom-call(s32[2,640]{1,0:T(2,128)S(1)} %reshape.654.index_ref, s32[16]{0:T(128)S(1)} %get-tuple-element.117.used_ref, bf16[256,8,128]{2,1,0:T(8,128)(2,1)} %collective-permute-done.13.refs_0_, bf16[256,8,128]{2,1,0:T(8,128)(2,1)} %collective-permute-done.11.refs_1_, ...), custom_call_target="tpu_custom_call" | custom-call | tf_op jit(solution)/shard_map/pallas_call | solution.py:149
  97.0 2.1 %copy-done = bf16[2312,8,128]{2,1,0:T(8,128)(2,1)} copy-done((bf16[2312,8,128]{2,1,0:T(8,128)(2,1)}, bf16[2312,8,128]{2,1,0:T(8,128)(2,1)S(1)}, u32[]{:S(2)}) %copy-start) | copy-done | bytes 4735000
  99.1 5.9 %collective-permute-start.15 = (bf16[640,256]{1,0:T(8,128)(2,1)S(1)}, bf16[640,256]{1,0:T(8,128)(2,1)}, u32[]{:S(2)}, u32[]{:S(2)}) collective-permute-start(bf16[640,256]{1,0:T(8,128)(2,1)S(1)} %get-tuple-element.100), channel_id=1, source_target_pairs={{0,1},{1,0},{2,3},{3,2},{4,5},{5,4},{6,7},{7,6},{8,9},{9,8},{10,11... | collective-permute-start | bytes 983048 | tf_op jit(solution)/shard_map/ppermute | solution.py:373
  105.2 2.3 %copy-done.1 = bf16[2312,8,128]{2,1,0:T(8,128)(2,1)S(1)} copy-done((bf16[2312,8,128]{2,1,0:T(8,128)(2,1)S(1)}, bf16[2312,8,128]{2,1,0:T(8,128)(2,1)}, u32[]{:S(2)}) %copy-start.1) | copy-done | bytes 4735000
  107.5 4.1 %shard_map.49 = bf16[640,256]{1,0:T(8,128)(2,1)S(1)} custom-call(s32[2,640]{1,0:T(2,128)S(1)} %reshape.653.index_ref, s32[16]{0:T(128)S(1)} %get-tuple-element.116.used_ref, bf16[2312,8,128]{2,1,0:T(8,128)(2,1)S(1)} %copy-done.1, bf16[1024,256]{1,0:T(8,128)(2,1)S(1)} %pad_maximum_fusion.2.refs_9_.basis_ref), custom_call_target="tpu_custom_call" | custom-call | flops 335544320 | bytes 8388608 | tf_op jit(solution)/shard_map/pallas_call | solution.py:169
  111.6 1.8 %add_convert_fusion = bf16[640,256]{1,0:T(8,128)(2,1)} fusion(bf16[640,256]{1,0:T(8,128)(2,1)} %collective-permute-done.15, bf16[640,256]{1,0:T(8,128)(2,1)S(1)} %shard_map.49), kind=kLoop, calls=%fused_computation.146 | loop fusion | flops 655360 | bytes 983040 | tf_op jit(solution)/shard_map/convert_element_type | solution.py:375
  113.4 6.8 %all-to-all-start.3 = ((bf16[16,40,256]{2,1,0:T(8,128)(2,1)}), bf16[16,40,256]{2,1,0:T(8,128)(2,1)S(1)}, u32[]{:S(2)}, u32[]{:S(2)}) async-start(bf16[16,40,256]{2,1,0:T(8,128)(2,1)} %bitcast.17), calls=%async_computation.3 | async-start | bytes 655360 | tf_op jit(solution)/shard_map/all_to_all | solution.py:377
  120.1 1.0 eq.167
  121.1 2.0 %convert_reduce_fusion.4 = (f32[16,32,16]{2,1,0:T(8,128)S(1)}, f32[16,32]{1,0:T(8,128)S(1)}) fusion(s32[32,16,32]{2,1,0:T(8,128)S(1)} %eq.167), kind=kLoop, calls=%fused_computation.128 | loop fusion | flops 1039872 | bytes 100352 | tf_op jit(solution)/shard_map/reduce_sum | solution.py:381
  123.2 0.5 copy-done.8
  123.9 4.8 %all-to-all-done.3 = bf16[16,40,256]{2,1,0:T(8,128)(2,1)S(1)} async-done(((bf16[16,40,256]{2,1,0:T(8,128)(2,1)}), bf16[16,40,256]{2,1,0:T(8,128)(2,1)S(1)}, u32[]{:S(2)}, u32[]{:S(2)}) %all-to-all-start.3) | async-done | bytes 327712 | tf_op jit(solution)/shard_map/all_to_all | solution.py:377
  128.7 0.9 fusion.68
  129.5 9.7 %all-to-all-start.4 = ((bf16[16,16,256]{2,1,0:T(8,128)(2,1)}), bf16[16,16,256]{2,1,0:T(8,128)(2,1)S(1)}, u32[]{:S(2)}, u32[]{:S(2)}) async-start(bf16[16,16,256]{2,1,0:T(8,128)(2,1)} %fusion.68), calls=%async_computation.4 | async-start | bytes 262144 | tf_op jit(solution)/shard_map/all_to_all | solution.py:401
  139.3 1.6 %reduce_max.28 = f32[]{:T(128)} reduce(f32[16,32,16]{2,1,0:T(8,128)} %copy-done.8, f32[]{:T(128)} %constant.406.clone.1), dimensions={0,1,2}, to_apply=%region_18.19 | reduce | flops 8191 | bytes 32776 | tf_op jit(solution)/shard_map/reduce_max | solution.py:384
  140.9 0.7 reduce_max.27
  143.0 8.3 %all-to-all-done.4 = bf16[16,16,256]{2,1,0:T(8,128)(2,1)S(1)} async-done(((bf16[16,16,256]{2,1,0:T(8,128)(2,1)}), bf16[16,16,256]{2,1,0:T(8,128)(2,1)S(1)}, u32[]{:S(2)}, u32[]{:S(2)}) %all-to-all-start.4) | async-done | bytes 131104 | tf_op jit(solution)/shard_map/all_to_all | solution.py:401
  151.6 0.6 copy-done.9
  (68 shorter events, 5.1 us)
Async XLA Ops:
  1.5 1.2 copy-start.4
  2.8 6.5 %copy-start.11 = (s32[256,2]{0,1:T(2,128)S(1)}, s32[256,2]{0,1:T(2,128)}, u32[]{:S(2)}) copy-start(s32[256,2]{0,1:T(2,128)} %param.11) | copy-start | bytes 6148
  2.8 6.6 %copy-start.10 = (s32[4096]{0:T(1024)S(1)}, s32[4096]{0:T(1024)}, u32[]{:S(2)}) copy-start(s32[4096]{0:T(1024)} %param.12) | copy-start | bytes 49156
  4.5 11.8 %all-to-all-start.1 = ((bf16[4,64,8,128]{3,2,1,0:T(8,128)(2,1)}), bf16[4,64,8,128]{3,2,1,0:T(8,128)(2,1)S(1)}, u32[]{:S(2)}, u32[]{:S(2)}) async-start(bf16[4,64,8,128]{3,2,1,0:T(8,128)(2,1)} %copy_bitcast_fusion.2), calls=%async_computation.1 | async-start | bytes 1048576 | tf_op jit(solution)/shard_map/all_to_all | solution.py:334
  16.9 23.1 %collective-permute-start.9 = (bf16[256,8,128]{2,1,0:T(8,128)(2,1)S(1)}, bf16[256,8,128]{2,1,0:T(8,128)(2,1)S(1)}, u32[]{:S(2)}, u32[]{:S(2)}) collective-permute-start(bf16[256,8,128]{2,1,0:T(8,128)(2,1)S(1)} %bitcast.59), channel_id=1, source_target_pairs={{0,480},{32,0},{64,32},{96,64},{128,96},{160,128},{192,160},{224,1... | collective-permute-start | bytes 1572872 | tf_op jit(solution)/shard_map/ppermute | solution.py:203
  29.4 15.1 %collective-permute-start.7 = (bf16[256,8,128]{2,1,0:T(8,128)(2,1)S(1)}, bf16[256,8,128]{2,1,0:T(8,128)(2,1)S(1)}, u32[]{:S(2)}, u32[]{:S(2)}) collective-permute-start(bf16[256,8,128]{2,1,0:T(8,128)(2,1)S(1)} %bitcast.60), channel_id=1, source_target_pairs={{0,32},{32,64},{64,96},{96,128},{128,160},{160,192},{192,224},{224... | collective-permute-start | bytes 1572872 | tf_op jit(solution)/shard_map/ppermute | solution.py:202
  31.3 23.8 %all-to-all-start.2 = ((s32[64,4,128]{2,1,0:T(4,128)}), s32[64,4,128]{2,1,0:T(4,128)S(1)}, u32[]{:S(2)}, u32[]{:S(2)}) async-start(s32[64,4,128]{2,1,0:T(4,128)} %broadcast_in_dim.74), calls=%async_computation.2 | async-start | bytes 262144 | tf_op jit(solution)/shard_map/all_to_all | solution.py:336
  40.0 18.0 %collective-permute-start.10 = (bf16[256,8,128]{2,1,0:T(8,128)(2,1)S(1)}, bf16[256,8,128]{2,1,0:T(8,128)(2,1)S(1)}, u32[]{:S(2)}, u32[]{:S(2)}) collective-permute-start(bf16[256,8,128]{2,1,0:T(8,128)(2,1)S(1)} %collective-permute-done.9.refs_5_), channel_id=1, source_target_pairs={{0,480},{32,0},{64,32},{96,64},{128,96},{160,128},{192,160},{224,1... | collective-permute-start | bytes 1572872 | tf_op jit(solution)/shard_map/ppermute | solution.py:203
  44.4 14.2 %collective-permute-start.8 = (bf16[256,8,128]{2,1,0:T(8,128)(2,1)S(1)}, bf16[256,8,128]{2,1,0:T(8,128)(2,1)}, u32[]{:S(2)}, u32[]{:S(2)}) collective-permute-start(bf16[256,8,128]{2,1,0:T(8,128)(2,1)S(1)} %collective-permute-done.7.refs_3_), channel_id=1, source_target_pairs={{0,32},{32,64},{64,96},{96,128},{128,160},{160,192},{192,224},{224... | collective-permute-start | bytes 1572872 | tf_op jit(solution)/shard_map/ppermute | solution.py:202
  58.6 11.4 %collective-permute-start.11 = (bf16[256,8,128]{2,1,0:T(8,128)(2,1)}, bf16[256,8,128]{2,1,0:T(8,128)(2,1)}, u32[]{:S(2)}, u32[]{:S(2)}) collective-permute-start(bf16[256,8,128]{2,1,0:T(8,128)(2,1)} %collective-permute-done.8.refs_2_), channel_id=1, source_target_pairs={{0,32},{32,64},{64,96},{96,128},{128,160},{160,192},{192,224},{224... | collective-permute-start | bytes 1572872 | tf_op jit(solution)/shard_map/ppermute | solution.py:202
  61.7 12.0 %collective-permute-start.12 = (bf16[256,8,128]{2,1,0:T(8,128)(2,1)S(1)}, bf16[256,8,128]{2,1,0:T(8,128)(2,1)}, u32[]{:S(2)}, u32[]{:S(2)}) collective-permute-start(bf16[256,8,128]{2,1,0:T(8,128)(2,1)S(1)} %collective-permute-done.10.refs_6_), channel_id=1, source_target_pairs={{0,480},{32,0},{64,32},{96,64},{128,96},{160,128},{192,160},{224,1... | collective-permute-start | bytes 1572872 | tf_op jit(solution)/shard_map/ppermute | solution.py:203
  73.7 13.8 %collective-permute-start.13 = (bf16[256,8,128]{2,1,0:T(8,128)(2,1)}, bf16[256,8,128]{2,1,0:T(8,128)(2,1)}, u32[]{:S(2)}, u32[]{:S(2)}) collective-permute-start(bf16[256,8,128]{2,1,0:T(8,128)(2,1)} %collective-permute-done.11.refs_1_), channel_id=1, source_target_pairs={{0,32},{32,64},{64,96},{96,128},{128,160},{160,192},{192,224},{224... | collective-permute-start | bytes 1572872 | tf_op jit(solution)/shard_map/ppermute | solution.py:202
  78.8 12.5 %collective-permute-start.14 = (bf16[256,8,128]{2,1,0:T(8,128)(2,1)}, bf16[256,8,128]{2,1,0:T(8,128)(2,1)}, u32[]{:S(2)}, u32[]{:S(2)}) collective-permute-start(bf16[256,8,128]{2,1,0:T(8,128)(2,1)} %collective-permute-done.12.refs_7_), channel_id=1, source_target_pairs={{0,480},{32,0},{64,32},{96,64},{128,96},{160,128},{192,160},{224,1... | collective-permute-start | bytes 1572872 | tf_op jit(solution)/shard_map/ppermute | solution.py:203
  97.0 2.1 %copy-start = (bf16[2312,8,128]{2,1,0:T(8,128)(2,1)}, bf16[2312,8,128]{2,1,0:T(8,128)(2,1)S(1)}, u32[]{:S(2)}) copy-start(bf16[2312,8,128]{2,1,0:T(8,128)(2,1)S(1)} %get-tuple-element.99.table) | copy-start | bytes 14204932
  99.1 12.5 %collective-permute-start.15 = (bf16[640,256]{1,0:T(8,128)(2,1)S(1)}, bf16[640,256]{1,0:T(8,128)(2,1)}, u32[]{:S(2)}, u32[]{:S(2)}) collective-permute-start(bf16[640,256]{1,0:T(8,128)(2,1)S(1)} %get-tuple-element.100), channel_id=1, source_target_pairs={{0,1},{1,0},{2,3},{3,2},{4,5},{5,4},{6,7},{7,6},{8,9},{9,8},{10,11... | collective-permute-start | bytes 983048 | tf_op jit(solution)/shard_map/ppermute | solution.py:373
  105.2 2.3 %copy-start.1 = (bf16[2312,8,128]{2,1,0:T(8,128)(2,1)S(1)}, bf16[2312,8,128]{2,1,0:T(8,128)(2,1)}, u32[]{:S(2)}) copy-start(bf16[2312,8,128]{2,1,0:T(8,128)(2,1)} %copy-done) | copy-start | bytes 14204932
  113.4 15.3 %all-to-all-start.3 = ((bf16[16,40,256]{2,1,0:T(8,128)(2,1)}), bf16[16,40,256]{2,1,0:T(8,128)(2,1)S(1)}, u32[]{:S(2)}, u32[]{:S(2)}) async-start(bf16[16,40,256]{2,1,0:T(8,128)(2,1)} %bitcast.17), calls=%async_computation.3 | async-start | bytes 655360 | tf_op jit(solution)/shard_map/all_to_all | solution.py:377
  123.1 0.7 copy-start.8
  129.5 21.8 %all-to-all-start.4 = ((bf16[16,16,256]{2,1,0:T(8,128)(2,1)}), bf16[16,16,256]{2,1,0:T(8,128)(2,1)S(1)}, u32[]{:S(2)}, u32[]{:S(2)}) async-start(bf16[16,16,256]{2,1,0:T(8,128)(2,1)} %fusion.68), calls=%async_computation.4 | async-start | bytes 262144 | tf_op jit(solution)/shard_map/all_to_all | solution.py:401
  151.6 0.6 copy-start.9
